TPU v7x, 32 devices: a whole 2x2x4 slice. The times are simulated.
32 devices in a mesh: batch: 8 (over z, x), seq: 4 (over y, core).
Axes of the slice: x: 2, y: 2, z: 4, core: 2. Of those that a mesh axis runs over, the one named last changes fastest.
Arguments:
- stream_in: bfloat16 [8, 1024, 2048], P('batch', 'seq'), may hold values from -6 to 6
- segment_ids: int32 [8, 1024], P('batch', 'seq'), may hold values from 0 to 3, never falling along the last dimension, each value on 1 to 768 neighbouring positions
- out_grad: bfloat16 [8, 1024, 2048], P('batch', 'seq'), may hold values from -6 to 6
- branch_weight: bfloat16 [2048, 2730], P(('batch', 'seq')), may hold values from -0.125 to 0.125
- gating_weight: bfloat16 [2048, 2730], P(('batch', 'seq')), may hold values from -0.125 to 0.125
- output_weight: bfloat16 [2048, 2730], P(('batch', 'seq')), may hold values from -0.21875 to 0.21875
- hidden_gate: bfloat16 [2048, 6144], P(('batch', 'seq')), may hold values from -0.125 to 0.125
- hidden_linear: bfloat16 [2048, 6144], P(('batch', 'seq')), may hold values from -0.125 to 0.125
- hidden_output: bfloat16 [2048, 6144], P(('batch', 'seq')), may hold values from -0.15625 to 0.15625
- mixer_gain: bfloat16 [2048], P(('batch', 'seq')), may hold values from 0.5 to 1.5
- hidden_gain: bfloat16 [2048], P(('batch', 'seq')), may hold values from 0.5 to 1.5
- gate_blocks: bfloat16 [2, 16, 171, 171], replicated, may hold values from -0.4375 to 0.4375
- gate_biases: float32 [2, 2730], replicated, may hold values from -3 to 3
- conv_taps: float32 [4, 2730], replicated, may hold values from -3 to 3
- conv_bias: float32 [2730], replicated, may hold values from -3 to 3
- decay_param: float32 [2730], replicated, may hold values from 3 to 10, as said below
Outputs:
- stream_out: bfloat16 [8, 1024, 2048], P('batch', 'seq')
- stream_grad: bfloat16 [8, 1024, 2048], P('batch', 'seq')
- branch_grad: float32 [2048, 2730], P(('batch', 'seq'))
- gating_grad: float32 [2048, 2730], P(('batch', 'seq'))
- output_grad: float32 [2048, 2730], P(('batch', 'seq'))
- hidden_gate_grad: float32 [2048, 6144], P(('batch', 'seq'))
- hidden_linear_grad: float32 [2048, 6144], P(('batch', 'seq'))
- hidden_output_grad: float32 [2048, 6144], P(('batch', 'seq'))
- mixer_gain_grad: float32 [2048], P(('batch', 'seq'))
- hidden_gain_grad: float32 [2048], P(('batch', 'seq'))
- gate_blocks_grad: float32 [2, 16, 171, 171], replicated
- gate_biases_grad: float32 [2, 2730], replicated
- conv_taps_grad: float32 [4, 2730], replicated
- conv_bias_grad: float32 [2730], replicated
- decay_grad: float32 [2730], replicated
Inputs may be any that keep to these rules, and one draw needn't show every extreme that they name: `segment_ids`: within a row the numbers never fall; each document has at most three quarters of 1024 tokens and one has exactly that many. softplus(-decay_param) lies between 1e-4 and 0.03.
All inputs are finite; a program needn't handle non-finite values.
Results may differ from a plain program's by a relative error of at most 0.01.
Values may be sent and summed in bfloat16 or wider, within the bound.
No kernel may reach another device: no remote copies, remote signals or barrier semaphores. Data moves between devices by JAX's collectives and lax.ppermute only.
A program may use at most 512 MiB of HBM per device.

v0:
```python
import jax
import jax.numpy as jnp
from jax import lax
from jax.sharding import PartitionSpec as P

NBLK = 16
BLK = 171
NBIG = 10
KW = 4
R = 2730


EPSILON = 1e-06


def shifted(array, axis, by):
    count = lax.axis_size(axis)
    pairs = [(i, i + by) for i in range(count) if 0 <= i + by < count]
    return lax.ppermute(array, axis, pairs)


def carried_in(part, axis, combine, identity, reverse):
    count = lax.axis_size(axis)
    place = lax.axis_index(axis)
    ahead = count - 1 - place if reverse else place
    gathered = jax.tree.map(lambda a: lax.all_gather(a, axis), part)
    state = jax.tree.map(lambda a, e: jnp.zeros_like(a) + jnp.asarray(e, a.dtype), part, identity)

    def one(turn, state):
        source = count - 1 - turn if reverse else turn
        return combine(
            state, jax.tree.map(lambda a: lax.dynamic_index_in_dim(a, source, 0, False), gathered)
        )

    return lax.fori_loop(0, ahead, one, state)


def to_blocks(values):
    leading = values.shape[:-1]
    larger = values[..., : NBIG * BLK].reshape(leading + (NBIG, BLK))
    smaller = values[..., NBIG * BLK :].reshape(leading + (NBLK - NBIG, BLK - 1))
    smaller = jnp.pad(smaller, [(0, 0)] * len(leading) + [(0, 0), (0, 1)])
    return jnp.concatenate([larger, smaller], axis=-2)


def from_blocks(values):
    leading = values.shape[:-2]
    larger = values[..., :NBIG, :].reshape(leading + (NBIG * BLK,))
    smaller = values[..., NBIG:, : BLK - 1].reshape(leading + ((NBLK - NBIG) * (BLK - 1),))
    return jnp.concatenate([larger, smaller], axis=-1)


def rms_scale(values):
    return lax.rsqrt(jnp.mean(values * values, axis=-1, keepdims=True) + EPSILON)


def norm_apply(values, gain):
    return values * rms_scale(values) * gain


def affine_join(earlier, later):
    return (earlier[0] * later[0], later[0] * earlier[1] + later[1])


def gate_math(recur_pre, input_pre, decay_param, conv_sum, starts):
    recur_gate = jax.nn.sigmoid(recur_pre)
    input_gate = jax.nn.sigmoid(input_pre)
    log_decay = -8.0 * recur_gate * jax.nn.softplus(-decay_param)
    decay = jnp.exp(log_decay)
    carry_mult = jnp.where(starts, 0.0, decay)
    scale_in = jnp.where(starts, 1.0, jnp.sqrt(-jnp.expm1(2.0 * log_decay)))
    return (carry_mult, scale_in * input_gate * conv_sum)


def linear_step(carry, pair):
    fresh = pair[0] * carry + pair[1]
    return (fresh, fresh)


def final_step(carry, pair):
    return (pair[0] * carry + pair[1], None)


def chain_final(mult, addend, reverse):
    start = jnp.zeros_like(addend[:, 0])
    ending, ignored = lax.scan(
        final_step,
        start,
        (jnp.swapaxes(mult, 0, 1), jnp.swapaxes(addend, 0, 1)),
        reverse=reverse,
        unroll=16,
    )
    return ending


def chain_values(mult, addend, start, reverse):
    ignored, values = lax.scan(
        linear_step,
        start,
        (jnp.swapaxes(mult, 0, 1), jnp.swapaxes(addend, 0, 1)),
        reverse=reverse,
        unroll=16,
    )
    return jnp.swapaxes(values, 0, 1)


def product(left, right):
    return jnp.dot(left, right, preferred_element_type=jnp.float32)


def contract_rows(left, right):
    return lax.dot_general(
        left, right, (((0,), (0,)), ((), ())), preferred_element_type=jnp.float32
    )


def contract_cols(left, right):
    return lax.dot_general(
        left, right, (((1,), (1,)), ((), ())), preferred_element_type=jnp.float32
    )


def hidden_forward(normed_mid, weight_gate, weight_linear, weight_output):
    gate_pre = product(normed_mid, weight_gate)
    linear_pre = product(normed_mid, weight_linear)
    gate_value, gate_back = jax.vjp(jax.nn.gelu, gate_pre)
    hidden = (gate_value * linear_pre).astype(jnp.bfloat16)
    return (contract_cols(hidden, weight_output), (linear_pre, gate_value, gate_back, hidden))


def hidden_backward(normed_mid, upstream_low, kept, weight_gate, weight_linear, weight_output):
    linear_pre, gate_value, gate_back, hidden = kept
    d_hidden = product(upstream_low, weight_output)
    grad_houtput = contract_rows(upstream_low, hidden)
    d_gate = gate_back(d_hidden * linear_pre)[0].astype(jnp.bfloat16)
    d_linear = (d_hidden * gate_value).astype(jnp.bfloat16)
    grad_hgate = contract_rows(normed_mid, d_gate)
    grad_hlinear = contract_rows(normed_mid, d_linear)
    d_normed_mid = contract_cols(d_gate, weight_gate) + contract_cols(d_linear, weight_linear)
    return (d_normed_mid, grad_hgate, grad_hlinear, grad_houtput)


def local(
    stream_in,
    segment_ids,
    out_grad,
    branch_weight,
    gating_weight,
    output_weight,
    hidden_gate,
    hidden_linear,
    hidden_output,
    mixer_gain,
    hidden_gain,
    gate_blocks,
    gate_biases,
    conv_taps,
    conv_bias,
    decay_param,
):
    rows_here, steps_here, model_width = stream_in.shape
    tokens = rows_here * steps_here
    gathered_branch, gathered_gating, gathered_output, gathered_mgain, gathered_hgain = (
        lax.all_gather(branch_weight, ("batch", "seq"), axis=0, tiled=True),
        lax.all_gather(gating_weight, ("batch", "seq"), axis=0, tiled=True),
        lax.all_gather(output_weight, ("batch", "seq"), axis=0, tiled=True),
        lax.all_gather(mixer_gain, ("batch", "seq"), axis=0, tiled=True),
        lax.all_gather(hidden_gain, ("batch", "seq"), axis=0, tiled=True),
    )
    inputs = stream_in.astype(jnp.float32).reshape(tokens, model_width)
    mixer_scale = gathered_mgain.astype(jnp.float32)
    normed = norm_apply(inputs, mixer_scale).astype(jnp.bfloat16)
    branch = product(normed, gathered_branch)
    gating = product(normed, gathered_gating)
    branch_rows = branch.reshape(rows_here, steps_here, R)
    seg_float = segment_ids.astype(jnp.float32)
    rim_values, rim_segments = shifted(
        (branch_rows[:, steps_here - KW + 1 :], seg_float[:, steps_here - KW + 1 :]), "seq", 1
    )
    padded = jnp.concatenate([rim_values, branch_rows], axis=1)
    seg_padded = jnp.concatenate([rim_segments, seg_float], axis=1)
    conv_sum = conv_bias + jnp.zeros_like(branch_rows)
    masks = []
    for offset in range(KW):
        begin = KW - 1 - offset
        same = (seg_padded[:, begin : begin + steps_here] == seg_float).astype(jnp.float32)[
            ..., None
        ]
        masks.append(same)
        conv_sum = conv_sum + conv_taps[offset] * padded[:, begin : begin + steps_here] * same
    position = lax.axis_index("seq") * steps_here + lax.broadcasted_iota(
        jnp.int32, (rows_here, steps_here), 1
    )
    starts = ((seg_float != seg_padded[:, KW - 2 : KW - 2 + steps_here]) | (position == 0))[
        ..., None
    ]
    conv_low = conv_sum.reshape(tokens, R).astype(jnp.bfloat16)
    conv_blocks = to_blocks(conv_low)
    pre_blocks = jnp.einsum(
        "nki,gkij->gnkj", conv_blocks, gate_blocks, preferred_element_type=jnp.float32
    )
    pre_both = from_blocks(pre_blocks) + gate_biases[:, None, :]
    recur_pre = pre_both[0].reshape(rows_here, steps_here, R)
    input_pre = pre_both[1].reshape(rows_here, steps_here, R)

    def local_gates(recur_in, input_in, decay_in, conv_in):
        return gate_math(recur_in, input_in, decay_in, conv_in, starts)

    (carry_mult, drive), gates_back = jax.vjp(
        local_gates, recur_pre, input_pre, decay_param, conv_sum
    )
    shard_mult = jnp.prod(carry_mult, axis=1)
    shard_state = chain_final(carry_mult, drive, False)
    carried = carried_in(
        (shard_mult, shard_state),
        "seq",
        affine_join,
        (jnp.ones_like(shard_mult), jnp.zeros_like(shard_state)),
        False,
    )
    state_in = carried[1]
    state = chain_values(carry_mult, drive, state_in, False)
    state_flat = state.reshape(tokens, R)
    gate_act, gating_back = jax.vjp(jax.nn.gelu, gating)
    mixed = (state_flat * gate_act).astype(jnp.bfloat16)
    middle = inputs + contract_cols(mixed, gathered_output)
    hidden_scale = gathered_hgain.astype(jnp.float32)
    normed_mid = norm_apply(middle, hidden_scale).astype(jnp.bfloat16)
    upstream = out_grad.astype(jnp.float32).reshape(tokens, model_width)
    upstream_low = upstream.astype(jnp.bfloat16)
    gathered_hgate, gathered_hlinear, gathered_houtput = (
        lax.all_gather(hidden_gate, ("batch", "seq"), axis=0, tiled=True),
        lax.all_gather(hidden_linear, ("batch", "seq"), axis=0, tiled=True),
        lax.all_gather(hidden_output, ("batch", "seq"), axis=0, tiled=True),
    )
    hidden_out, hidden_kept = hidden_forward(
        normed_mid, gathered_hgate, gathered_hlinear, gathered_houtput
    )
    result = (middle + hidden_out).astype(jnp.bfloat16).reshape(rows_here, steps_here, model_width)
    d_normed_mid, grad_hgate, grad_hlinear, grad_houtput = hidden_backward(
        normed_mid, upstream_low, hidden_kept, gathered_hgate, gathered_hlinear, gathered_houtput
    )
    hidden_sums = (
        lax.psum_scatter(grad_hgate, ("batch", "seq"), scatter_dimension=0, tiled=True),
        lax.psum_scatter(grad_hlinear, ("batch", "seq"), scatter_dimension=0, tiled=True),
        lax.psum_scatter(grad_houtput, ("batch", "seq"), scatter_dimension=0, tiled=True),
    )
    ignored_mid, norm_back_mid = jax.vjp(norm_apply, middle, hidden_scale)
    d_middle_part, grad_hgain = norm_back_mid(d_normed_mid)
    d_middle = upstream + d_middle_part
    middle_low = d_middle.astype(jnp.bfloat16)
    d_mixed = product(middle_low, gathered_output)
    grad_output = contract_rows(middle_low, mixed)
    d_state = (d_mixed * gate_act).reshape(rows_here, steps_here, R)
    d_gating = gating_back(d_mixed * state_flat)[0].astype(jnp.bfloat16)
    next_mult = jnp.concatenate([carry_mult[:, 1:], jnp.ones_like(carry_mult[:, :1])], axis=1)
    first_mult = carry_mult[:, 0]
    shard_back_mult = jnp.prod(next_mult, axis=1)
    shard_back_acc = chain_final(next_mult, d_state, True)
    incoming = carried_in(
        (first_mult * shard_back_mult, first_mult * shard_back_acc),
        "seq",
        affine_join,
        (jnp.ones_like(first_mult), jnp.zeros_like(first_mult)),
        True,
    )
    adjoint = chain_values(next_mult, d_state, incoming[1], True)
    state_prev = jnp.concatenate([state_in[:, None], state[:, :-1]], axis=1)
    d_recur_pre, d_input_pre, grad_decay, d_conv_direct = gates_back(
        (adjoint * state_prev, adjoint)
    )
    d_pre_both = jnp.stack([d_recur_pre.reshape(tokens, R), d_input_pre.reshape(tokens, R)])
    grad_gbias = jnp.sum(d_pre_both, axis=1)
    pre_low_blocks = to_blocks(d_pre_both.astype(jnp.bfloat16))
    d_conv_gates = from_blocks(
        jnp.einsum(
            "gnkj,gkij->nki", pre_low_blocks, gate_blocks, preferred_element_type=jnp.float32
        )
    )
    grad_gblocks = jnp.einsum(
        "nki,gnkj->gkij", conv_blocks, pre_low_blocks, preferred_element_type=jnp.float32
    )
    d_conv = d_conv_direct + d_conv_gates.reshape(rows_here, steps_here, R)
    grad_cbias = jnp.sum(d_conv, axis=(0, 1))
    tap_list = []
    d_padded = jnp.zeros_like(padded)
    for offset in range(KW):
        begin = KW - 1 - offset
        tap_list.append(
            jnp.sum(d_conv * padded[:, begin : begin + steps_here] * masks[offset], axis=(0, 1))
        )
        d_padded = d_padded + jnp.pad(
            d_conv * conv_taps[offset] * masks[offset], ((0, 0), (begin, offset), (0, 0))
        )
    grad_taps = jnp.stack(tap_list)
    rim_back = shifted(d_padded[:, : KW - 1], "seq", -1)
    d_branch = d_padded[:, KW - 1 :] + jnp.pad(rim_back, ((0, 0), (steps_here - KW + 1, 0), (0, 0)))
    d_branch = d_branch.reshape(tokens, R).astype(jnp.bfloat16)
    grad_branch = contract_rows(normed, d_branch)
    grad_gating = contract_rows(normed, d_gating)
    d_normed = contract_cols(d_branch, gathered_branch) + contract_cols(d_gating, gathered_gating)
    ignored_in, norm_back_in = jax.vjp(norm_apply, inputs, mixer_scale)
    d_input_part, grad_mgain = norm_back_in(d_normed)
    stream_grad = (
        (d_middle + d_input_part).astype(jnp.bfloat16).reshape(rows_here, steps_here, model_width)
    )
    mixer_sums = (
        lax.psum_scatter(grad_branch, ("batch", "seq"), scatter_dimension=0, tiled=True),
        lax.psum_scatter(grad_gating, ("batch", "seq"), scatter_dimension=0, tiled=True),
        lax.psum_scatter(grad_output, ("batch", "seq"), scatter_dimension=0, tiled=True),
        lax.psum_scatter(grad_mgain, ("batch", "seq"), scatter_dimension=0, tiled=True),
        lax.psum_scatter(grad_hgain, ("batch", "seq"), scatter_dimension=0, tiled=True),
    )
    small_sums = lax.psum(
        (grad_gblocks, grad_gbias, grad_taps, grad_cbias, grad_decay), ("batch", "seq")
    )
    return (
        result,
        stream_grad,
        mixer_sums[0],
        mixer_sums[1],
        mixer_sums[2],
        hidden_sums[0],
        hidden_sums[1],
        hidden_sums[2],
        mixer_sums[3],
        mixer_sums[4],
        small_sums[0],
        small_sums[1],
        small_sums[2],
        small_sums[3],
        small_sums[4],
    )


def solution(mesh):
    return jax.shard_map(
        local,
        mesh=mesh,
        in_specs=(
            P("batch", "seq", None),
            P("batch", "seq"),
            P("batch", "seq", None),
            P(("batch", "seq"), None),
            P(("batch", "seq"), None),
            P(("batch", "seq"), None),
            P(("batch", "seq"), None),
            P(("batch", "seq"), None),
            P(("batch", "seq"), None),
            P(("batch", "seq")),
            P(("batch", "seq")),
            P(),
            P(),
            P(),
            P(),
            P(),
        ),
        out_specs=(
            P("batch", "seq", None),
            P("batch", "seq", None),
            P(("batch", "seq"), None),
            P(("batch", "seq"), None),
            P(("batch", "seq"), None),
            P(("batch", "seq"), None),
            P(("batch", "seq"), None),
            P(("batch", "seq"), None),
            P(("batch", "seq")),
            P(("batch", "seq")),
            P(),
            P(),
            P(),
            P(),
            P(),
        ),
        check_vma=False,
    )
```

profile of v0, /device:TPU:0, one launch (start us, length us, event | category | flops | bytes accessed | tf_op | source)
XLA Modules:
  0.0 3334.6 jit_solution(3627987356088839190)
XLA Ops:
  14.4 42.5 %all-reduce.14 = (bf16[2048]{0:T(1024)(128)(2,1)S(1)}, bf16[2048]{0:T(1024)(128)(2,1)S(1)}) all-reduce(bf16[2048]{0:T(1024)(128)(2,1)S(1)} %dynamic-update-slice, bf16[2048]{0:T(1024)(128)(2,1)S(1)} %dynamic-update-slice.2), channel_id=1, replica_groups=mesh['batch'=8,'seq'=4] {'batch','seq'}, use_global_device_ids=true, to_apply=%add.8 | all-reduce | flops 4096 | bytes 16384
  60.1 45.7 %all-gather.12.cloned.1.call-done = bf16[2048,2730]{1,0:T(8,128)(2,1)} async-done(((bf16[64,2730]{1,0:T(8,128)(2,1)}), bf16[2048,2730]{1,0:T(8,128)(2,1)}) %all-gather.12.cloned.1.call-update) | async-done | bytes 11182096 | tf_op jit(solution)/shard_map/all_gather | solution.py:164
  105.9 6.6 fusion.244
  137.8 5.0 copy.155
  142.8 4.9 copy.182
  147.8 5.0 reshape.563
  160.2 4.5 copy.157
  169.2 18.9 while.84
  188.1 7.5 all-gather.3
  195.9 12.4 all-reduce.9
  210.4 205.7 %while.81 = (s32[]{:T(128)}, f32[1,2730]{1,0:T(1,128)S(1)}, f32[16,16,1,2730]{3,1,2,0:T(8,128)}, f32[16,16,1,2730]{3,2,1,0:T(1,128)}, f32[16,16,1,2730]{3,2,1,0:...) while((s32[]{:T(128)}, f32[1,2730]{1,0:T(1,128)S(1)}, ...), condition=%wide.region_7.8_spmd, body=%wide.region_6.7_spmd.sunk | while | flops 92836 | bytes 1256301 | solution.py:97
  430.5 5.7 all_gather.58
  436.2 12.8 multiply_convert_fusion.2
  449.1 8.2 multiply_reduce_fusion.7
  459.8 13.8 fusion.283
  473.6 128.6 %all-gather.20.cloned.1.call-done = bf16[2048,6144]{1,0:T(8,128)(2,1)} async-done(((bf16[64,6144]{1,0:T(8,128)(2,1)}), bf16[2048,6144]{1,0:T(8,128)(2,1)}) %all-gather.20.cloned.1.call-update) | async-done | bytes 25165840 | tf_op jit(solution)/shard_map/all_gather | solution.py:233
  602.2 13.8 fusion.284
  616.0 141.8 %all-gather.22.cloned.1.call-done = bf16[2048,6144]{1,0:T(8,128)(2,1)} async-done(((bf16[64,6144]{1,0:T(8,128)(2,1)}), bf16[2048,6144]{1,0:T(8,128)(2,1)}) %all-gather.22.cloned.1.call-update) | async-done | bytes 25165840 | tf_op jit(solution)/shard_map/all_gather | solution.py:234
  757.8 20.9 multiply_convert_fusion
  778.7 13.8 fusion.285
  792.5 16.0 multiply_reduce_fusion.5
  811.9 13.9 fusion.197
  829.2 6.4 copy.164
  835.6 18.8 while.85
  855.3 5.2 all-gather.4
  862.6 33.2 while.83
  895.8 8.5 multiply_reduce_fusion
  919.1 4.8 reshape.564
  940.6 11.6 multiply_reduce_fusion.3
  956.7 6.3 fusion.286
  964.2 9.8 fusion.182
  974.2 5.2 convolution_bitcast_fusion.1
  981.0 11.3 fusion.213
  994.0 9.6 fusion.240
  1003.7 11.4 fusion.202
  1016.3 21.4 fusion.287
  1037.7 21.5 fusion.288
  1060.5 21.4 convolution_bitcast_fusion
  1081.8 49.2 %copy.185 = f32[2048,6144]{1,0:T(8,128)} copy(f32[2048,6144]{0,1:T(8,128)} %convolution_bitcast_fusion) | data formatting | bytes 100663296
  1131.1 14.6 fusion.180
  1152.0 103.6 %all-reduce.18.cloned.1.call-done = f32[2,16,171,171]{2,3,0,1:T(8,128)} async-done(((f32[2,16,171,171]{2,3,0,1:T(8,128)}), f32[2,16,171,171]{2,3,0,1:T(8,128)}) %all-reduce.18.cloned.1.call-update) | async-done | bytes 3742864 | tf_op jit(solution)/shard_map/psum | solution.py:314
  1255.7 7.1 copy.178
  1262.8 242.2 %reduce-scatter.13.cloned.1.call-done = f32[64,2730]{1,0:T(8,128)} async-done(((f32[2048,2730]{1,0:T(8,128)}), f32[64,2730]{1,0:T(8,128)}) %reduce-scatter.13.cloned.1.call-update) | async-done | bytes 698896 | tf_op jit(solution)/shard_map/reduce_scatter | solution.py:310
  1505.0 252.3 %reduce-scatter.11.cloned.1.call-done = f32[64,2730]{1,0:T(8,128)} async-done(((f32[2048,2730]{1,0:T(8,128)}), f32[64,2730]{1,0:T(8,128)}) %reduce-scatter.11.cloned.1.call-update) | async-done | bytes 698896 | tf_op jit(solution)/shard_map/reduce_scatter | solution.py:309
  1757.3 252.6 %reduce-scatter.9.cloned.1.call-done = f32[64,2730]{1,0:T(8,128)} async-done(((f32[2048,2730]{1,0:T(8,128)}), f32[64,2730]{1,0:T(8,128)}) %reduce-scatter.9.cloned.1.call-update) | async-done | bytes 698896 | tf_op jit(solution)/shard_map/reduce_scatter | solution.py:308
  2009.9 440.6 %reduce-scatter.15.cloned.1.call-done = f32[64,6144]{1,0:T(8,128)} async-done(((f32[2048,6144]{1,0:T(8,128)}), f32[64,6144]{1,0:T(8,128)}) %reduce-scatter.15.cloned.1.call-update) | async-done | bytes 1572880 | tf_op jit(solution)/shard_map/reduce_scatter | solution.py:244
  2450.5 437.4 %reduce-scatter.17.cloned.1.call-done = f32[64,6144]{1,0:T(8,128)} async-done(((f32[2048,6144]{1,0:T(8,128)}), f32[64,6144]{1,0:T(8,128)}) %reduce-scatter.17.cloned.1.call-update) | async-done | bytes 1572880 | tf_op jit(solution)/shard_map/reduce_scatter | solution.py:245
  2888.0 437.4 %reduce-scatter.19.cloned.1.call-done = f32[64,6144]{1,0:T(8,128)} async-done(((f32[2048,6144]{1,0:T(8,128)}), f32[64,6144]{1,0:T(8,128)}) %reduce-scatter.19.cloned.1.call-update) | async-done | bytes 1572880
  (839 shorter events, 402.0 us)
Async XLA Ops:
  7.2 119.8 %copy-start = (bf16[2,16,171,171]{3,1,2,0:T(8,128)(2,1)S(1)}, bf16[2,16,171,171]{3,1,2,0:T(8,128)(2,1)}, u32[]{:S(2)}) copy-start(bf16[2,16,171,171]{3,1,2,0:T(8,128)(2,1)} %param.39) | copy-start | bytes 5614276
  7.2 51.5 %copy-start.65 = (u32[32]{0:T(128)S(1)}, u32[32]{0:T(128)}, u32[]{:S(2)}) copy-start(u32[32]{0:T(128)} %constant.219) | copy-start | bytes 388
  7.2 52.8 %copy-start.61 = (s32[1,256]{1,0:T(1,128)S(1)}, s32[1,256]{1,0:T(1,128)}, u32[]{:S(2)}) copy-start(s32[1,256]{1,0:T(1,128)} %param.29) | copy-start | bytes 3076
  7.2 51.3 %copy-start.41 = (f32[4,2730]{1,0:T(4,128)S(1)}, f32[4,2730]{1,0:T(4,128)}, u32[]{:S(2)}) copy-start(f32[4,2730]{1,0:T(4,128)} %param.41) | copy-start | bytes 131044
  7.2 51.4 %copy-start.39 = (f32[2730]{0:T(1024)S(1)}, f32[2730]{0:T(1024)}, u32[]{:S(2)}) copy-start(f32[2730]{0:T(1024)} %param.43) | copy-start | bytes 32764
  7.3 98.6 %all-gather.12.cloned.1.call-start = ((), (), s32[]{:S(2)}) async-start(), calls=%async_computation.6 | async-start | bytes 11894784 | tf_op jit(solution)/shard_map/all_gather | solution.py:164
  8.0 428.2 %all-gather.14.cloned.1.call-start = ((), (), s32[]{:S(2)}) async-start(), calls=%async_computation.7 | async-start | bytes 11894784 | tf_op jit(solution)/shard_map/all_gather | solution.py:165
  8.7 440.3 %all-gather.16.cloned.1.call-start = ((), (), s32[]{:S(2)}) async-start(), calls=%async_computation.8 | async-start | bytes 11894784 | tf_op jit(solution)/shard_map/all_gather | solution.py:166
  9.5 450.4 %all-gather.18.cloned.1.call-start = ((), (), s32[]{:S(2)}) async-start(), calls=%async_computation.9 | async-start | bytes 25952256 | tf_op jit(solution)/shard_map/all_gather | solution.py:232
  10.1 592.1 %all-gather.20.cloned.1.call-start = ((), (), s32[]{:S(2)}) async-start(), calls=%async_computation.10 | async-start | bytes 25952256 | tf_op jit(solution)/shard_map/all_gather | solution.py:233
  10.6 747.2 %all-gather.22.cloned.1.call-start = ((), (), s32[]{:S(2)}) async-start(), calls=%async_computation.11 | async-start | bytes 25952256 | tf_op jit(solution)/shard_map/all_gather | solution.py:234
  11.4 48.5 %collective-permute-start = (f32[1,3]{1,0:T(1,128)S(1)}, f32[1,3]{1,0:T(1,128)S(1)}, u32[]{:S(2)}, u32[]{:S(2)}) collective-permute-start(f32[1,3]{1,0:T(1,128)S(1)} %slice.1076), channel_id=1, source_target_pairs={{0,1},{1,2},{2,3},{4,5},{5,6},{6,7},{8,9},{9,10},{10,11},{12,13},{... | collective-permute-start | bytes 44 | tf_op jit(solution)/shard_map/ppermute | solution.py:19
  13.8 1135.7 %all-reduce.20.cloned.1.call-start = ((), (), s32[]{:S(2)}) async-start(), calls=%async_computation.19 | async-start | bytes 217088
  57.0 379.3 %copy-start.28 = (f32[2048]{0:T(1024)}, f32[2048]{0:T(1024)S(1)}, u32[]{:S(2)}) copy-start(f32[2048]{0:T(1024)S(1)} %convert_element_type.85) | copy-start | bytes 24580
  58.5 377.7 %copy-start.43 = (f32[256]{0:T(256)}, f32[256]{0:T(256)S(1)}, u32[]{:S(2)}) copy-start(f32[256]{0:T(256)S(1)} %fusion.226) | copy-start | bytes 3076
  58.7 57.0 %copy-start.31 = (f32[2730]{0:T(1024)}, f32[2730]{0:T(1024)S(1)}, u32[]{:S(2)}) copy-start(f32[2730]{0:T(1024)S(1)} %get-tuple-element.599) | copy-start | bytes 32764
  58.7 57.0 %copy-start.33 = (f32[2730]{0:T(1024)}, f32[2730]{0:T(1024)S(1)}, u32[]{:S(2)}) copy-start(f32[2730]{0:T(1024)S(1)} %get-tuple-element.600) | copy-start | bytes 32764
  58.7 57.0 %copy-start.35 = (f32[2730]{0:T(1024)}, f32[2730]{0:T(1024)S(1)}, u32[]{:S(2)}) copy-start(f32[2730]{0:T(1024)S(1)} %get-tuple-element.601) | copy-start | bytes 32764
  58.7 57.0 %copy-start.37 = (f32[2730]{0:T(1024)}, f32[2730]{0:T(1024)S(1)}, u32[]{:S(2)}) copy-start(f32[2730]{0:T(1024)S(1)} %get-tuple-element.602) | copy-start | bytes 32764
  60.1 55.6 %copy-start.48 = (f32[1,256]{1,0:T(1,128)}, f32[1,256]{1,0:T(1,128)S(1)}, u32[]{:S(2)}) copy-start(f32[1,256]{1,0:T(1,128)S(1)} %get-tuple-element.721) | copy-start | bytes 3076
  60.1 55.6 %copy-start.50 = (f32[1,256]{1,0:T(1,128)}, f32[1,256]{1,0:T(1,128)S(1)}, u32[]{:S(2)}) copy-start(f32[1,256]{1,0:T(1,128)S(1)} %get-tuple-element.738) | copy-start | bytes 3076
  60.1 55.6 %copy-start.52 = (f32[1,256]{1,0:T(1,128)}, f32[1,256]{1,0:T(1,128)S(1)}, u32[]{:S(2)}) copy-start(f32[1,256]{1,0:T(1,128)S(1)} %get-tuple-element.739) | copy-start | bytes 3076
  60.1 55.6 %copy-start.58 = (f32[2730]{0:T(1024)S(1)}, f32[2730]{0:T(1024)}, u32[]{:S(2)}) copy-start(f32[2730]{0:T(1024)} %param.42) | copy-start | bytes 32764
  112.6 3.0 collective-permute-start.1
  811.8 14.0 copy-start.10
  940.5 11.6 copy-start.32
  940.5 11.6 copy-start.34
  940.5 11.6 copy-start.36
  940.6 11.6 copy-start.38
  954.5 9.5 collective-permute-start.2
  964.2 9.9 copy-start.22
  974.1 281.6 %all-reduce.18.cloned.1.call-start = ((), (), s32[]{:S(2)}) async-start(), calls=%async_computation.17 | async-start | bytes 11534336 | tf_op jit(solution)/shard_map/psum | solution.py:314
  979.4 525.6 %reduce-scatter.13.cloned.1.call-start = ((), (), s32[]{:S(2)}) async-start(), calls=%async_computation.14 | async-start | bytes 23789568 | tf_op jit(solution)/shard_map/reduce_scatter | solution.py:310
  992.4 765.0 %reduce-scatter.11.cloned.1.call-start = ((), (), s32[]{:S(2)}) async-start(), calls=%async_computation.13 | async-start | bytes 23789568 | tf_op jit(solution)/shard_map/reduce_scatter | solution.py:309
  1003.6 1006.3 %reduce-scatter.9.cloned.1.call-start = ((), (), s32[]{:S(2)}) async-start(), calls=%async_computation.12 | async-start | bytes 23789568 | tf_op jit(solution)/shard_map/reduce_scatter | solution.py:308
  1015.1 1435.4 %reduce-scatter.15.cloned.1.call-start = ((), (), s32[]{:S(2)}) async-start(), calls=%async_computation.15 | async-start | bytes 51904512 | tf_op jit(solution)/shard_map/reduce_scatter | solution.py:244
  1037.7 1850.3 %reduce-scatter.17.cloned.1.call-start = ((), (), s32[]{:S(2)}) async-start(), calls=%async_computation.16 | async-start | bytes 51904512 | tf_op jit(solution)/shard_map/reduce_scatter | solution.py:245
  1059.2 2266.1 %reduce-scatter.19.cloned.1.call-start = ((), (), s32[]{:S(2)}) async-start(), calls=%async_computation.18 | async-start | bytes 51904512
  1131.0 14.6 copy-start.60
  1131.0 14.6 copy-start.62
  1131.1 14.6 copy-start.12
  1131.1 14.6 copy-start.30
  1131.1 14.6 copy-start.45
  1152.0 2173.4 %copy-start.47 = (f32[2,2730]{1,0:T(2,128)S(1)}, f32[2,2730]{1,0:T(2,128)}, u32[]{:S(2)}) copy-start(f32[2,2730]{1,0:T(2,128)} %get-tuple-element.1344) | copy-start | bytes 65524
  1152.0 2174.0 %copy-start.42 = (f32[4,2730]{1,0:T(4,128)S(1)}, f32[4,2730]{1,0:T(4,128)}, u32[]{:S(2)}) copy-start(f32[4,2730]{1,0:T(4,128)} %get-tuple-element.1345) | copy-start | bytes 131044
  1152.0 2174.6 %copy-start.57 = (f32[2730]{0:T(1024)S(1)}, f32[2730]{0:T(1024)}, u32[]{:S(2)}) copy-start(f32[2730]{0:T(1024)} %get-tuple-element.1346) | copy-start | bytes 32764
  1152.0 2175.2 %copy-start.56 = (f32[2730]{0:T(1024)S(1)}, f32[2730]{0:T(1024)}, u32[]{:S(2)}) copy-start(f32[2730]{0:T(1024)} %get-tuple-element.1347) | copy-start | bytes 32764
  1255.7 2072.2 %copy-start.1 = (bf16[2,16,171,171]{3,1,2,0:T(8,128)(2,1)S(1)}, bf16[2,16,171,171]{3,1,2,0:T(8,128)(2,1)}, u32[]{:S(2)}) copy-start(bf16[2,16,171,171]{3,1,2,0:T(8,128)(2,1)} %param.39) | copy-start | bytes 5614276
  (35 other events, 143.7 us)
Sparse Core Ops, SparseCore 0:
  10.9 94.8 all-gather.11
  108.7 89.5 all-gather.13
  201.2 89.5 all-gather.15
  293.6 153.0 all-gather.17
  449.3 152.8 all-gather.19
  604.9 152.8 all-gather.21
  974.2 123.3 all-reduce.19
  1103.3 152.3 all-reduce.17
  1258.6 246.4 reduce-scatter.12
  1507.7 249.5 reduce-scatter.10
  1760.2 249.6 reduce-scatter.8
  2016.8 433.6 reduce-scatter.14
  2457.5 430.3 reduce-scatter.16
  2894.8 430.5 reduce-scatter.18
where the time goes:
time: 3380 us; the launch traced here: 3330 us
  waiting for transfers between devices  2490 us (74%)
  other arithmetic  304 us (9%)
  matrix products  259 us (8%)
  local copies, waits for them, and re-layouts  188 us (6%)
  blocking collectives  73.3 us (2%)
    unnamed x16, waiting for transfers between devices  441 us
    reduce_scatter x1, waiting for transfers between devices, local(): lax.psum_scatter(grad_hgate, ('batch', 'seq'), scatter_dimension=0, tiled...  441 us
    reduce_scatter x1, waiting for transfers between devices, local(): lax.psum_scatter(grad_hlinear, ('batch', 'seq'), scatter_dimension=0, til...  437 us
    reduce_scatter x1, waiting for transfers between devices, local(): lax.psum_scatter(grad_branch, ('batch', 'seq'), scatter_dimension=0, tile...  253 us
    reduce_scatter x1, waiting for transfers between devices, local(): lax.psum_scatter(grad_gating, ('batch', 'seq'), scatter_dimension=0, tile...  252 us
    reduce_scatter x1, waiting for transfers between devices, local(): lax.psum_scatter(grad_output, ('batch', 'seq'), scatter_dimension=0, tile...  242 us
    while x256, other arithmetic  201 us
    all_gather x1, waiting for transfers between devices, local(): lax.all_gather(hidden_output, ('batch', 'seq'), axis=0, tiled=True)  142 us
  transfers between devices with their start and end apart: 17, of which 11 were waited for; matrix products, arithmetic and copies ran while one was open for 16% of the time, Pallas kernels for 0%

commit v1 on v0

v1 whole, which is shorter than its diff:
```python
import functools

import jax
import jax.numpy as jnp
from jax import lax
from jax.experimental import pallas as pl
from jax.experimental.pallas import tpu as pltpu
from jax.sharding import PartitionSpec as P

NBLK = 16
BLK = 171
NBIG = 10
KW = 4
R = 2730

EPSILON = 1e-06

GROUP = 8
AXES = ("batch", "seq")
PAD = 192
WIDE = 2 * PAD
SIZES = [BLK] * NBIG + [BLK - 1] * (NBLK - NBIG)
BEGINS = [sum(SIZES[:i]) for i in range(NBLK)]
ORDER = (0, 2, 4, 6, 1, 3, 5, 7)

BF16 = jnp.bfloat16
F32 = jnp.float32


def device_count():
    return lax.axis_size("batch") * lax.axis_size("seq")


def flat_index():
    return lax.axis_index("batch") * lax.axis_size("seq") + lax.axis_index("seq")


def swap(values, bit):
    return lax.ppermute(values, AXES, [(i, i ^ bit) for i in range(device_count())])


def onward(values):
    count = device_count()
    return lax.ppermute(values, AXES, [(i, (i + GROUP) % count) for i in range(count)])


def low(values):
    return values.astype(BF16)


def wide(values):
    return values.astype(F32)


def pick(values, index):
    return lax.dynamic_index_in_dim(values, index, 0, False)


def put(values, part, index):
    return lax.dynamic_update_index_in_dim(values, part, index, 0)


def after(values, *others):
    return lax.optimization_barrier((values,) + others)[0]


def exchange(pieces, place):
    out = jnp.zeros_like(pieces)
    for bit in range(GROUP):
        part = pick(pieces, place ^ bit)
        out = put(out, swap(part, bit) if bit else part, place ^ bit)
    return out


def ring_gather(block, turn, groups):
    out = jnp.broadcast_to(block, (groups,) + block.shape)
    arrivals = []
    for step in range(1, groups):
        block = onward(block)
        arrivals.append(block)
        out = put(out, block, (turn + groups - step) % groups)
    return out.reshape((-1,) + block.shape[1:]), arrivals


def ring_reduce(values, turn, groups):
    values = values.reshape((groups, -1) + values.shape[1:])
    total = pick(values, (turn + groups - 1) % groups)
    for step in range(1, groups):
        total = wide(onward(low(total))) + pick(values, (turn + 2 * groups - 1 - step) % groups)
    return total


def tiny_gather(values, place):
    for bit in (1, 2, 4):
        other = swap(values, bit)
        values = jnp.where(
            (place & bit) != 0,
            jnp.concatenate([other, values], axis=0),
            jnp.concatenate([values, other], axis=0),
        )
    return values


def group_gather(own):
    half = own.shape[0] // 2
    across, along = swap(own, 4), swap(own, 2)
    first, second = swap(across[:half], 2), swap(along[half:], 4)
    mine = [own, along, across, first, second]
    return jnp.concatenate(mine + [swap(part, 1) for part in mine], axis=0)


def group_reduce(near, far):
    near = near.reshape(4, -1, near.shape[-1])
    total = near + wide(swap(low(far), 1)).reshape(near.shape)
    half = near.shape[1] // 2
    first, second = swap(low(total[3, :half]), 4), swap(low(total[3, half:]), 2)
    across = swap(low(total[2, :half]), 4)
    along = swap(low(total[1, half:]), 2)
    across_rest = swap(low(total[2, half:] + wide(second)), 4)
    along_rest = swap(low(total[1, :half] + wide(first)), 2)
    return (
        total[0]
        + wide(jnp.concatenate([across, across_rest], axis=0))
        + wide(jnp.concatenate([along_rest, along], axis=0))
    )


def to_windows(values):
    leading = [(0, 0)] * (values.ndim - 1)
    parts = [
        jnp.pad(values[..., begin : begin + size], leading + [(0, PAD - size)])
        for begin, size in zip(BEGINS, SIZES)
    ]
    return jnp.concatenate(parts, axis=-1).reshape(values.shape[:-1] + (GROUP, WIDE))


def from_windows(values):
    flat = values.reshape(values.shape[:-2] + (GROUP * WIDE,))
    parts = [flat[..., i * PAD : i * PAD + size] for i, size in enumerate(SIZES)]
    return jnp.concatenate(parts, axis=-1)


def rms_scale(values):
    return lax.rsqrt(jnp.mean(values * values, axis=-1, keepdims=True) + EPSILON)


def norm_back(values, scale, gain, grads):
    scaled = grads * gain
    return scale * (
        scaled - values * scale * scale * jnp.mean(scaled * values, axis=-1, keepdims=True)
    )


def product(left, right):
    return jnp.dot(left, right, preferred_element_type=F32)


def contract_rows(left, right):
    return lax.dot_general(left, right, (((0,), (0,)), ((), ())), preferred_element_type=F32)


def contract_cols(left, right):
    return lax.dot_general(left, right, (((1,), (1,)), ((), ())), preferred_element_type=F32)


def reduce_product(left, right):
    half = left.shape[0] // 2
    far = low(contract_cols(left[half:], right))
    return group_reduce(contract_cols(left[:half], right), far)


def sigmoid(values):
    return 1.0 / (1.0 + jnp.exp(-values))


GELU_A = 0.7978845608028654
GELU_B = 0.044715


def gelu_both(values):
    square = values * values
    bent = jnp.tanh(GELU_A * values * (1.0 + GELU_B * square))
    value = 0.5 * values * (1.0 + bent)
    slope = 0.5 * (1.0 + bent) + 0.5 * values * (1.0 - bent * bent) * GELU_A * (
        1.0 + 3.0 * GELU_B * square
    )
    return value, slope


def minus_expm1(values):
    series = 1.0 / 40320.0
    for divisor in (5040.0, 720.0, 120.0, 24.0, 6.0, 2.0, 1.0):
        series = series * values + 1.0 / divisor
    return -values * series


def gate_values(conv, masks, weight, bias, rate):
    pre = product(low(conv), weight) + bias
    width = conv.shape[1]
    recur, enter = sigmoid(pre[:, :width]), sigmoid(pre[:, width:])
    log_decay = rate * recur
    decay = jnp.exp(log_decay)
    raw_scale = jnp.sqrt(minus_expm1(2.0 * log_decay))
    fresh = masks[:, 3:4] > 0.5
    carry = jnp.where(fresh, 0.0, decay)
    scale = jnp.where(fresh, 1.0, raw_scale)
    return recur, enter, decay, raw_scale, fresh, carry, scale


def convolve(padded, masks, params, steps):
    conv = params[6:7] + params[2:3] * padded[8 : 8 + steps]
    for offset in range(1, KW):
        conv = conv + params[2 + offset : 3 + offset] * (
            padded[8 - offset : 8 - offset + steps] * masks[:, offset - 1 : offset]
        )
    return conv


def forward_kernel(
    place, pre, masks, weight, bias, params, state_out, mixed_out, padded, mult, partial, chain
):
    steps, width = padded.shape[0] - 8, padded.shape[1]
    chunk = steps // 8

    @pl.when(pl.program_id(1) == 0)
    def _():
        padded[0:8] = jnp.zeros((8, width), F32)
        chain[...] = jnp.zeros_like(chain)

    @pl.when(pl.program_id(1) > 0)
    def _():
        padded[0:8] = padded[steps : steps + 8]

    padded[8 : 8 + steps] = pre[0, :, :width]
    conv = convolve(padded, masks[0], params, steps)
    recur, enter, decay, raw_scale, fresh, carry, scale = gate_values(
        conv, masks[0], weight[...], bias[...], params[7:8]
    )
    for lane in range(width // 128):
        lanes = slice(lane * 128, lane * 128 + 128)
        mult[lane] = carry[:, lanes]
        partial[lane] = (scale * enter * conv)[:, lanes]
    for lane in range(width // 128):
        state = jnp.zeros((8, 128), F32)
        reach = jnp.ones((8, 128), F32)
        for step in range(chunk):
            rows = pl.ds(step, 8, stride=chunk)
            factor = mult[lane, rows, :]
            state = factor * state + partial[lane, rows, :]
            reach = factor * reach
            partial[lane, rows, :] = state
            mult[lane, rows, :] = reach
        lanes = slice(lane * 128, lane * 128 + 128)
        entering = chain[0:1, lanes]
        for part in range(8):
            rows = slice(part * chunk, part * chunk + chunk)
            state_out[0, rows, lanes] = partial[lane, rows, :] + mult[lane, rows, :] * entering
            entering = state[part : part + 1] + reach[part : part + 1] * entering
        chain[0:1, lanes] = entering
    value, _ = gelu_both(pre[0, :, width:])
    mixed_out[0] = low(state_out[0] * value)


def backward_kernel(
    place,
    pre,
    rim,
    masks,
    state,
    state_rim,
    d_mixed,
    weight,
    bias,
    params,
    d_both,
    grad_gate,
    grad_small,
    padded,
    mult,
    partial,
    adjoint_all,
    chain,
    later,
):
    steps, width = padded.shape[0] - 8, padded.shape[1]
    chunk = steps // 8
    last = pl.program_id(1) == 0

    @pl.when(last & (pl.program_id(0) == 0))
    def _():
        grad_gate[...] = jnp.zeros_like(grad_gate)
        grad_small[...] = jnp.zeros_like(grad_small)

    @pl.when(last)
    def _():
        chain[...] = jnp.zeros_like(chain)
        later[:, steps : steps + 8] = jnp.zeros((KW - 1, 8, width), F32)

    @pl.when(jnp.logical_not(last))
    def _():
        later[:, steps : steps + 8] = later[:, 0:8]

    mask = masks[0]
    padded[0:8] = rim[0]
    padded[8 : 8 + steps] = pre[0, :, :width]
    conv = convolve(padded, mask, params, steps)
    recur, enter, decay, raw_scale, fresh, carry, scale = gate_values(
        conv, mask, weight[...], bias[...], params[7:8]
    )
    value, slope = gelu_both(pre[0, :, width:])
    d_out = d_mixed[0]
    d_both[0, :, width:] = low(d_out * state[0] * slope)
    d_state = d_out * value
    for lane in range(width // 128):
        lanes = slice(lane * 128, lane * 128 + 128)
        mult[lane, 0:steps, :] = carry[:, lanes]
        mult[lane, steps : steps + 8, :] = jnp.ones((8, 128), F32)
        partial[lane] = d_state[:, lanes]
    for lane in range(width // 128):
        lanes = slice(lane * 128, lane * 128 + 128)
        first_mult = mult[lane, 0:1, :]
        total = jnp.zeros((8, 128), F32)
        reach = jnp.ones((8, 128), F32)
        for step in reversed(range(chunk)):
            rows = pl.ds(step, 8, stride=chunk)
            factor = mult[lane, pl.ds(step + 1, 8, stride=chunk), :]
            total = factor * total + partial[lane, rows, :]
            reach = factor * reach
            partial[lane, rows, :] = total
            mult[lane, pl.ds(step + 1, 8, stride=chunk), :] = reach
        entering = chain[0:1, lanes]
        for part in reversed(range(8)):
            begin = part * chunk
            adjoint_all[begin : begin + chunk, lanes] = (
                partial[lane, begin : begin + chunk, :]
                + mult[lane, begin + 1 : begin + 1 + chunk, :] * entering
            )
            entering = total[part : part + 1] + reach[part : part + 1] * entering
        chain[0:1, lanes] = first_mult * entering
    adjoint = adjoint_all[...]
    padded_state = jnp.concatenate([state_rim[0, 7:8], state[0, : steps - 1]], axis=0)
    d_scale = adjoint * enter * conv
    d_enter = adjoint * scale * conv
    d_log = jnp.where(
        fresh, 0.0, decay * (adjoint * padded_state - d_scale * decay / raw_scale)
    )
    d_recur_pre = d_log * params[7:8] * recur * (1.0 - recur)
    d_enter_pre = d_enter * enter * (1.0 - enter)
    d_pre = jnp.concatenate([d_recur_pre, d_enter_pre], axis=1)
    d_pre_low = low(d_pre)
    d_conv = adjoint * scale * enter + contract_cols(d_pre_low, weight[...])
    grad_gate[...] += contract_rows(low(conv), d_pre_low)
    sums = [
        jnp.sum(d_recur_pre, axis=0, keepdims=True),
        jnp.sum(d_enter_pre, axis=0, keepdims=True),
        jnp.sum(d_conv * padded[8 : 8 + steps], axis=0, keepdims=True),
    ]
    d_branch = d_conv * params[2:3]
    for offset in range(1, KW):
        masked = d_conv * mask[:, offset - 1 : offset]
        sums.append(
            jnp.sum(masked * padded[8 - offset : 8 - offset + steps], axis=0, keepdims=True)
        )
        later[offset - 1, 0:steps] = masked * params[2 + offset : 3 + offset]
        d_branch = d_branch + later[offset - 1, offset : offset + steps]
    sums.append(jnp.sum(d_conv, axis=0, keepdims=True))
    sums.append(jnp.sum(d_log * recur, axis=0, keepdims=True))
    for row, value_sum in enumerate(sums):
        grad_small[row : row + 1] += value_sum
    d_both[0, :, :width] = low(d_branch)


def mixer_calls(rows, shards, steps, channels):
    blocks = rows * shards

    def position(row, shard, place):
        offset = (row * shards + shard) ^ place
        return (offset // 2) + (offset % 2) * (GROUP // 2)

    def whole(*dims):
        return pl.BlockSpec(dims, lambda row, shard, place: (0,) * len(dims))

    params = pltpu.CompilerParams(
        dimension_semantics=("arbitrary", "arbitrary"), vmem_limit_bytes=48 * 1024 * 1024
    )
    lanes = channels // 128
    forward = pl.pallas_call(
        forward_kernel,
        grid_spec=pltpu.PrefetchScalarGridSpec(
            num_scalar_prefetch=1,
            grid=(rows, shards),
            in_specs=[
                pl.BlockSpec(
                    (1, steps, 2 * channels), lambda r, s, p: (position(r, s, p[0]), 0, 0)
                ),
                pl.BlockSpec((1, steps, 8), lambda r, s, p: (r * shards + s, 0, 0)),
                whole(channels, 2 * channels),
                whole(1, 2 * channels),
                whole(8, channels),
            ],
            out_specs=[
                pl.BlockSpec((1, steps, channels), lambda r, s, p: (r * shards + s, 0, 0)),
                pl.BlockSpec((1, steps, channels), lambda r, s, p: (position(r, s, p[0]), 0, 0)),
            ],
            scratch_shapes=[
                pltpu.VMEM((steps + 8, channels), F32),
                pltpu.VMEM((lanes, steps, 128), F32),
                pltpu.VMEM((lanes, steps, 128), F32),
                pltpu.VMEM((8, channels), F32),
            ],
        ),
        out_shape=[
            jax.ShapeDtypeStruct((blocks, steps, channels), F32),
            jax.ShapeDtypeStruct((blocks, steps, channels), BF16),
        ],
        compiler_params=params,
        cost_estimate=pl.CostEstimate(
            flops=blocks * steps * channels * channels * 4,
            bytes_accessed=blocks * steps * channels * 14,
            transcendentals=blocks * steps * channels * 6,
        ),
        name="mixer_forward",
    )

    def turned(shard):
        return shards - 1 - shard

    def before(shard):
        return jnp.maximum(shards - 2 - shard, 0)

    backward = pl.pallas_call(
        backward_kernel,
        grid_spec=pltpu.PrefetchScalarGridSpec(
            num_scalar_prefetch=1,
            grid=(rows, shards),
            in_specs=[
                pl.BlockSpec(
                    (1, steps, 2 * channels), lambda r, s, p: (position(r, turned(s), p[0]), 0, 0)
                ),
                pl.BlockSpec(
                    (1, 8, channels),
                    lambda r, s, p: (position(r, before(s), p[0]), steps // 8 - 1, 0),
                ),
                pl.BlockSpec((1, steps, 8), lambda r, s, p: (r * shards + turned(s), 0, 0)),
                pl.BlockSpec((1, steps, channels), lambda r, s, p: (r * shards + turned(s), 0, 0)),
                pl.BlockSpec(
                    (1, 8, channels),
                    lambda r, s, p: (r * shards + before(s), steps // 8 - 1, 0),
                ),
                pl.BlockSpec(
                    (1, steps, channels), lambda r, s, p: (position(r, turned(s), p[0]), 0, 0)
                ),
                whole(channels, 2 * channels),
                whole(1, 2 * channels),
                whole(8, channels),
            ],
            out_specs=[
                pl.BlockSpec(
                    (1, steps, 2 * channels), lambda r, s, p: (position(r, turned(s), p[0]), 0, 0)
                ),
                whole(channels, 2 * channels),
                whole(8, channels),
            ],
            scratch_shapes=[
                pltpu.VMEM((steps + 8, channels), F32),
                pltpu.VMEM((lanes, steps + 8, 128), F32),
                pltpu.VMEM((lanes, steps, 128), F32),
                pltpu.VMEM((steps, channels), F32),
                pltpu.VMEM((8, channels), F32),
                pltpu.VMEM((KW - 1, steps + 8, channels), F32),
            ],
        ),
        out_shape=[
            jax.ShapeDtypeStruct((blocks, steps, 2 * channels), BF16),
            jax.ShapeDtypeStruct((channels, 2 * channels), F32),
            jax.ShapeDtypeStruct((8, channels), F32),
        ],
        compiler_params=params,
        cost_estimate=pl.CostEstimate(
            flops=blocks * steps * channels * channels * 12,
            bytes_accessed=blocks * steps * channels * 24,
            transcendentals=blocks * steps * channels * 8,
        ),
        name="mixer_backward",
    )
    return forward, backward


def local(
    stream_in,
    segment_ids,
    out_grad,
    branch_weight,
    gating_weight,
    output_weight,
    hidden_gate,
    hidden_linear,
    hidden_output,
    mixer_gain,
    hidden_gain,
    gate_blocks,
    gate_biases,
    conv_taps,
    conv_bias,
    decay_param,
):
    rows_here, steps, model_width = stream_in.shape
    shards = lax.axis_size("seq")
    rows = GROUP // shards
    assert rows_here == 1 and rows * shards == GROUP
    groups = device_count() // GROUP
    place = flat_index() % GROUP
    turn = flat_index() // GROUP
    own_rows, hidden_width = hidden_gate.shape
    hidden_part = hidden_width // GROUP
    tokens = GROUP * steps

    tiny = jnp.concatenate(
        [wide(mixer_gain)[None], wide(hidden_gain)[None], wide(segment_ids)], axis=1
    )
    tiny = tiny_gather(tiny, place)
    gains, _ = ring_gather(tiny[:, : 2 * own_rows], turn, groups)
    mixer_scale = gains[:, :own_rows].reshape(1, model_width)
    hidden_scale = gains[:, own_rows:].reshape(1, model_width)
    segments = tiny[:, 2 * own_rows :].reshape(rows, shards * steps)
    flags = []
    for offset in range(1, KW):
        flags.append(
            jnp.pad(
                wide(segments[:, offset:] == segments[:, :-offset]), ((0, 0), (offset, 0))
            )
        )
    flags.append(1.0 - flags[0])
    flags = flags + [jnp.zeros_like(flags[0])] * 4
    masks = jnp.stack(flags, axis=-1).reshape(GROUP, steps, 8)

    mixer_pieces = jnp.concatenate(
        [to_windows(branch_weight), to_windows(gating_weight), to_windows(output_weight)], axis=-1
    )
    mixer_pieces = exchange(jnp.swapaxes(mixer_pieces, 0, 1), place).reshape(-1, 3 * WIDE)
    hidden_pieces = jnp.concatenate(
        [
            hidden_gate.reshape(own_rows, GROUP, hidden_part),
            hidden_linear.reshape(own_rows, GROUP, hidden_part),
            hidden_output.reshape(own_rows, GROUP, hidden_part),
        ],
        axis=-1,
    )
    hidden_pieces = exchange(
        after(jnp.swapaxes(hidden_pieces, 0, 1), mixer_pieces), place
    ).reshape(-1, 3 * hidden_part)
    both_weight, arrivals = ring_gather(mixer_pieces[:, : 2 * WIDE], turn, groups)
    out_weight, arrivals = ring_gather(
        after(mixer_pieces[:, 2 * WIDE :], arrivals[-2]), turn, groups
    )
    pair_weight, arrivals = ring_gather(
        after(hidden_pieces[:, : 2 * hidden_part], arrivals[-2]), turn, groups
    )
    last_weight, arrivals = ring_gather(
        after(hidden_pieces[:, 2 * hidden_part :], arrivals[-2]), turn, groups
    )

    inputs = wide(stream_in).reshape(steps, model_width)
    inputs_scale = rms_scale(inputs)
    normed = group_gather(low(inputs * inputs_scale * mixer_scale))
    upstream = wide(out_grad).reshape(steps, model_width)
    upstream_all = group_gather(after(out_grad.reshape(steps, model_width), normed))
    pre = product(normed, both_weight).reshape(GROUP, steps, 2 * WIDE)

    rate = -8.0 * jax.nn.softplus(-decay_param)
    params = jnp.concatenate(
        [gate_biases, conv_taps, conv_bias[None], rate[None]], axis=0
    )
    params = pick(jnp.swapaxes(to_windows(params), 0, 1), place)
    bias = params[:2].reshape(1, 2 * WIDE)
    params = params.at[7].set(jnp.where(params[7] == 0.0, -0.01, params[7]))
    blocks = lax.dynamic_slice_in_dim(gate_blocks, 2 * place, 2, 1)
    blocks = jnp.pad(blocks, ((0, 0), (0, 0), (0, PAD - BLK), (0, PAD - BLK)))
    empty = jnp.zeros((PAD, PAD), BF16)
    gate_weight = jnp.concatenate(
        [
            jnp.concatenate([blocks[0, 0], empty, blocks[1, 0], empty], axis=1),
            jnp.concatenate([empty, blocks[0, 1], empty, blocks[1, 1]], axis=1),
        ],
        axis=0,
    )
    mixer_forward, mixer_backward = mixer_calls(rows, shards, steps, WIDE)
    where = place.astype(jnp.int32).reshape(1)
    state, mixed = mixer_forward(where, pre, masks, gate_weight, bias, params)
    mixed = mixed.reshape(tokens, WIDE)
    middle = inputs + reduce_product(mixed, out_weight)

    middle_scale = rms_scale(middle)
    normed_mid = group_gather(low(middle * middle_scale * hidden_scale))
    pair = product(normed_mid, pair_weight)
    gate_pre, linear_pre = pair[:, :hidden_part], pair[:, hidden_part:]
    value, slope = gelu_both(gate_pre)
    hidden = low(value * linear_pre)
    d_hidden = product(upstream_all, last_weight)
    d_pair = jnp.concatenate(
        [low(d_hidden * linear_pre * slope), low(d_hidden * value)], axis=1
    )
    d_middle = upstream + norm_back(
        middle, middle_scale, hidden_scale, reduce_product(d_pair, pair_weight)
    )
    result = low(middle + reduce_product(hidden, last_weight))
    grad_pair = ring_reduce(contract_rows(normed_mid, d_pair), turn, groups)
    grad_last = ring_reduce(contract_rows(upstream_all, hidden), turn, groups)

    middle_low = group_gather(low(d_middle))
    d_mixed = product(middle_low, out_weight).reshape(GROUP, steps, WIDE)
    d_both, grad_gate, grad_small = mixer_backward(
        where, pre, pre, masks, state, state, d_mixed, gate_weight, bias, params
    )
    d_both = d_both.reshape(tokens, 2 * WIDE)
    stream_grad = low(
        d_middle
        + norm_back(inputs, inputs_scale, mixer_scale, reduce_product(d_both, both_weight))
    )
    grad_out = ring_reduce(contract_rows(middle_low, mixed), turn, groups)
    grad_both = ring_reduce(contract_rows(normed, d_both), turn, groups)

    def to_owner(grads):
        return wide(exchange(low(grads).reshape(GROUP, own_rows, -1), place))

    def hidden_rows(grads):
        return jnp.swapaxes(grads, 0, 1).reshape(own_rows, hidden_width)

    def mixer_rows(grads):
        return from_windows(jnp.swapaxes(grads, 0, 1))

    grad_pair, grad_last = to_owner(grad_pair), to_owner(grad_last)
    grad_both, grad_out = to_owner(grad_both), to_owner(grad_out)
    grad_hgate = hidden_rows(grad_pair[..., :hidden_part])
    grad_hlinear = hidden_rows(grad_pair[..., hidden_part:])
    grad_houtput = hidden_rows(grad_last)
    grad_branch = mixer_rows(grad_both[..., :WIDE])
    grad_gating = mixer_rows(grad_both[..., WIDE:])
    grad_output = mixer_rows(grad_out)
    grad_hgain = jnp.sum(
        wide(hidden_gate) * grad_hgate + wide(hidden_linear) * grad_hlinear, axis=1
    ) / wide(hidden_gain)
    grad_mgain = jnp.sum(
        wide(branch_weight) * grad_branch + wide(gating_weight) * grad_gating, axis=1
    ) / wide(mixer_gain)

    upper = lax.broadcasted_iota(jnp.int32, (PAD, 2 * WIDE), 1) % WIDE < PAD
    packed = low(jnp.where(upper, grad_gate[:PAD], grad_gate[PAD:]))
    packed, _ = ring_gather(packed, turn, groups)
    packed = low(jnp.sum(wide(packed.reshape(groups, PAD, 2 * WIDE)), axis=0))
    packed = wide(tiny_gather(packed[None], place))
    packed = packed.reshape(GROUP, PAD, 2, 2, PAD).transpose(2, 0, 3, 1, 4)
    grad_gblocks = packed.reshape(2, NBLK, PAD, PAD)[:, :, :BLK, :BLK]
    small, _ = ring_gather(grad_small, turn, groups)
    small = jnp.sum(small.reshape(groups, 8, WIDE), axis=0)
    small = from_windows(jnp.swapaxes(tiny_gather(small[None], place), 0, 1))
    grad_decay = 8.0 * jax.nn.sigmoid(-decay_param) * small[7]

    shape = (rows_here, steps, model_width)
    return (
        result.reshape(shape),
        stream_grad.reshape(shape),
        grad_branch,
        grad_gating,
        grad_output,
        grad_hgate,
        grad_hlinear,
        grad_houtput,
        grad_mgain,
        grad_hgain,
        grad_gblocks,
        small[:2],
        small[2:6],
        small[6],
        grad_decay,
    )


def solution(mesh):
    return jax.shard_map(
        local,
        mesh=mesh,
        in_specs=(
            P("batch", "seq", None),
            P("batch", "seq"),
            P("batch", "seq", None),
            P(("batch", "seq"), None),
            P(("batch", "seq"), None),
            P(("batch", "seq"), None),
            P(("batch", "seq"), None),
            P(("batch", "seq"), None),
            P(("batch", "seq"), None),
            P(("batch", "seq")),
            P(("batch", "seq")),
            P(),
            P(),
            P(),
            P(),
            P(),
        ),
        out_specs=(
            P("batch", "seq", None),
            P("batch", "seq", None),
            P(("batch", "seq"), None),
            P(("batch", "seq"), None),
            P(("batch", "seq"), None),
            P(("batch", "seq"), None),
            P(("batch", "seq"), None),
            P(("batch", "seq"), None),
            P(("batch", "seq")),
            P(("batch", "seq")),
            P(),
            P(),
            P(),
            P(),
            P(),
        ),
        check_vma=False,
    )
```

time: 3380 us -> 1190 us (0.35)
  waiting for transfers between devices: 2490 us -> 455 us
  other arithmetic: 304 us -> 81.8 us
  local copies, waits for them, and re-layouts: 188 us -> 331 us
  matrix products: 259 us -> 153 us
  starting transfers between devices: 6.84 us -> 94.7 us
  blocking collectives: 73.3 us -> 0 us
  Pallas kernels: 0 us -> 51.4 us
    reduce_scatter x5 -> x0, waiting for transfers between devices: 1630 us -> none  [the longest x1 441 us: local(): lax.psum_scatter(grad_hgate, ('batch', 'seq'), scatter_dimension=0, tiled...]
    ppermute x3 -> x148, waiting for transfers between devices: 0.6 us -> 455 us  [the longest x33 284 us: onward(): lax.ppermute(values, AXES, [(i, (i + GROUP) % count) for i in range(count)])]
    unnamed x16 -> x0, waiting for transfers between devices: 441 us -> none
    all_gather x6 -> x0, waiting for transfers between devices: 316 us -> none  [the longest x1 142 us: local(): lax.all_gather(hidden_output, ('batch', 'seq'), axis=0, tiled=True)]
    while x256 -> x0, other arithmetic: 201 us -> none
    dynamic_update_slice x32 -> x68, local copies, waits for them, and re-layouts: 22.1 us -> 130 us  [put(): return lax.dynamic_update_index_in_dim(values, part, index, 0)]
    psum x1 -> x0, waiting for transfers between devices: 104 us -> none  [local(): lax.psum((grad_gblocks, grad_gbias, grad_taps, grad_cbias, grad_decay), (...]
    ppermute x3 -> x148, starting transfers between devices: 6.28 us -> 94.7 us  [the longest x115 83.7 us: swap(): lax.ppermute(values, AXES, [(i, i ^ bit) for i in range(device_count())])]
  transfers between devices with their start and end apart: 17 -> 148, of which waited for: 11 -> 54; matrix products, arithmetic and copies ran while one was open for 16% -> 42% of each run, Pallas kernels for 0% -> 2%
where the time goes in v1:
time: 1190 us; the launch traced here: 1170 us
  waiting for transfers between devices  455 us (38%)
  local copies, waits for them, and re-layouts  331 us (28%)
  matrix products  153 us (13%)
  starting transfers between devices  94.7 us (8%)
  other arithmetic  81.8 us (7%)
  Pallas kernels  51.4 us (4%)
    ppermute x33, waiting for transfers between devices, onward(): lax.ppermute(values, AXES, [(i, (i + GROUP) % count) for i in range(count)])  284 us
    ppermute x115, waiting for transfers between devices, swap(): lax.ppermute(values, AXES, [(i, i ^ bit) for i in range(device_count())])  171 us
    dynamic_update_slice x68, local copies, waits for them, and re-layouts, put(): return lax.dynamic_update_index_in_dim(values, part, index, 0)  130 us
    ppermute x115, starting transfers between devices, swap(): lax.ppermute(values, AXES, [(i, i ^ bit) for i in range(device_count())])  83.7 us
    dot_general x8, matrix products, contract_cols(): lax.dot_general(left, right, (((1,), (1,)), ((), ())), preferred_element_...  60.3 us
    dot_general x4, matrix products, product(): return jnp.dot(left, right, preferred_element_type=F32)  48.5 us
    unnamed x274, local copies, waits for them, and re-layouts  45.2 us
    dot_general x4, matrix products, contract_rows(): lax.dot_general(left, right, (((0,), (0,)), ((), ())), preferred_element_...  44.6 us
  transfers between devices with their start and end apart: 148, of which 54 were waited for; matrix products, arithmetic and copies ran while one was open for 42% of the time, Pallas kernels for 2%

profile of v1, /device:TPU:0, one launch (start us, length us, event | category | flops | bytes accessed | tf_op | source)
XLA Modules:
  0.0 1172.2 jit_solution(3138316179707579246)
XLA Ops:
  57.6 8.1 constant_dynamic-slice_fusion.10
  140.8 16.8 %collective-permute-done.45 = bf16[64,2304]{1,0:T(8,128)(2,1)S(1)} collective-permute-done((bf16[64,2304]{1,0:T(8,128)(2,1)S(1)}, bf16[64,2304]{1,0:T(8,128)(2,1)S(1)}, u32[]{:S(2)}, u32[]{:S(2)}) %collective-permute-start.45) | collective-permute-done | bytes 294944 | tf_op jit(solution)/shard_map/ppermute | solution.py:39
  158.8 8.1 collective-permute-done.46
  168.2 7.7 collective-permute-done.47
  178.7 12.5 %collective-permute-done.8 = bf16[128,2048]{1,0:T(8,128)(2,1)S(1)} collective-permute-done((bf16[128,2048]{1,0:T(8,128)(2,1)S(1)}, bf16[128,2048]{1,0:T(8,128)(2,1)S(1)}, u32[]{:S(2)}, u32[]{:S(2)}) %collective-permute-start.8) | collective-permute-done | bytes 524320 | tf_op jit(solution)/shard_map/ppermute | solution.py:39
  198.7 13.1 %collective-permute-done.25 = bf16[512,384]{1,0:T(8,128)(2,1)S(1)} collective-permute-done((bf16[512,384]{1,0:T(8,128)(2,1)S(1)}, bf16[512,384]{1,0:T(8,128)(2,1)S(1)}, u32[]{:S(2)}, u32[]{:S(2)}) %collective-permute-start.25) | collective-permute-done | bytes 393248 | tf_op jit(solution)/shard_map/ppermute | solution.py:44
  215.4 26.9 %collective-permute-done.26 = bf16[512,384]{1,0:T(8,128)(2,1)S(1)} collective-permute-done((bf16[512,384]{1,0:T(8,128)(2,1)S(1)}, bf16[512,384]{1,0:T(8,128)(2,1)S(1)}, u32[]{:S(2)}, u32[]{:S(2)}) %collective-permute-start.26) | collective-permute-done | bytes 393248 | tf_op jit(solution)/shard_map/ppermute | solution.py:44
  242.8 8.5 fusion.101.pre.rim
  251.3 20.4 %mixer_forward.1 = (f32[8,256,384]{2,1,0:T(8,128)}, bf16[8,256,384]{2,1,0:T(8,128)(2,1)S(1)}) custom-call(s32[1]{0:T(128)} %bitcast.place, f32[8,256,768]{2,1,0:T(8,128)} %fusion.101.pre.rim, f32[8,256,8]{2,1,0:T(8,128)S(1)} %stack.29.masks, bf16[384,768]{1,0:T(8,128)(2,1)S(1)} %maximum_maximum_fusion.weight, f32[1,768]{1,0:T(1,128)S(1)} %bitcast.553, ...), custom_call_target="tpu_custom_call" | custom-call | flops 1207959552 | bytes 11010048 | tf_op jit(solution)/shard_map/mixer_forward/pallas_call | solution.py:589
  285.2 17.8 %collective-permute-done.65 = bf16[256,2048]{1,0:T(8,128)(2,1)} collective-permute-done((bf16[256,2048]{1,0:T(8,128)(2,1)}, bf16[256,2048]{1,0:T(8,128)(2,1)}, u32[]{:S(2)}, u32[]{:S(2)}) %collective-permute-start.65) | collective-permute-done | bytes 1048608 | tf_op jit(solution)/shard_map/ppermute | solution.py:39
  307.8 12.3 %copy.232 = bf16[2048,2048]{1,0:T(8,128)(2,1)} copy(bf16[2048,2048]{0,1:T(8,128)(2,1)} %bitcast.561) | data formatting | bytes 16777216 | tf_op jit(solution)/shard_map/dot_general | solution.py:159
  353.1 28.0 %collective-permute-done.52 = bf16[512,1536]{1,0:T(8,128)(2,1)S(1)} collective-permute-done((bf16[512,1536]{1,0:T(8,128)(2,1)}, bf16[512,1536]{1,0:T(8,128)(2,1)S(1)}, u32[]{:S(2)}, u32[]{:S(2)}) %collective-permute-start.52) | collective-permute-done | bytes 1572896 | tf_op jit(solution)/shard_map/ppermute | solution.py:44
  385.9 16.5 %collective-permute-done.54 = bf16[512,768]{1,0:T(8,128)(2,1)S(1)} collective-permute-done((bf16[512,768]{1,0:T(8,128)(2,1)S(1)}, bf16[512,768]{1,0:T(8,128)(2,1)S(1)}, u32[]{:S(2)}, u32[]{:S(2)}) %collective-permute-start.54) | collective-permute-done | bytes 786464 | tf_op jit(solution)/shard_map/ppermute | solution.py:44
  410.9 45.5 %collective-permute-done.55 = bf16[512,768]{1,0:T(8,128)(2,1)S(1)} collective-permute-done((bf16[512,768]{1,0:T(8,128)(2,1)S(1)}, bf16[512,768]{1,0:T(8,128)(2,1)S(1)}, u32[]{:S(2)}, u32[]{:S(2)}) %collective-permute-start.55) | collective-permute-done | bytes 786464 | tf_op jit(solution)/shard_map/ppermute | solution.py:44
  459.2 16.5 %collective-permute-done.56 = bf16[512,768]{1,0:T(8,128)(2,1)S(1)} collective-permute-done((bf16[512,768]{1,0:T(8,128)(2,1)S(1)}, bf16[512,768]{1,0:T(8,128)(2,1)S(1)}, u32[]{:S(2)}, u32[]{:S(2)}) %collective-permute-start.56) | collective-permute-done | bytes 786464 | tf_op jit(solution)/shard_map/ppermute | solution.py:44
  481.5 15.9 %fusion.102 = f32[2048,1536]{1,0:T(8,128)} fusion(bf16[2048,2048]{1,0:T(8,128)(2,1)S(1)} %constant_dynamic-update-slice_fusion.13, bf16[2048,1536]{1,0:T(8,128)(2,1)S(1)} %bitcast.578), kind=kOutput, calls=%fused_computation.371 | convolution fusion | flops 12884901888 | bytes 27262976 | tf_op jit(solution)/shard_map/dot_general | solution.py:155
  497.5 17.7 %multiply_convert_fusion = (bf16[2048,768]{1,0:T(8,128)(2,1)}, bf16[2048,768]{1,0:T(8,128)(2,1)}, bf16[2048,768]{1,0:T(8,128)(2,1)}) fusion(f32[2048,1536]{1,0:T(8,128)} %fusion.102, bf16[2048,2048]{1,0:T(8,128)(2,1)} %constant_dynamic-update-slice_fusion.23, bf16[2048,768]{1,0:T(8,128)(2,1)S(1)} %bitcast.617), kind=kOutput, calls=%fused_computation.10 | convolution fusion | flops 6480199680 | bytes 33554432 | tf_op jit(solution)/shard_map/dot_general | solution.py:155
  515.2 10.6 fusion.106
  528.5 17.7 %fusion = f32[2048,1536]{1,0:T(8,128)S(1)} fusion(bf16[2048,2048]{1,0:T(8,128)(2,1)} %copy-done.77, bf16[2048,768]{1,0:T(8,128)(2,1)S(1)} %copy-done.49, bf16[2048,768]{1,0:T(8,128)(2,1)} %get-tuple-element.118), kind=kOutput, calls=%fused_computation.9 | convolution fusion | flops 12897484800 | bytes 27262976 | tf_op jit(solution)/shard_map/dot_general | solution.py:159
  549.0 9.7 convolution_convert_fusion
  561.5 9.7 collective-permute-done.127
  573.7 8.0 convolution_convert_fusion.3
  583.5 36.6 %collective-permute-done.128 = bf16[512,768]{1,0:T(8,128)(2,1)S(1)} collective-permute-done((bf16[512,768]{1,0:T(8,128)(2,1)}, bf16[512,768]{1,0:T(8,128)(2,1)S(1)}, u32[]{:S(2)}, u32[]{:S(2)}) %collective-permute-start.128) | collective-permute-done | bytes 786464 | tf_op jit(solution)/shard_map/ppermute | solution.py:44
  651.0 10.1 collective-permute-done.117
  662.7 12.4 %fusion.99 = (bf16[4,256,2048]{2,1,0:T(8,128)(2,1)}, f32[4,256,2048]{2,1,0:T(8,128)}) fusion(bf16[4,256,2048]{2,1,0:T(8,128)(2,1)} %bitcast.219, bf16[4,256,1536]{2,1,0:T(8,128)(2,1)} %bitcast.613, bf16[2048,1536,1]{1,0,2:T(8,128)(2,1)S(1)} %bitcast.580), kind=kOutput, calls=%fused_computation.368 | convolution fusion | flops 6448742400 | bytes 26214400 | tf_op jit(solution)/shard_map/dot_general | solution.py:163
  681.1 7.2 fusion.98
  689.5 12.4 %collective-permute-done.77 = bf16[128,2048]{1,0:T(8,128)(2,1)} collective-permute-done((bf16[128,2048]{1,0:T(8,128)(2,1)S(1)}, bf16[128,2048]{1,0:T(8,128)(2,1)}, u32[]{:S(2)}, u32[]{:S(2)}) %collective-permute-start.77) | collective-permute-done | bytes 524320 | tf_op jit(solution)/shard_map/ppermute | solution.py:39
  710.5 17.5 %collective-permute-done.76 = bf16[128,2048]{1,0:T(8,128)(2,1)S(1)} collective-permute-done((bf16[128,2048]{1,0:T(8,128)(2,1)S(1)}, bf16[128,2048]{1,0:T(8,128)(2,1)S(1)}, u32[]{:S(2)}, u32[]{:S(2)}) %collective-permute-start.76) | collective-permute-done | bytes 524320 | tf_op jit(solution)/shard_map/ppermute | solution.py:39
  759.3 8.4 dynamic_update_slice.266
  767.7 8.7 dynamic_update_slice.267
  776.5 8.5 dynamic_update_slice.268
  785.0 8.5 dynamic_update_slice.269
  793.5 8.5 dynamic_update_slice.270
  802.0 8.5 dynamic_update_slice.271
  810.6 8.5 dynamic_update_slice.272
  827.8 7.5 collective-permute-done.60
  852.3 31.0 %mixer_backward.1 = (bf16[8,256,768]{2,1,0:T(8,128)(2,1)S(1)}, f32[384,768]{1,0:T(8,128)S(1)}, f32[8,384]{1,0:T(8,128)S(1)}) custom-call(s32[1]{0:T(128)} %bitcast.place, f32[8,256,768]{2,1,0:T(8,128)} %fusion.101.pre.rim, f32[8,256,768]{2,1,0:T(8,128)} %fusion.101.pre.rim, f32[8,256,8]{2,1,0:T(8,128)S(1)} %stack.29.masks, ...), custom_call_target="tpu_custom_call" | custom-call | flops 3623878656 | bytes 18874368 | tf_op jit(solution)/shard_map/mixer_backward/pallas_call | solution.py:612
  884.0 9.5 fusion.104
  898.8 17.7 %collective-permute-done.143 = f32[8,384]{1,0:T(8,128)S(1)} collective-permute-done((f32[8,384]{1,0:T(8,128)S(1)}, f32[8,384]{1,0:T(8,128)S(1)}, u32[]{:S(2)}, u32[]{:S(2)}) %collective-permute-start.143) | collective-permute-done | bytes 12320 | tf_op jit(solution)/shard_map/ppermute | solution.py:44
  922.1 6.9 convolution_convert_fusion.2
  929.4 12.5 %copy.233 = bf16[2048,2048]{1,0:T(8,128)(2,1)} copy(bf16[2048,2048]{0,1:T(8,128)(2,1)} %bitcast.559) | data formatting | bytes 16777216 | tf_op jit(solution)/shard_map/dot_general | solution.py:159
  943.7 6.9 fusion.105
  957.6 8.6 collective-permute-done.106
  989.1 22.3 %collective-permute-done.108 = bf16[512,384]{1,0:T(8,128)(2,1)S(1)} collective-permute-done((bf16[512,384]{1,0:T(8,128)(2,1)S(1)}, bf16[512,384]{1,0:T(8,128)(2,1)S(1)}, u32[]{:S(2)}, u32[]{:S(2)}) %collective-permute-start.108) | collective-permute-done | bytes 393248 | tf_op jit(solution)/shard_map/ppermute | solution.py:44
  1028.6 9.5 collective-permute-done.110
  1116.2 7.2 fusion.100
  1143.7 8.0 fusion.1
  1164.0 7.7 fusion.13
  (865 shorter events, 508.6 us)
Async XLA Ops:
  2.8 77.9 %collective-permute-start = (f32[1,384]{1,0:T(1,128)}, f32[1,384]{1,0:T(1,128)}, u32[]{:S(2)}, u32[]{:S(2)}) collective-permute-start(f32[1,384]{1,0:T(1,128)} %pad_maximum_fusion.3), channel_id=1, source_target_pairs={{0,1},{1,0},{2,3},{3,2},{4,5},{5,4},{6,7},{7,6},{8,9},{9,8},{10,11... | collective-permute-start | bytes 4616 | tf_op jit(solution)/shard_map/ppermute | solution.py:39
  66.3 48.9 %collective-permute-start.15 = (bf16[64,1152]{1,0:T(8,128)(2,1)}, bf16[64,1152]{1,0:T(8,128)(2,1)}, u32[]{:S(2)}, u32[]{:S(2)}) collective-permute-start(bf16[64,1152]{1,0:T(8,128)(2,1)} %bitcast.550), channel_id=1, source_target_pairs={{0,1},{1,0},{2,3},{3,2},{4,5},{5,4},{6,7},{7,6},{8,9},{9,8},{10,11... | collective-permute-start | bytes 442376 | tf_op jit(solution)/shard_map/ppermute | solution.py:39
  67.1 51.2 %collective-permute-start.16 = (bf16[64,1152]{1,0:T(8,128)(2,1)}, bf16[64,1152]{1,0:T(8,128)(2,1)}, u32[]{:S(2)}, u32[]{:S(2)}) collective-permute-start(bf16[64,1152]{1,0:T(8,128)(2,1)} %bitcast.549), channel_id=1, source_target_pairs={{0,2},{1,3},{2,0},{3,1},{4,6},{5,7},{6,4},{7,5},{8,10},{9,11},{10,... | collective-permute-start | bytes 442376 | tf_op jit(solution)/shard_map/ppermute | solution.py:39
  70.7 50.7 %collective-permute-start.17 = (bf16[64,1152]{1,0:T(8,128)(2,1)}, bf16[64,1152]{1,0:T(8,128)(2,1)}, u32[]{:S(2)}, u32[]{:S(2)}) collective-permute-start(bf16[64,1152]{1,0:T(8,128)(2,1)} %bitcast.548), channel_id=1, source_target_pairs={{0,3},{1,2},{2,1},{3,0},{4,7},{5,6},{6,5},{7,4},{8,11},{9,10},{10,... | collective-permute-start | bytes 442376 | tf_op jit(solution)/shard_map/ppermute | solution.py:39
  71.4 51.7 %collective-permute-start.18 = (bf16[64,1152]{1,0:T(8,128)(2,1)}, bf16[64,1152]{1,0:T(8,128)(2,1)}, u32[]{:S(2)}, u32[]{:S(2)}) collective-permute-start(bf16[64,1152]{1,0:T(8,128)(2,1)} %bitcast.547), channel_id=1, source_target_pairs={{0,4},{1,5},{2,6},{3,7},{4,0},{5,1},{6,2},{7,3},{8,12},{9,13},{10,... | collective-permute-start | bytes 442376 | tf_op jit(solution)/shard_map/ppermute | solution.py:39
  121.5 77.0 %collective-permute-start.10 = (bf16[256,2048]{1,0:T(8,128)(2,1)S(1)}, bf16[256,2048]{1,0:T(8,128)(2,1)S(1)}, u32[]{:S(2)}, u32[]{:S(2)}) collective-permute-start(bf16[256,2048]{1,0:T(8,128)(2,1)S(1)} %get-tuple-element.116), channel_id=1, source_target_pairs={{0,1},{1,0},{2,3},{3,2},{4,5},{5,4},{6,7},{7,6},{8,9},{9,8},{10,11... | collective-permute-start | bytes 3145736 | tf_op jit(solution)/shard_map/ppermute | solution.py:39
  123.1 53.5 %collective-permute-start.7 = (bf16[256,2048]{1,0:T(8,128)(2,1)S(1)}, bf16[256,2048]{1,0:T(8,128)(2,1)S(1)}, u32[]{:S(2)}, u32[]{:S(2)}) collective-permute-start(bf16[256,2048]{1,0:T(8,128)(2,1)S(1)} %get-tuple-element.116), channel_id=1, source_target_pairs={{0,4},{1,5},{2,6},{3,7},{4,0},{5,1},{6,2},{7,3},{8,12},{9,13},{10,... | collective-permute-start | bytes 3145736 | tf_op jit(solution)/shard_map/ppermute | solution.py:39
  126.1 51.8 %collective-permute-start.6 = (bf16[256,2048]{1,0:T(8,128)(2,1)S(1)}, bf16[256,2048]{1,0:T(8,128)(2,1)S(1)}, u32[]{:S(2)}, u32[]{:S(2)}) collective-permute-start(bf16[256,2048]{1,0:T(8,128)(2,1)S(1)} %get-tuple-element.116), channel_id=1, source_target_pairs={{0,2},{1,3},{2,0},{3,1},{4,6},{5,7},{6,4},{7,5},{8,10},{9,11},{10,... | collective-permute-start | bytes 3145736 | tf_op jit(solution)/shard_map/ppermute | solution.py:39
  130.7 46.0 %collective-permute-start.22 = (bf16[512,768]{1,0:T(8,128)(2,1)S(1)}, bf16[512,768]{1,0:T(8,128)(2,1)S(1)}, u32[]{:S(2)}, u32[]{:S(2)}) collective-permute-start(bf16[512,768]{1,0:T(8,128)(2,1)S(1)} %slice.875), channel_id=1, source_target_pairs={{0,8},{1,9},{2,10},{3,11},{4,12},{5,13},{6,14},{7,15},{8,16},{9,17... | collective-permute-start | bytes 2359304 | tf_op jit(solution)/shard_map/ppermute | solution.py:44
  175.9 100.5 %collective-permute-start.48 = (bf16[64,2304]{1,0:T(8,128)(2,1)S(1)}, bf16[64,2304]{1,0:T(8,128)(2,1)S(1)}, u32[]{:S(2)}, u32[]{:S(2)}) collective-permute-start(bf16[64,2304]{1,0:T(8,128)(2,1)S(1)} %bitcast.645), channel_id=1, source_target_pairs={{0,5},{1,4},{2,7},{3,6},{4,1},{5,0},{6,3},{7,2},{8,13},{9,12},{10,... | collective-permute-start | bytes 884744 | tf_op jit(solution)/shard_map/ppermute | solution.py:39
  212.0 30.6 %collective-permute-start.24 = (bf16[512,768]{1,0:T(8,128)(2,1)S(1)}, bf16[512,768]{1,0:T(8,128)(2,1)S(1)}, u32[]{:S(2)}, u32[]{:S(2)}) collective-permute-start(bf16[512,768]{1,0:T(8,128)(2,1)S(1)} %collective-permute-done.23), channel_id=1, source_target_pairs={{0,8},{1,9},{2,10},{3,11},{4,12},{5,13},{6,14},{7,15},{8,16},{9,17... | collective-permute-start | bytes 2359304 | tf_op jit(solution)/shard_map/ppermute | solution.py:44
  212.2 65.9 %collective-permute-start.49 = (bf16[64,2304]{1,0:T(8,128)(2,1)S(1)}, bf16[64,2304]{1,0:T(8,128)(2,1)S(1)}, u32[]{:S(2)}, u32[]{:S(2)}) collective-permute-start(bf16[64,2304]{1,0:T(8,128)(2,1)S(1)} %bitcast.644), channel_id=1, source_target_pairs={{0,6},{1,7},{2,4},{3,5},{4,2},{5,3},{6,0},{7,1},{8,14},{9,15},{10,... | collective-permute-start | bytes 884744 | tf_op jit(solution)/shard_map/ppermute | solution.py:39
  212.9 29.3 %collective-permute-start.26 = (bf16[512,384]{1,0:T(8,128)(2,1)S(1)}, bf16[512,384]{1,0:T(8,128)(2,1)S(1)}, u32[]{:S(2)}, u32[]{:S(2)}) collective-permute-start(bf16[512,384]{1,0:T(8,128)(2,1)S(1)} %collective-permute-done.25), channel_id=1, source_target_pairs={{0,8},{1,9},{2,10},{3,11},{4,12},{5,13},{6,14},{7,15},{8,16},{9,17... | collective-permute-start | bytes 1179656 | tf_op jit(solution)/shard_map/ppermute | solution.py:44
  213.7 65.2 %collective-permute-start.50 = (bf16[64,2304]{1,0:T(8,128)(2,1)S(1)}, bf16[64,2304]{1,0:T(8,128)(2,1)S(1)}, u32[]{:S(2)}, u32[]{:S(2)}) collective-permute-start(bf16[64,2304]{1,0:T(8,128)(2,1)S(1)} %bitcast.643), channel_id=1, source_target_pairs={{0,7},{1,6},{2,5},{3,4},{4,3},{5,2},{6,1},{7,0},{8,15},{9,14},{10,... | collective-permute-start | bytes 884744 | tf_op jit(solution)/shard_map/ppermute | solution.py:39
  242.3 29.6 %collective-permute-start.27 = (bf16[512,384]{1,0:T(8,128)(2,1)S(1)}, bf16[512,384]{1,0:T(8,128)(2,1)S(1)}, u32[]{:S(2)}, u32[]{:S(2)}) collective-permute-start(bf16[512,384]{1,0:T(8,128)(2,1)S(1)} %collective-permute-done.26), channel_id=1, source_target_pairs={{0,8},{1,9},{2,10},{3,11},{4,12},{5,13},{6,14},{7,15},{8,16},{9,17... | collective-permute-start | bytes 1179656 | tf_op jit(solution)/shard_map/ppermute | solution.py:44
  276.4 66.6 %collective-permute-start.28 = (bf16[1024,2048]{1,0:T(8,128)(2,1)}, bf16[1024,2048]{1,0:T(8,128)(2,1)}, u32[]{:S(2)}, u32[]{:S(2)}) collective-permute-start(bf16[1024,2048]{1,0:T(8,128)(2,1)} %convolution_convert_fusion.1), channel_id=1, source_target_pairs={{0,1},{1,0},{2,3},{3,2},{4,5},{5,4},{6,7},{7,6},{8,9},{9,8},{10,11... | collective-permute-start | bytes 12582920 | tf_op jit(solution)/shard_map/ppermute | solution.py:39
  278.8 41.3 %collective-permute-start.64 = (bf16[256,2048]{1,0:T(8,128)(2,1)}, bf16[256,2048]{1,0:T(8,128)(2,1)}, u32[]{:S(2)}, u32[]{:S(2)}) collective-permute-start(bf16[256,2048]{1,0:T(8,128)(2,1)} %bitcast.78), channel_id=1, source_target_pairs={{0,2},{1,3},{2,0},{3,1},{4,6},{5,7},{6,4},{7,5},{8,10},{9,11},{10,... | collective-permute-start | bytes 3145736 | tf_op jit(solution)/shard_map/ppermute | solution.py:39
  282.4 55.9 %collective-permute-start.51 = (bf16[512,1536]{1,0:T(8,128)(2,1)}, bf16[512,1536]{1,0:T(8,128)(2,1)}, u32[]{:S(2)}, u32[]{:S(2)}) collective-permute-start(bf16[512,1536]{1,0:T(8,128)(2,1)} %slice.912), channel_id=1, source_target_pairs={{0,8},{1,9},{2,10},{3,11},{4,12},{5,13},{6,14},{7,15},{8,16},{9,17... | collective-permute-start | bytes 4718600 | tf_op jit(solution)/shard_map/ppermute | solution.py:44
  285.1 50.4 %collective-permute-start.68 = (bf16[256,2048]{1,0:T(8,128)(2,1)}, bf16[256,2048]{1,0:T(8,128)(2,1)}, u32[]{:S(2)}, u32[]{:S(2)}) collective-permute-start(bf16[256,2048]{1,0:T(8,128)(2,1)} %bitcast.78), channel_id=1, source_target_pairs={{0,1},{1,0},{2,3},{3,2},{4,5},{5,4},{6,7},{7,6},{8,9},{9,8},{10,11... | collective-permute-start | bytes 3145736 | tf_op jit(solution)/shard_map/ppermute | solution.py:39
  341.9 39.1 %collective-permute-start.52 = (bf16[512,1536]{1,0:T(8,128)(2,1)}, bf16[512,1536]{1,0:T(8,128)(2,1)S(1)}, u32[]{:S(2)}, u32[]{:S(2)}) collective-permute-start(bf16[512,1536]{1,0:T(8,128)(2,1)} %collective-permute-done.51), channel_id=1, source_target_pairs={{0,8},{1,9},{2,10},{3,11},{4,12},{5,13},{6,14},{7,15},{8,16},{9,17... | collective-permute-start | bytes 4718600 | tf_op jit(solution)/shard_map/ppermute | solution.py:44
  347.8 35.8 %collective-permute-start.32 = (bf16[128,2048]{1,0:T(8,128)(2,1)S(1)}, bf16[128,2048]{1,0:T(8,128)(2,1)S(1)}, u32[]{:S(2)}, u32[]{:S(2)}) collective-permute-start(bf16[128,2048]{1,0:T(8,128)(2,1)S(1)} %get-tuple-element.142), channel_id=1, source_target_pairs={{0,4},{1,5},{2,6},{3,7},{4,0},{5,1},{6,2},{7,3},{8,12},{9,13},{10,... | collective-permute-start | bytes 1572872 | tf_op jit(solution)/shard_map/ppermute | solution.py:39
  348.5 35.1 %collective-permute-start.30 = (bf16[128,2048]{1,0:T(8,128)(2,1)S(1)}, bf16[128,2048]{1,0:T(8,128)(2,1)S(1)}, u32[]{:S(2)}, u32[]{:S(2)}) collective-permute-start(bf16[128,2048]{1,0:T(8,128)(2,1)S(1)} %get-tuple-element.143), channel_id=1, source_target_pairs={{0,2},{1,3},{2,0},{3,1},{4,6},{5,7},{6,4},{7,5},{8,10},{9,11},{10,... | collective-permute-start | bytes 1572872 | tf_op jit(solution)/shard_map/ppermute | solution.py:39
  402.3 54.1 %collective-permute-start.53 = (bf16[512,1536]{1,0:T(8,128)(2,1)S(1)}, bf16[512,1536]{1,0:T(8,128)(2,1)S(1)}, u32[]{:S(2)}, u32[]{:S(2)}) collective-permute-start(bf16[512,1536]{1,0:T(8,128)(2,1)S(1)} %collective-permute-done.52), channel_id=1, source_target_pairs={{0,8},{1,9},{2,10},{3,11},{4,12},{5,13},{6,14},{7,15},{8,16},{9,17... | collective-permute-start | bytes 4718600 | tf_op jit(solution)/shard_map/ppermute | solution.py:44
  402.3 54.0 %collective-permute-start.55 = (bf16[512,768]{1,0:T(8,128)(2,1)S(1)}, bf16[512,768]{1,0:T(8,128)(2,1)S(1)}, u32[]{:S(2)}, u32[]{:S(2)}) collective-permute-start(bf16[512,768]{1,0:T(8,128)(2,1)S(1)} %collective-permute-done.54), channel_id=1, source_target_pairs={{0,8},{1,9},{2,10},{3,11},{4,12},{5,13},{6,14},{7,15},{8,16},{9,17... | collective-permute-start | bytes 2359304 | tf_op jit(solution)/shard_map/ppermute | solution.py:44
  407.7 49.0 %collective-permute-start.36 = (bf16[256,2048]{1,0:T(8,128)(2,1)S(1)}, bf16[256,2048]{1,0:T(8,128)(2,1)S(1)}, u32[]{:S(2)}, u32[]{:S(2)}) collective-permute-start(bf16[256,2048]{1,0:T(8,128)(2,1)S(1)} %get-tuple-element.112), channel_id=1, source_target_pairs={{0,4},{1,5},{2,6},{3,7},{4,0},{5,1},{6,2},{7,3},{8,12},{9,13},{10,... | collective-permute-start | bytes 3145736 | tf_op jit(solution)/shard_map/ppermute | solution.py:39
  409.2 49.0 %collective-permute-start.35 = (bf16[256,2048]{1,0:T(8,128)(2,1)S(1)}, bf16[256,2048]{1,0:T(8,128)(2,1)S(1)}, u32[]{:S(2)}, u32[]{:S(2)}) collective-permute-start(bf16[256,2048]{1,0:T(8,128)(2,1)S(1)} %get-tuple-element.112), channel_id=1, source_target_pairs={{0,2},{1,3},{2,0},{3,1},{4,6},{5,7},{6,4},{7,5},{8,10},{9,11},{10,... | collective-permute-start | bytes 3145736 | tf_op jit(solution)/shard_map/ppermute | solution.py:39
  561.5 60.3 %collective-permute-start.116 = (bf16[512,1536]{1,0:T(8,128)(2,1)}, bf16[512,1536]{1,0:T(8,128)(2,1)S(1)}, u32[]{:S(2)}, u32[]{:S(2)}) collective-permute-start(bf16[512,1536]{1,0:T(8,128)(2,1)} %fusion.32), channel_id=1, source_target_pairs={{0,8},{1,9},{2,10},{3,11},{4,12},{5,13},{6,14},{7,15},{8,16},{9,17... | collective-permute-start | bytes 4718600 | tf_op jit(solution)/shard_map/ppermute | solution.py:44
  561.5 101.2 %collective-permute-start.73 = (bf16[1024,2048]{1,0:T(8,128)(2,1)}, bf16[1024,2048]{1,0:T(8,128)(2,1)}, u32[]{:S(2)}, u32[]{:S(2)}) collective-permute-start(bf16[1024,2048]{1,0:T(8,128)(2,1)} %convolution_convert_fusion), channel_id=1, source_target_pairs={{0,1},{1,0},{2,3},{3,2},{4,5},{5,4},{6,7},{7,6},{8,9},{9,8},{10,11... | collective-permute-start | bytes 12582920 | tf_op jit(solution)/shard_map/ppermute | solution.py:39
  573.7 46.4 %collective-permute-start.128 = (bf16[512,768]{1,0:T(8,128)(2,1)}, bf16[512,768]{1,0:T(8,128)(2,1)S(1)}, u32[]{:S(2)}, u32[]{:S(2)}) collective-permute-start(bf16[512,768]{1,0:T(8,128)(2,1)} %fusion.35), channel_id=1, source_target_pairs={{0,8},{1,9},{2,10},{3,11},{4,12},{5,13},{6,14},{7,15},{8,16},{9,17... | collective-permute-start | bytes 2359304 | tf_op jit(solution)/shard_map/ppermute | solution.py:44
  581.7 98.8 %collective-permute-start.57 = (bf16[1024,2048]{1,0:T(8,128)(2,1)}, bf16[1024,2048]{1,0:T(8,128)(2,1)}, u32[]{:S(2)}, u32[]{:S(2)}) collective-permute-start(bf16[1024,2048]{1,0:T(8,128)(2,1)} %convolution_convert_fusion.3), channel_id=1, source_target_pairs={{0,1},{1,0},{2,3},{3,2},{4,5},{5,4},{6,7},{7,6},{8,9},{9,8},{10,11... | collective-permute-start | bytes 12582920 | tf_op jit(solution)/shard_map/ppermute | solution.py:39
  622.5 38.6 %collective-permute-start.117 = (bf16[512,1536]{1,0:T(8,128)(2,1)S(1)}, bf16[512,1536]{1,0:T(8,128)(2,1)S(1)}, u32[]{:S(2)}, u32[]{:S(2)}) collective-permute-start(bf16[512,1536]{1,0:T(8,128)(2,1)S(1)} %fusion.7), channel_id=1, source_target_pairs={{0,8},{1,9},{2,10},{3,11},{4,12},{5,13},{6,14},{7,15},{8,16},{9,17... | collective-permute-start | bytes 4718600 | tf_op jit(solution)/shard_map/ppermute | solution.py:44
  662.7 43.4 %collective-permute-start.118 = (bf16[512,1536]{1,0:T(8,128)(2,1)}, bf16[512,1536]{1,0:T(8,128)(2,1)}, u32[]{:S(2)}, u32[]{:S(2)}) collective-permute-start(bf16[512,1536]{1,0:T(8,128)(2,1)} %fusion.6), channel_id=1, source_target_pairs={{0,8},{1,9},{2,10},{3,11},{4,12},{5,13},{6,14},{7,15},{8,16},{9,17... | collective-permute-start | bytes 4718600 | tf_op jit(solution)/shard_map/ppermute | solution.py:44
  677.0 32.8 %collective-permute-start.74 = (bf16[128,2048]{1,0:T(8,128)(2,1)S(1)}, bf16[128,2048]{1,0:T(8,128)(2,1)S(1)}, u32[]{:S(2)}, u32[]{:S(2)}) collective-permute-start(bf16[128,2048]{1,0:T(8,128)(2,1)S(1)} %get-tuple-element.132), channel_id=1, source_target_pairs={{0,4},{1,5},{2,6},{3,7},{4,0},{5,1},{6,2},{7,3},{8,12},{9,13},{10,... | collective-permute-start | bytes 1572872 | tf_op jit(solution)/shard_map/ppermute | solution.py:39
  677.6 32.9 %collective-permute-start.79 = (bf16[128,2048]{1,0:T(8,128)(2,1)S(1)}, bf16[128,2048]{1,0:T(8,128)(2,1)S(1)}, u32[]{:S(2)}, u32[]{:S(2)}) collective-permute-start(bf16[128,2048]{1,0:T(8,128)(2,1)S(1)} %get-tuple-element.133), channel_id=1, source_target_pairs={{0,2},{1,3},{2,0},{3,1},{4,6},{5,7},{6,4},{7,5},{8,10},{9,11},{10,... | collective-permute-start | bytes 1572872 | tf_op jit(solution)/shard_map/ppermute | solution.py:39
  701.9 34.8 %collective-permute-start.61 = (bf16[128,2048]{1,0:T(8,128)(2,1)S(1)}, bf16[128,2048]{1,0:T(8,128)(2,1)S(1)}, u32[]{:S(2)}, u32[]{:S(2)}) collective-permute-start(bf16[128,2048]{1,0:T(8,128)(2,1)S(1)} %get-tuple-element.136), channel_id=1, source_target_pairs={{0,4},{1,5},{2,6},{3,7},{4,0},{5,1},{6,2},{7,3},{8,12},{9,13},{10,... | collective-permute-start | bytes 1572872 | tf_op jit(solution)/shard_map/ppermute | solution.py:39
  710.5 29.6 %collective-permute-start.125 = (bf16[64,1536]{1,0:T(8,128)(2,1)S(1)}, bf16[64,1536]{1,0:T(8,128)(2,1)S(1)}, u32[]{:S(2)}, u32[]{:S(2)}) collective-permute-start(bf16[64,1536]{1,0:T(8,128)(2,1)S(1)} %get-tuple-element.154), channel_id=1, source_target_pairs={{0,7},{1,6},{2,5},{3,4},{4,3},{5,2},{6,1},{7,0},{8,15},{9,14},{10,... | collective-permute-start | bytes 589832 | tf_op jit(solution)/shard_map/ppermute | solution.py:39
  737.9 82.5 %collective-permute-start.81 = (bf16[256,2048]{1,0:T(8,128)(2,1)}, bf16[256,2048]{1,0:T(8,128)(2,1)}, u32[]{:S(2)}, u32[]{:S(2)}) collective-permute-start(bf16[256,2048]{1,0:T(8,128)(2,1)} %get-tuple-element.110), channel_id=1, source_target_pairs={{0,4},{1,5},{2,6},{3,7},{4,0},{5,1},{6,2},{7,3},{8,12},{9,13},{10,... | collective-permute-start | bytes 3145736 | tf_op jit(solution)/shard_map/ppermute | solution.py:39
  744.4 79.4 %collective-permute-start.80 = (bf16[256,2048]{1,0:T(8,128)(2,1)}, bf16[256,2048]{1,0:T(8,128)(2,1)}, u32[]{:S(2)}, u32[]{:S(2)}) collective-permute-start(bf16[256,2048]{1,0:T(8,128)(2,1)} %get-tuple-element.110), channel_id=1, source_target_pairs={{0,2},{1,3},{2,0},{3,1},{4,6},{5,7},{6,4},{7,5},{8,10},{9,11},{10,... | collective-permute-start | bytes 3145736 | tf_op jit(solution)/shard_map/ppermute | solution.py:39
  752.4 72.6 %collective-permute-start.63 = (bf16[128,2048]{1,0:T(8,128)(2,1)}, bf16[128,2048]{1,0:T(8,128)(2,1)}, u32[]{:S(2)}, u32[]{:S(2)}) collective-permute-start(bf16[128,2048]{1,0:T(8,128)(2,1)} %get-tuple-element.137), channel_id=1, source_target_pairs={{0,2},{1,3},{2,0},{3,1},{4,6},{5,7},{6,4},{7,5},{8,10},{9,11},{10,... | collective-permute-start | bytes 1572872 | tf_op jit(solution)/shard_map/ppermute | solution.py:39
  755.5 71.2 %collective-permute-start.58 = (bf16[128,2048]{1,0:T(8,128)(2,1)}, bf16[128,2048]{1,0:T(8,128)(2,1)}, u32[]{:S(2)}, u32[]{:S(2)}) collective-permute-start(bf16[128,2048]{1,0:T(8,128)(2,1)} %get-tuple-element.139), channel_id=1, source_target_pairs={{0,4},{1,5},{2,6},{3,7},{4,0},{5,1},{6,2},{7,3},{8,12},{9,13},{10,... | collective-permute-start | bytes 1572872 | tf_op jit(solution)/shard_map/ppermute | solution.py:39
  757.6 70.2 %collective-permute-start.62 = (bf16[128,2048]{1,0:T(8,128)(2,1)}, bf16[128,2048]{1,0:T(8,128)(2,1)}, u32[]{:S(2)}, u32[]{:S(2)}) collective-permute-start(bf16[128,2048]{1,0:T(8,128)(2,1)} %get-tuple-element.124), channel_id=1, source_target_pairs={{0,2},{1,3},{2,0},{3,1},{4,6},{5,7},{6,4},{7,5},{8,10},{9,11},{10,... | collective-permute-start | bytes 1572872 | tf_op jit(solution)/shard_map/ppermute | solution.py:39
  883.5 74.1 %collective-permute-start.136 = (bf16[192,768]{1,0:T(8,128)(2,1)S(1)}, bf16[192,768]{1,0:T(8,128)(2,1)S(1)}, u32[]{:S(2)}, u32[]{:S(2)}) collective-permute-start(bf16[192,768]{1,0:T(8,128)(2,1)S(1)} %select_convert_fusion), channel_id=1, source_target_pairs={{0,8},{1,9},{2,10},{3,11},{4,12},{5,13},{6,14},{7,15},{8,16},{9,17... | collective-permute-start | bytes 884744 | tf_op jit(solution)/shard_map/ppermute | solution.py:44
  894.6 78.0 %collective-permute-start.96 = (bf16[512,768]{1,0:T(8,128)(2,1)}, bf16[512,768]{1,0:T(8,128)(2,1)}, u32[]{:S(2)}, u32[]{:S(2)}) collective-permute-start(bf16[512,768]{1,0:T(8,128)(2,1)} %fusion.56), channel_id=1, source_target_pairs={{0,8},{1,9},{2,10},{3,11},{4,12},{5,13},{6,14},{7,15},{8,16},{9,17... | collective-permute-start | bytes 2359304 | tf_op jit(solution)/shard_map/ppermute | solution.py:44
  929.0 186.1 %collective-permute-start.89 = (bf16[1024,2048]{1,0:T(8,128)(2,1)}, bf16[1024,2048]{1,0:T(8,128)(2,1)}, u32[]{:S(2)}, u32[]{:S(2)}) collective-permute-start(bf16[1024,2048]{1,0:T(8,128)(2,1)} %convolution_convert_fusion.2), channel_id=1, source_target_pairs={{0,1},{1,0},{2,3},{3,2},{4,5},{5,4},{6,7},{7,6},{8,9},{9,8},{10,11... | collective-permute-start | bytes 12582920 | tf_op jit(solution)/shard_map/ppermute | solution.py:39
  975.2 43.2 %collective-permute-start.97 = (bf16[512,768]{1,0:T(8,128)(2,1)}, bf16[512,768]{1,0:T(8,128)(2,1)}, u32[]{:S(2)}, u32[]{:S(2)}) collective-permute-start(bf16[512,768]{1,0:T(8,128)(2,1)} %fusion.39), channel_id=1, source_target_pairs={{0,8},{1,9},{2,10},{3,11},{4,12},{5,13},{6,14},{7,15},{8,16},{9,17... | collective-permute-start | bytes 2359304 | tf_op jit(solution)/shard_map/ppermute | solution.py:44
  1021.4 44.2 %collective-permute-start.140 = (bf16[2,192,768]{2,1,0:T(8,128)(2,1)S(1)}, bf16[2,192,768]{2,1,0:T(8,128)(2,1)S(1)}, u32[]{:S(2)}, u32[]{:S(2)}) collective-permute-start(bf16[2,192,768]{2,1,0:T(8,128)(2,1)S(1)} %maximum_select_fusion.1), channel_id=1, source_target_pairs={{0,2},{1,3},{2,0},{3,1},{4,6},{5,7},{6,4},{7,5},{8,10},{9,11},{10,... | collective-permute-start | bytes 1769480 | tf_op jit(solution)/shard_map/ppermute | solution.py:39
  1023.4 42.8 %collective-permute-start.98 = (bf16[512,768]{1,0:T(8,128)(2,1)}, bf16[512,768]{1,0:T(8,128)(2,1)}, u32[]{:S(2)}, u32[]{:S(2)}) collective-permute-start(bf16[512,768]{1,0:T(8,128)(2,1)} %fusion.38), channel_id=1, source_target_pairs={{0,8},{1,9},{2,10},{3,11},{4,12},{5,13},{6,14},{7,15},{8,16},{9,17... | collective-permute-start | bytes 2359304 | tf_op jit(solution)/shard_map/ppermute | solution.py:44
  1081.4 50.4 %collective-permute-start.141 = (bf16[4,192,768]{2,1,0:T(8,128)(2,1)}, bf16[4,192,768]{2,1,0:T(8,128)(2,1)}, u32[]{:S(2)}, u32[]{:S(2)}) collective-permute-start(bf16[4,192,768]{2,1,0:T(8,128)(2,1)} %maximum_select_fusion), channel_id=1, source_target_pairs={{0,4},{1,5},{2,6},{3,7},{4,0},{5,1},{6,2},{7,3},{8,12},{9,13},{10,... | collective-permute-start | bytes 3538952 | tf_op jit(solution)/shard_map/ppermute | solution.py:39
  (205 other events, 2614.5 us)

commit v2 on v1

--- a/solution.py
+++ b/solution.py
@@ -18,6 +18,7 @@
 GROUP = 8
 AXES = ("batch", "seq")
 PAD = 192
+SMALL = 176
 WIDE = 2 * PAD
 SIZES = [BLK] * NBIG + [BLK - 1] * (NBLK - NBIG)
 BEGINS = [sum(SIZES[:i]) for i in range(NBLK)]
@@ -39,9 +40,10 @@
     return lax.ppermute(values, AXES, [(i, i ^ bit) for i in range(device_count())])
 
 
-def onward(values):
+def onward(values, turns):
     count = device_count()
-    return lax.ppermute(values, AXES, [(i, (i + GROUP) % count) for i in range(count)])
+    pairs = [(i, (i + turns * GROUP) % count) for i in range(count)]
+    return lax.ppermute(values, AXES, pairs)
 
 
 def low(values):
@@ -64,58 +66,76 @@
     return lax.optimization_barrier((values,) + others)[0]
 
 
-def exchange(pieces, place):
-    out = jnp.zeros_like(pieces)
-    for bit in range(GROUP):
-        part = pick(pieces, place ^ bit)
-        out = put(out, swap(part, bit) if bit else part, place ^ bit)
+def ring_groups():
+    count = device_count()
+    return [list(range(i, count, GROUP)) for i in range(GROUP)]
+
+
+def ring_gather(block):
+    return lax.all_gather(block, AXES, axis=0, tiled=True, axis_index_groups=ring_groups())
+
+
+def ring_reduce(values):
+    return lax.psum_scatter(
+        values, AXES, scatter_dimension=0, tiled=True, axis_index_groups=ring_groups()
+    )
+
+
+def ring_stack(block, turn, groups, wait_for=()):
+    arrived = [onward(block, step) for step in range(1, groups)]
+    arrived, _ = lax.optimization_barrier((arrived, wait_for))
+    out = jnp.broadcast_to(block, (groups,) + block.shape)
+    for step in range(1, groups):
+        out = put(out, arrived[step - 1], (turn + groups - step) % groups)
     return out
 
 
-def ring_gather(block, turn, groups):
-    out = jnp.broadcast_to(block, (groups,) + block.shape)
-    arrivals = []
+def ring_sum(values, turn, groups):
+    chunks = values.reshape((groups, -1) + values.shape[1:])
+    total = wide(pick(chunks, turn))
     for step in range(1, groups):
-        block = onward(block)
-        arrivals.append(block)
-        out = put(out, block, (turn + groups - step) % groups)
-    return out.reshape((-1,) + block.shape[1:]), arrivals
-
-
-def ring_reduce(values, turn, groups):
-    values = values.reshape((groups, -1) + values.shape[1:])
-    total = pick(values, (turn + groups - 1) % groups)
-    for step in range(1, groups):
-        total = wide(onward(low(total))) + pick(values, (turn + 2 * groups - 1 - step) % groups)
-    return total
-
-
-def tiny_gather(values, place):
-    for bit in (1, 2, 4):
-        other = swap(values, bit)
-        values = jnp.where(
-            (place & bit) != 0,
-            jnp.concatenate([other, values], axis=0),
-            jnp.concatenate([values, other], axis=0),
-        )
-    return values
-
-
-def group_gather(own):
+        total = total + wide(onward(pick(chunks, (turn + step) % groups), step))
+    return low(total)
+
+
+def all_swapped(parts):
+    return [parts[0]] + [swap(parts[bit], bit) for bit in range(1, GROUP)]
+
+
+def first_swaps(own):
+    return swap(own, 4), swap(own, 2)
+
+
+def group_parts(own, swapped=None):
     half = own.shape[0] // 2
-    across, along = swap(own, 4), swap(own, 2)
+    across, along = swapped or first_swaps(own)
     first, second = swap(across[:half], 2), swap(along[half:], 4)
     mine = [own, along, across, first, second]
-    return jnp.concatenate(mine + [swap(part, 1) for part in mine], axis=0)
-
-
-def group_reduce(near, far):
+    return mine + [swap(part, 1) for part in mine]
+
+
+def group_gather(own):
+    return jnp.concatenate(group_parts(own), axis=0)
+
+
+def pair_total(near, far):
     near = near.reshape(4, -1, near.shape[-1])
-    total = near + wide(swap(low(far), 1)).reshape(near.shape)
-    half = near.shape[1] // 2
-    first, second = swap(low(total[3, :half]), 4), swap(low(total[3, half:]), 2)
-    across = swap(low(total[2, :half]), 4)
-    along = swap(low(total[1, half:]), 2)
+    return near + wide(swap(low(far), 1)).reshape(near.shape)
+
+
+def send_totals(total):
+    half = total.shape[1] // 2
+    return (
+        swap(low(total[3, :half]), 4),
+        swap(low(total[3, half:]), 2),
+        swap(low(total[2, :half]), 4),
+        swap(low(total[1, half:]), 2),
+    )
+
+
+def join_totals(total, arrived):
+    first, second, across, along = arrived
+    half = total.shape[1] // 2
     across_rest = swap(low(total[2, half:] + wide(second)), 4)
     along_rest = swap(low(total[1, :half] + wide(first)), 2)
     return (
@@ -123,6 +143,10 @@
         + wide(jnp.concatenate([across, across_rest], axis=0))
         + wide(jnp.concatenate([along_rest, along], axis=0))
     )
+
+
+def group_total(total):
+    return join_totals(total, send_totals(total))
 
 
 def to_windows(values):
@@ -134,10 +158,139 @@
     return jnp.concatenate(parts, axis=-1).reshape(values.shape[:-1] + (GROUP, WIDE))
 
 
-def from_windows(values):
-    flat = values.reshape(values.shape[:-2] + (GROUP * WIDE,))
-    parts = [flat[..., i * PAD : i * PAD + size] for i, size in enumerate(SIZES)]
-    return jnp.concatenate(parts, axis=-1)
+def norm_kernel(values, gain, out):
+    rows = wide(values[...])
+    out[...] = low(rows * rms_scale(rows) * gain[...])
+
+
+def norm_rows(values, gain, steps):
+    rows, width = values.shape
+    return pl.pallas_call(
+        norm_kernel,
+        grid=(rows // steps,),
+        in_specs=[
+            pl.BlockSpec((steps, width), lambda i: (i, 0)),
+            pl.BlockSpec((1, width), lambda i: (0, 0)),
+        ],
+        out_specs=pl.BlockSpec((steps, width), lambda i: (i, 0)),
+        out_shape=jax.ShapeDtypeStruct((rows, width), BF16),
+        compiler_params=pltpu.CompilerParams(vmem_limit_bytes=48 * 1024 * 1024),
+        cost_estimate=pl.CostEstimate(flops=1, bytes_accessed=1, transcendentals=0),
+        name="norm_rows",
+    )(values, gain)
+
+
+SCALAR = pl.BlockSpec(memory_space=pltpu.SMEM)
+BUFFER = pl.BlockSpec(memory_space=pltpu.VMEM)
+
+
+def simple_call(kernel, name, place, arrays, outs, scratch=()):
+    moved = sum(a.size * a.dtype.itemsize for a in arrays)
+    return pl.pallas_call(
+        kernel,
+        in_specs=[SCALAR] + [BUFFER] * len(arrays),
+        out_specs=[BUFFER] * len(outs),
+        out_shape=[jax.ShapeDtypeStruct(shape, dtype) for shape, dtype in outs],
+        scratch_shapes=list(scratch),
+        compiler_params=pltpu.CompilerParams(vmem_limit_bytes=48 * 1024 * 1024),
+        cost_estimate=pl.CostEstimate(flops=moved, bytes_accessed=2 * moved, transcendentals=0),
+        name=name,
+    )(place, *arrays)
+
+
+def split_mixer_kernel(place, branch, gating, output, tiny, *rest):
+    outs, held = rest[:GROUP], rest[GROUP]
+    rows = branch.shape[0]
+    held[...] = jnp.zeros_like(held)
+    for slot, ref in enumerate((branch, gating, output)):
+        values = wide(ref[...])
+        for i in range(NBLK):
+            begin = slot * WIDE + (i % 2) * PAD
+            held[i // 2, :, begin : begin + SIZES[i]] = values[
+                :, BEGINS[i] : BEGINS[i] + SIZES[i]
+            ]
+    for bit in range(GROUP):
+        outs[bit][:rows] = low(held[place[0] ^ bit])
+        outs[bit][rows:] = tiny[...]
+
+
+def split_hidden_kernel(place, gate, linear, output, *outs):
+    part = gate.shape[1] // GROUP
+    for bit in range(GROUP):
+        columns = pl.ds(pl.multiple_of((place[0] ^ bit) * part, 128), part)
+        for slot, ref in enumerate((gate, linear, output)):
+            outs[bit][:, slot * part : (slot + 1) * part] = ref[:, columns]
+
+
+def collect_kernel(place, *refs):
+    parts, (first, second) = refs[:GROUP], refs[GROUP:]
+    cut = first.shape[2]
+    for bit in range(GROUP):
+        first[place[0] ^ bit] = parts[bit][:, :cut]
+        second[place[0] ^ bit] = parts[bit][:, cut:]
+
+
+def collect_mixer_kernel(place, *refs):
+    parts, (columns, tiny) = refs[:GROUP], refs[GROUP:]
+    rows = columns.shape[1]
+    for bit in range(GROUP):
+        columns[place[0] ^ bit] = parts[bit][:rows]
+        tiny[place[0] ^ bit] = wide(parts[bit][rows:])[:1, : tiny.shape[2]]
+
+
+def deal_kernel(place, *refs):
+    values, outs = refs[:-GROUP], refs[-GROUP:]
+    for bit in range(GROUP):
+        begin = 0
+        for ref in values:
+            outs[bit][:, begin : begin + ref.shape[2]] = ref[place[0] ^ bit]
+            begin += ref.shape[2]
+
+
+def hidden_owner_kernel(place, gate, linear, gain, *refs):
+    parts, outs = refs[:GROUP], refs[GROUP:]
+    part = gate.shape[1] // GROUP
+    total = jnp.zeros((gate.shape[0], 1), F32)
+    for bit in range(GROUP):
+        columns = pl.ds(pl.multiple_of((place[0] ^ bit) * part, 128), part)
+        d_gate, d_linear = wide(parts[bit][:, :part]), wide(parts[bit][:, part : 2 * part])
+        outs[0][:, columns] = d_gate
+        outs[1][:, columns] = d_linear
+        outs[2][:, columns] = wide(parts[bit][:, 2 * part : 3 * part])
+        terms = d_gate * wide(gate[:, columns]) + d_linear * wide(linear[:, columns])
+        total = total + jnp.sum(terms, axis=1, keepdims=True)
+    outs[3][...] = total / gain[...]
+
+
+def mixer_owner_kernel(place, branch, gating, gain, *refs):
+    boths, lasts = refs[:GROUP], refs[GROUP : 2 * GROUP]
+    outs, held = refs[2 * GROUP : -1], refs[-1]
+    for bit in range(GROUP):
+        held[place[0] ^ bit, :, : 2 * WIDE] = wide(boths[bit][...])
+        held[place[0] ^ bit, :, 2 * WIDE :] = wide(lasts[bit][:, -WIDE:])
+    for slot in range(3):
+        for i in range(NBLK):
+            begin = slot * WIDE + (i % 2) * PAD
+            outs[slot][:, BEGINS[i] : BEGINS[i] + SIZES[i]] = held[
+                i // 2, :, begin : begin + SIZES[i]
+            ]
+    terms = outs[0][...] * wide(branch[...]) + outs[1][...] * wide(gating[...])
+    outs[3][...] = jnp.sum(terms, axis=1, keepdims=True) / gain[...]
+
+
+def gates_owner_kernel(place, *refs):
+    parts, (blocks, small), held = refs[:GROUP], refs[GROUP : GROUP + 2], refs[-1]
+    for part, bit in zip(parts, ORDER):
+        device = place[0] ^ bit
+        for gate in range(2):
+            for block in range(2):
+                begin = gate * WIDE + block * PAD
+                blocks[gate, 2 * device + block] = wide(part[:BLK, begin : begin + BLK])
+        ending = wide(part[SMALL:PAD])[:8]
+        held[device] = ending[:, :WIDE] + ending[:, WIDE:]
+    for i in range(NBLK):
+        begin = (i % 2) * PAD
+        small[:, BEGINS[i] : BEGINS[i] + SIZES[i]] = held[i // 2, :, begin : begin + SIZES[i]]
 
 
 def rms_scale(values):
@@ -163,10 +316,11 @@
     return lax.dot_general(left, right, (((1,), (1,)), ((), ())), preferred_element_type=F32)
 
 
-def reduce_product(left, right):
+def pair_product(left, right, first=None):
     half = left.shape[0] // 2
     far = low(contract_cols(left[half:], right))
-    return group_reduce(contract_cols(left[:half], right), far)
+    near = left[:half] if first is None else after(left[:half], first)
+    return pair_total(contract_cols(near, right), far)
 
 
 def sigmoid(values):
@@ -194,30 +348,54 @@
     return -values * series
 
 
-def gate_values(conv, masks, weight, bias, rate):
+def repeated(values, width):
+    return jnp.concatenate([values] * (width // 128), axis=1)
+
+
+def gate_values(conv, fresh, weight, bias, rate):
     pre = product(low(conv), weight) + bias
     width = conv.shape[1]
     recur, enter = sigmoid(pre[:, :width]), sigmoid(pre[:, width:])
     log_decay = rate * recur
     decay = jnp.exp(log_decay)
     raw_scale = jnp.sqrt(minus_expm1(2.0 * log_decay))
-    fresh = masks[:, 3:4] > 0.5
     carry = jnp.where(fresh, 0.0, decay)
     scale = jnp.where(fresh, 1.0, raw_scale)
-    return recur, enter, decay, raw_scale, fresh, carry, scale
+    return recur, enter, decay, raw_scale, carry, scale
+
+
+def same_masks(numbers, steps, width):
+    own = numbers[8 : 8 + steps]
+    masks = [
+        repeated(jnp.where(numbers[8 - k : 8 - k + steps] == own, 1.0, 0.0), width)
+        for k in range(1, KW)
+    ]
+    return masks, masks[0] < 0.5
 
 
 def convolve(padded, masks, params, steps):
     conv = params[6:7] + params[2:3] * padded[8 : 8 + steps]
     for offset in range(1, KW):
         conv = conv + params[2 + offset : 3 + offset] * (
-            padded[8 - offset : 8 - offset + steps] * masks[:, offset - 1 : offset]
+            padded[8 - offset : 8 - offset + steps] * masks[offset - 1]
         )
     return conv
 
 
 def forward_kernel(
-    place, pre, masks, weight, bias, params, state_out, mixed_out, padded, mult, partial, chain
+    place,
+    pre,
+    segment,
+    weight,
+    bias,
+    params,
+    state_out,
+    mixed_out,
+    padded,
+    mult,
+    partial,
+    chain,
+    numbers,
 ):
     steps, width = padded.shape[0] - 8, padded.shape[1]
     chunk = steps // 8
@@ -225,16 +403,20 @@
     @pl.when(pl.program_id(1) == 0)
     def _():
         padded[0:8] = jnp.zeros((8, width), F32)
+        numbers[0:8] = jnp.full((8, 128), -1.0, F32)
         chain[...] = jnp.zeros_like(chain)
 
     @pl.when(pl.program_id(1) > 0)
     def _():
         padded[0:8] = padded[steps : steps + 8]
+        numbers[0:8] = numbers[steps : steps + 8]
 
     padded[8 : 8 + steps] = pre[0, :, :width]
-    conv = convolve(padded, masks[0], params, steps)
-    recur, enter, decay, raw_scale, fresh, carry, scale = gate_values(
-        conv, masks[0], weight[...], bias[...], params[7:8]
+    numbers[8 : 8 + steps] = segment[0]
+    masks, fresh = same_masks(numbers, steps, width)
+    conv = convolve(padded, masks, params, steps)
+    recur, enter, decay, raw_scale, carry, scale = gate_values(
+        conv, fresh, weight[...], bias[...], params[7:8]
     )
     for lane in range(width // 128):
         lanes = slice(lane * 128, lane * 128 + 128)
@@ -265,7 +447,8 @@
     place,
     pre,
     rim,
-    masks,
+    segment,
+    segment_rim,
     state,
     state_rim,
     d_mixed,
@@ -273,18 +456,21 @@
     bias,
     params,
     d_both,
-    grad_gate,
-    grad_small,
+    packed,
     padded,
     mult,
     partial,
     adjoint_all,
     chain,
     later,
+    numbers,
+    grad_gate,
+    grad_small,
 ):
     steps, width = padded.shape[0] - 8, padded.shape[1]
     chunk = steps // 8
     last = pl.program_id(1) == 0
+    first = pl.program_id(1) == pl.num_programs(1) - 1
 
     @pl.when(last & (pl.program_id(0) == 0))
     def _():
@@ -300,12 +486,14 @@
     def _():
         later[:, steps : steps + 8] = later[:, 0:8]
 
-    mask = masks[0]
     padded[0:8] = rim[0]
     padded[8 : 8 + steps] = pre[0, :, :width]
-    conv = convolve(padded, mask, params, steps)
-    recur, enter, decay, raw_scale, fresh, carry, scale = gate_values(
-        conv, mask, weight[...], bias[...], params[7:8]
+    numbers[0:8] = jnp.where(first, -1.0, segment_rim[0])
+    numbers[8 : 8 + steps] = segment[0]
+    masks, fresh = same_masks(numbers, steps, width)
+    conv = convolve(padded, masks, params, steps)
+    recur, enter, decay, raw_scale, carry, scale = gate_values(
+        conv, fresh, weight[...], bias[...], params[7:8]
     )
     value, slope = gelu_both(pre[0, :, width:])
     d_out = d_mixed[0]
@@ -357,7 +545,7 @@
     ]
     d_branch = d_conv * params[2:3]
     for offset in range(1, KW):
-        masked = d_conv * mask[:, offset - 1 : offset]
+        masked = d_conv * masks[offset - 1]
         sums.append(
             jnp.sum(masked * padded[8 - offset : 8 - offset + steps], axis=0, keepdims=True)
         )
@@ -369,6 +557,16 @@
         grad_small[row : row + 1] += value_sum
     d_both[0, :, :width] = low(d_branch)
 
+    @pl.when(first & (pl.program_id(0) == pl.num_programs(0) - 1))
+    def _():
+        side = lax.broadcasted_iota(jnp.int32, (PAD, 2 * width), 1) % width
+        blocks = jnp.where(side < PAD, grad_gate[0:PAD], grad_gate[PAD : 2 * PAD])
+        rest = grad_small[...] - wide(low(grad_small[...]))
+        packed[...] = low(blocks)
+        packed[SMALL:PAD] = low(
+            jnp.concatenate([jnp.concatenate([grad_small[...], rest], axis=1), blocks[-8:]], axis=0)
+        )
+
 
 def mixer_calls(rows, shards, steps, channels):
     blocks = rows * shards
@@ -393,7 +591,7 @@
                 pl.BlockSpec(
                     (1, steps, 2 * channels), lambda r, s, p: (position(r, s, p[0]), 0, 0)
                 ),
-                pl.BlockSpec((1, steps, 8), lambda r, s, p: (r * shards + s, 0, 0)),
+                pl.BlockSpec((1, steps, 128), lambda r, s, p: (r * shards + s, 0, 0)),
                 whole(channels, 2 * channels),
                 whole(1, 2 * channels),
                 whole(8, channels),
@@ -407,6 +605,7 @@
                 pltpu.VMEM((lanes, steps, 128), F32),
                 pltpu.VMEM((lanes, steps, 128), F32),
                 pltpu.VMEM((8, channels), F32),
+                pltpu.VMEM((steps + 8, 128), F32),
             ],
         ),
         out_shape=[
@@ -414,11 +613,7 @@
             jax.ShapeDtypeStruct((blocks, steps, channels), BF16),
         ],
         compiler_params=params,
-        cost_estimate=pl.CostEstimate(
-            flops=blocks * steps * channels * channels * 4,
-            bytes_accessed=blocks * steps * channels * 14,
-            transcendentals=blocks * steps * channels * 6,
-        ),
+        cost_estimate=pl.CostEstimate(flops=1, bytes_accessed=1, transcendentals=0),
         name="mixer_forward",
     )
 
@@ -441,7 +636,10 @@
                     (1, 8, channels),
                     lambda r, s, p: (position(r, before(s), p[0]), steps // 8 - 1, 0),
                 ),
-                pl.BlockSpec((1, steps, 8), lambda r, s, p: (r * shards + turned(s), 0, 0)),
+                pl.BlockSpec((1, steps, 128), lambda r, s, p: (r * shards + turned(s), 0, 0)),
+                pl.BlockSpec(
+                    (1, 8, 128), lambda r, s, p: (r * shards + before(s), steps // 8 - 1, 0)
+                ),
                 pl.BlockSpec((1, steps, channels), lambda r, s, p: (r * shards + turned(s), 0, 0)),
                 pl.BlockSpec(
                     (1, 8, channels),
@@ -458,8 +656,7 @@
                 pl.BlockSpec(
                     (1, steps, 2 * channels), lambda r, s, p: (position(r, turned(s), p[0]), 0, 0)
                 ),
-                whole(channels, 2 * channels),
-                whole(8, channels),
+                whole(PAD, 2 * channels),
             ],
             scratch_shapes=[
                 pltpu.VMEM((steps + 8, channels), F32),
@@ -468,12 +665,14 @@
                 pltpu.VMEM((steps, channels), F32),
                 pltpu.VMEM((8, channels), F32),
                 pltpu.VMEM((KW - 1, steps + 8, channels), F32),
+                pltpu.VMEM((steps + 8, 128), F32),
+                pltpu.VMEM((channels, 2 * channels), F32),
+                pltpu.VMEM((8, channels), F32),
             ],
         ),
         out_shape=[
             jax.ShapeDtypeStruct((blocks, steps, 2 * channels), BF16),
-            jax.ShapeDtypeStruct((channels, 2 * channels), F32),
-            jax.ShapeDtypeStruct((8, channels), F32),
+            jax.ShapeDtypeStruct((PAD, 2 * channels), BF16),
         ],
         compiler_params=params,
         cost_estimate=pl.CostEstimate(
@@ -515,57 +714,63 @@
     hidden_part = hidden_width // GROUP
     tokens = GROUP * steps
 
+    where = place.astype(jnp.int32).reshape(1)
     tiny = jnp.concatenate(
-        [wide(mixer_gain)[None], wide(hidden_gain)[None], wide(segment_ids)], axis=1
-    )
-    tiny = tiny_gather(tiny, place)
-    gains, _ = ring_gather(tiny[:, : 2 * own_rows], turn, groups)
-    mixer_scale = gains[:, :own_rows].reshape(1, model_width)
-    hidden_scale = gains[:, own_rows:].reshape(1, model_width)
-    segments = tiny[:, 2 * own_rows :].reshape(rows, shards * steps)
-    flags = []
-    for offset in range(1, KW):
-        flags.append(
-            jnp.pad(
-                wide(segments[:, offset:] == segments[:, :-offset]), ((0, 0), (offset, 0))
-            )
-        )
-    flags.append(1.0 - flags[0])
-    flags = flags + [jnp.zeros_like(flags[0])] * 4
-    masks = jnp.stack(flags, axis=-1).reshape(GROUP, steps, 8)
-
-    mixer_pieces = jnp.concatenate(
-        [to_windows(branch_weight), to_windows(gating_weight), to_windows(output_weight)], axis=-1
-    )
-    mixer_pieces = exchange(jnp.swapaxes(mixer_pieces, 0, 1), place).reshape(-1, 3 * WIDE)
-    hidden_pieces = jnp.concatenate(
+        [mixer_gain[None], hidden_gain[None], low(segment_ids)], axis=1
+    )
+    tiny_width = tiny.shape[1]
+    mixer_parts = simple_call(
+        split_mixer_kernel,
+        "split_mixer",
+        where,
+        (
+            branch_weight,
+            gating_weight,
+            output_weight,
+            jnp.pad(tiny, ((0, 15), (0, 3 * WIDE - tiny_width))),
+        ),
+        [((own_rows + 16, 3 * WIDE), BF16)] * GROUP,
+        [pltpu.VMEM((GROUP, own_rows, 3 * WIDE), F32)],
+    )
+    mixer_rows, tiny = simple_call(
+        collect_mixer_kernel,
+        "collect_mixer",
+        where,
+        all_swapped(mixer_parts),
         [
-            hidden_gate.reshape(own_rows, GROUP, hidden_part),
-            hidden_linear.reshape(own_rows, GROUP, hidden_part),
-            hidden_output.reshape(own_rows, GROUP, hidden_part),
+            ((GROUP, own_rows, 3 * WIDE), BF16),
+            ((GROUP, 1, tiny_width), F32),
         ],
-        axis=-1,
-    )
-    hidden_pieces = exchange(
-        after(jnp.swapaxes(hidden_pieces, 0, 1), mixer_pieces), place
-    ).reshape(-1, 3 * hidden_part)
-    both_weight, arrivals = ring_gather(mixer_pieces[:, : 2 * WIDE], turn, groups)
-    out_weight, arrivals = ring_gather(
-        after(mixer_pieces[:, 2 * WIDE :], arrivals[-2]), turn, groups
-    )
-    pair_weight, arrivals = ring_gather(
-        after(hidden_pieces[:, : 2 * hidden_part], arrivals[-2]), turn, groups
-    )
-    last_weight, arrivals = ring_gather(
-        after(hidden_pieces[:, 2 * hidden_part :], arrivals[-2]), turn, groups
-    )
+    )
+    tiny = tiny.reshape(GROUP, tiny_width)
+    mixer_weight = ring_gather(mixer_rows.reshape(-1, 3 * WIDE))
+    both_weight, out_weight = mixer_weight[:, : 2 * WIDE], mixer_weight[:, 2 * WIDE :]
+    gains = ring_stack(tiny[:, : 2 * own_rows], turn, groups)
+    mixer_scale = gains[..., :own_rows].reshape(1, model_width)
+    hidden_scale = gains[..., own_rows:].reshape(1, model_width)
+    segments = jnp.broadcast_to(tiny[:, 2 * own_rows :, None], (GROUP, steps, 128))
 
     inputs = wide(stream_in).reshape(steps, model_width)
     inputs_scale = rms_scale(inputs)
-    normed = group_gather(low(inputs * inputs_scale * mixer_scale))
+    parts = group_parts(stream_in.reshape(steps, model_width))
+    normed = norm_rows(jnp.concatenate(parts, axis=0), mixer_scale, steps)
     upstream = wide(out_grad).reshape(steps, model_width)
-    upstream_all = group_gather(after(out_grad.reshape(steps, model_width), normed))
-    pre = product(normed, both_weight).reshape(GROUP, steps, 2 * WIDE)
+    hidden_parts = simple_call(
+        split_hidden_kernel,
+        "split_hidden",
+        where,
+        (hidden_gate, hidden_linear, hidden_output),
+        [((own_rows, 3 * hidden_part), BF16)] * GROUP,
+    )
+    pair_rows, last_rows = simple_call(
+        collect_kernel,
+        "collect_hidden",
+        where,
+        all_swapped(lax.optimization_barrier((hidden_parts, parts[3:5]))[0]),
+        [((GROUP, own_rows, 2 * hidden_part), BF16), ((GROUP, own_rows, hidden_part), BF16)],
+    )
+    pair_weight = ring_gather(pair_rows.reshape(-1, 2 * hidden_part))
+    pre = product(after(normed, pair_rows), both_weight).reshape(GROUP, steps, 2 * WIDE)
 
     rate = -8.0 * jax.nn.softplus(-decay_param)
     params = jnp.concatenate(
@@ -585,75 +790,90 @@
         axis=0,
     )
     mixer_forward, mixer_backward = mixer_calls(rows, shards, steps, WIDE)
-    where = place.astype(jnp.int32).reshape(1)
-    state, mixed = mixer_forward(where, pre, masks, gate_weight, bias, params)
+    state, mixed = mixer_forward(where, pre, segments, gate_weight, bias, params)
     mixed = mixed.reshape(tokens, WIDE)
-    middle = inputs + reduce_product(mixed, out_weight)
+    last_weight = ring_gather(after(last_rows, mixed).reshape(-1, hidden_part))
+    middle = inputs + group_total(pair_product(mixed, out_weight))
 
     middle_scale = rms_scale(middle)
-    normed_mid = group_gather(low(middle * middle_scale * hidden_scale))
+    own = low(middle * middle_scale * hidden_scale)
+    parts = group_parts(own, lax.optimization_barrier((first_swaps(own), pair_weight))[0])
+    own = out_grad.reshape(steps, model_width)
+    swapped = first_swaps(lax.optimization_barrier((own, parts[3:5]))[0])
+    normed_mid = jnp.concatenate(parts, axis=0)
+    upstream_all = jnp.concatenate(group_parts(own, swapped), axis=0)
     pair = product(normed_mid, pair_weight)
     gate_pre, linear_pre = pair[:, :hidden_part], pair[:, hidden_part:]
     value, slope = gelu_both(gate_pre)
     hidden = low(value * linear_pre)
-    d_hidden = product(upstream_all, last_weight)
+    grad_last_low = low(contract_rows(upstream_all, hidden))
+    grad_last = ring_reduce(grad_last_low)
+    d_hidden = product(after(upstream_all, grad_last_low), last_weight)
     d_pair = jnp.concatenate(
         [low(d_hidden * linear_pre * slope), low(d_hidden * value)], axis=1
     )
+    grad_pair_low = low(contract_rows(normed_mid, d_pair))
+    grad_pair = ring_reduce(grad_pair_low)
+    d_normed_mid = pair_product(after(d_pair, grad_pair_low), pair_weight)
+    hidden_out = pair_product(after(hidden, d_normed_mid), last_weight)
+    result = low(middle + group_total(hidden_out))
     d_middle = upstream + norm_back(
-        middle, middle_scale, hidden_scale, reduce_product(d_pair, pair_weight)
-    )
-    result = low(middle + reduce_product(hidden, last_weight))
-    grad_pair = ring_reduce(contract_rows(normed_mid, d_pair), turn, groups)
-    grad_last = ring_reduce(contract_rows(upstream_all, hidden), turn, groups)
-
-    middle_low = group_gather(low(d_middle))
+        middle, middle_scale, hidden_scale, group_total(d_normed_mid)
+    )
+
+    def to_owner(name, *grads):
+        grads = [values.reshape(GROUP, own_rows, -1) for values in grads]
+        width = sum(values.shape[2] for values in grads)
+        parts = simple_call(
+            deal_kernel, name, where, grads, [((own_rows, width), BF16)] * GROUP
+        )
+        return all_swapped(parts)
+
+    middle_low = group_gather(after(low(d_middle), grad_last, hidden_out))
     d_mixed = product(middle_low, out_weight).reshape(GROUP, steps, WIDE)
-    d_both, grad_gate, grad_small = mixer_backward(
-        where, pre, pre, masks, state, state, d_mixed, gate_weight, bias, params
+    grad_out_low = low(contract_rows(middle_low, mixed))
+    grad_out = ring_reduce(grad_out_low)
+    d_mixed = after(d_mixed, grad_out_low, grad_pair)
+    d_both, packed = mixer_backward(
+        where, pre, pre, segments, segments, state, state, d_mixed, gate_weight, bias, params
     )
     d_both = d_both.reshape(tokens, 2 * WIDE)
-    stream_grad = low(
-        d_middle
-        + norm_back(inputs, inputs_scale, mixer_scale, reduce_product(d_both, both_weight))
-    )
-    grad_out = ring_reduce(contract_rows(middle_low, mixed), turn, groups)
-    grad_both = ring_reduce(contract_rows(normed, d_both), turn, groups)
-
-    def to_owner(grads):
-        return wide(exchange(low(grads).reshape(GROUP, own_rows, -1), place))
-
-    def hidden_rows(grads):
-        return jnp.swapaxes(grads, 0, 1).reshape(own_rows, hidden_width)
-
-    def mixer_rows(grads):
-        return from_windows(jnp.swapaxes(grads, 0, 1))
-
-    grad_pair, grad_last = to_owner(grad_pair), to_owner(grad_last)
-    grad_both, grad_out = to_owner(grad_both), to_owner(grad_out)
-    grad_hgate = hidden_rows(grad_pair[..., :hidden_part])
-    grad_hlinear = hidden_rows(grad_pair[..., hidden_part:])
-    grad_houtput = hidden_rows(grad_last)
-    grad_branch = mixer_rows(grad_both[..., :WIDE])
-    grad_gating = mixer_rows(grad_both[..., WIDE:])
-    grad_output = mixer_rows(grad_out)
-    grad_hgain = jnp.sum(
-        wide(hidden_gate) * grad_hgate + wide(hidden_linear) * grad_hlinear, axis=1
-    ) / wide(hidden_gain)
-    grad_mgain = jnp.sum(
-        wide(branch_weight) * grad_branch + wide(gating_weight) * grad_gating, axis=1
-    ) / wide(mixer_gain)
-
-    upper = lax.broadcasted_iota(jnp.int32, (PAD, 2 * WIDE), 1) % WIDE < PAD
-    packed = low(jnp.where(upper, grad_gate[:PAD], grad_gate[PAD:]))
-    packed, _ = ring_gather(packed, turn, groups)
-    packed = low(jnp.sum(wide(packed.reshape(groups, PAD, 2 * WIDE)), axis=0))
-    packed = wide(tiny_gather(packed[None], place))
-    packed = packed.reshape(GROUP, PAD, 2, 2, PAD).transpose(2, 0, 3, 1, 4)
-    grad_gblocks = packed.reshape(2, NBLK, PAD, PAD)[:, :, :BLK, :BLK]
-    small, _ = ring_gather(grad_small, turn, groups)
-    small = jnp.sum(small.reshape(groups, 8, WIDE), axis=0)
-    small = from_windows(jnp.swapaxes(tiny_gather(small[None], place), 0, 1))
+    grad_both_low = low(contract_rows(normed, after(d_both, grad_out)))
+    grad_both = ring_reduce(grad_both_low)
+    early_parts = to_owner("deal_early", grad_pair, grad_last, grad_out)
+    d_normed = pair_product(after(d_both, grad_both_low), both_weight)
+    d_normed = group_total(d_normed)
+    stream_grad = low(d_middle + norm_back(inputs, inputs_scale, mixer_scale, d_normed))
+
+    grad_hgate, grad_hlinear, grad_houtput, grad_hgain = simple_call(
+        hidden_owner_kernel,
+        "hidden_owner",
+        where,
+        (hidden_gate, hidden_linear, wide(hidden_gain)[:, None])
+        + tuple(early_parts),
+        [((own_rows, hidden_width), F32)] * 3 + [((own_rows, 1), F32)],
+    )
+    grad_branch, grad_gating, grad_output, grad_mgain = simple_call(
+        mixer_owner_kernel,
+        "mixer_owner",
+        where,
+        (branch_weight, gating_weight, wide(mixer_gain)[:, None])
+        + tuple(to_owner("deal_both", grad_both) + early_parts),
+        [((own_rows, R), F32)] * 3 + [((own_rows, 1), F32)],
+        [pltpu.VMEM((GROUP, own_rows, 3 * WIDE), F32)],
+    )
+
+    packed = ring_stack(ring_sum(packed, turn, groups), turn, groups).reshape(PAD, 2 * WIDE)
+    across, along = swap(packed, 4), swap(packed, 2)
+    near = [packed, along, across, swap(across, 2)]
+    grad_gblocks, small = simple_call(
+        gates_owner_kernel,
+        "gates_owner",
+        where,
+        near + [swap(part, 1) for part in near],
+        [((2, NBLK, BLK, BLK), F32), ((8, R), F32)],
+        [pltpu.VMEM((GROUP, 8, WIDE), F32)],
+    )
     grad_decay = 8.0 * jax.nn.sigmoid(-decay_param) * small[7]
 
     shape = (rows_here, steps, model_width)
@@ -666,8 +886,8 @@
         grad_hgate,
         grad_hlinear,
         grad_houtput,
-        grad_mgain,
-        grad_hgain,
+        grad_mgain.reshape(own_rows),
+        grad_hgain.reshape(own_rows),
         grad_gblocks,
         small[:2],
         small[2:6],

time: 1190 us -> 740 us (0.62)
  local copies, waits for them, and re-layouts: 331 us -> 82.3 us
  waiting for transfers between devices: 455 us -> 254 us
  other arithmetic: 81.8 us -> 44.8 us
  Pallas kernels: 51.4 us -> 72.8 us
  between operations: 4.29 us -> 16.2 us
    ppermute x33 -> x9, waiting for transfers between devices: 284 us -> 29.7 us  [onward(): return lax.ppermute(values, AXES, pairs)]
    dynamic_update_slice x68 -> x6, local copies, waits for them, and re-layouts: 130 us -> 0.04 us  [put(): return lax.dynamic_update_index_in_dim(values, part, index, 0)]
    pad x60 -> x15, local copies, waits for them, and re-layouts: 29.4 us -> 0.1 us  [to_windows(): jnp.pad(values[..., begin:begin + size], leading + [(0, PAD - size)])]
    ppermute x115 -> x99, waiting for transfers between devices: 171 us -> 200 us  [swap(): lax.ppermute(values, AXES, [(i, i ^ bit) for i in range(device_count())])]
    dot_general x2 -> x0, local copies, waits for them, and re-layouts: 24.8 us -> none  [contract_rows(): lax.dot_general(left, right, (((0,), (0,)), ((), ())), preferred_element_...]
    all_gather x0 -> x3, waiting for transfers between devices: none -> 24.8 us  [ring_gather(): lax.all_gather(block, AXES, axis=0, tiled=True, axis_index_groups=ring_gr...]
    pallas_call x2 -> x12, Pallas kernels: 51.4 us -> 72.8 us  [the longest x1 29.3 us: local(): mixer_backward(where, pre, pre, segments, segments, state, state, d_mixed...]
    another operation x9 -> x0, local copies, waits for them, and re-layouts: 20.7 us -> none  [the longest x6 12.6 us: local(): masks = jnp.stack(flags, axis=-1).reshape(GROUP, steps, 8)]
  transfers between devices with their start and end apart: 148 -> 115, of which waited for: 54 -> 47; matrix products, arithmetic and copies ran while one was open for 42% -> 34% of each run, Pallas kernels for 2% -> 10%
where the time goes in v2:
time: 740 us; the launch traced here: 731 us
  waiting for transfers between devices  254 us (34%)
  matrix products  162 us (22%)
  starting transfers between devices  98.7 us (13%)
  local copies, waits for them, and re-layouts  82.3 us (11%)
  Pallas kernels  72.8 us (10%)
  other arithmetic  44.8 us (6%)
  between operations  16.2 us (2%)
    ppermute x99, waiting for transfers between devices, swap(): lax.ppermute(values, AXES, [(i, i ^ bit) for i in range(device_count())])  200 us
    ppermute x99, starting transfers between devices, swap(): lax.ppermute(values, AXES, [(i, i ^ bit) for i in range(device_count())])  87.2 us
    unnamed x220, local copies, waits for them, and re-layouts  65.3 us
    dot_general x4, matrix products, product(): return jnp.dot(left, right, preferred_element_type=F32)  58.3 us
    dot_general x8, matrix products, contract_cols(): lax.dot_general(left, right, (((1,), (1,)), ((), ())), preferred_element_...  57.5 us
    dot_general x4, matrix products, contract_rows(): lax.dot_general(left, right, (((0,), (0,)), ((), ())), preferred_element_...  46.1 us
    ppermute x9, waiting for transfers between devices, onward(): return lax.ppermute(values, AXES, pairs)  29.7 us
    pallas_call x1, Pallas kernels, local(): mixer_backward(where, pre, pre, segments, segments, state, state, d_mixed...  29.3 us
  transfers between devices with their start and end apart: 115, of which 47 were waited for; matrix products, arithmetic and copies ran while one was open for 34% of the time, Pallas kernels for 10%

profile of v2, /device:TPU:0, one launch (start us, length us, event | category | flops | bytes accessed | tf_op | source)
XLA Modules:
  0.0 731.1 jit_solution(16342271143958057698)
XLA Ops:
  25.9 5.7 collective-permute-done.14.refs_6_
  31.6 3.9 collective-permute-done.15.refs_7_
  53.2 9.1 %collective-permute-done.1 = bf16[256,2048]{1,0:T(8,128)(2,1)} collective-permute-done((bf16[256,2048]{1,0:T(8,128)(2,1)}, bf16[256,2048]{1,0:T(8,128)(2,1)}, u32[]{:S(2)}, u32[]{:S(2)}) %collective-permute-start.1) | collective-permute-done | bytes 1048608 | tf_op jit(solution)/shard_map/ppermute | solution.py:40
  67.9 8.8 %collective-permute-done.2 = bf16[128,2048]{1,0:T(8,128)(2,1)S(1)} collective-permute-done((bf16[128,2048]{1,0:T(8,128)(2,1)S(1)}, bf16[128,2048]{1,0:T(8,128)(2,1)S(1)}, u32[]{:S(2)}, u32[]{:S(2)}) %collective-permute-start.2) | collective-permute-done | bytes 524320 | tf_op jit(solution)/shard_map/ppermute | solution.py:40
  91.0 4.1 collective-permute-done.21.refs_3_
  102.5 3.9 collective-permute-done.24.refs_6_
  106.4 5.6 collective-permute-done.25.refs_7_
  117.8 10.3 %norm_rows.1 = bf16[2048,2048]{1,0:T(8,128)(2,1)} custom-call(bf16[2048,2048]{1,0:T(8,128)(2,1)} %constant_dynamic-update-slice_fusion.values, f32[1,2048]{1,0:T(1,128)S(1)} %reshape.527.gain), custom_call_target="tpu_custom_call" | custom-call | flops 1 | bytes 1 | tf_op jit(solution)/shard_map/norm_rows/pallas_call | solution.py:168
  128.1 11.7 %fusion.8 = f32[2048,768]{1,0:T(8,128)} fusion(bf16[2048,2048]{1,0:T(8,128)(2,1)} %norm_rows.1, bf16[2048,1152]{1,0:T(8,128)(2,1)} %all-gather.4.cloned.1.call-done), kind=kOutput, calls=%fused_computation.31 | convolution fusion | flops 6442450944 | bytes 17825792 | tf_op jit(solution)/shard_map/dot_general | solution.py:308
  140.1 20.3 %mixer_forward.1 = (f32[8,256,384]{2,1,0:T(8,128)}, bf16[8,256,384]{2,1,0:T(8,128)(2,1)S(1)}) custom-call(s32[1]{0:T(128)} %bitcast.place, f32[8,256,768]{2,1,0:T(8,128)} %bitcast.271, f32[8,256,128]{2,1,0:T(8,128)S(1)} %broadcast_in_dim.71.segment.segment_rim, bf16[384,768]{1,0:T(8,128)(2,1)S(1)} %maximum_maximum_fusion.weight, f32[1,768]{1,0:T(1,128)S(1)} %bitcast.266, ...), custom_call_target="tpu_custom_call" | custom-call | flops 1 | bytes 1 | tf_op jit(solution)/shard_map/mixer_forward/pallas_call | solution.py:793
  163.6 6.8 collective-permute-done.26
  177.0 10.7 %collective-permute-done.28 = bf16[128,2048]{1,0:T(8,128)(2,1)S(1)} collective-permute-done((bf16[128,2048]{1,0:T(8,128)(2,1)S(1)}, bf16[128,2048]{1,0:T(8,128)(2,1)S(1)}, u32[]{:S(2)}, u32[]{:S(2)}) %collective-permute-start.28) | collective-permute-done | bytes 524320 | tf_op jit(solution)/shard_map/ppermute | solution.py:40
  192.3 8.0 %collective-permute-done.27 = bf16[128,2048]{1,0:T(8,128)(2,1)S(1)} collective-permute-done((bf16[128,2048]{1,0:T(8,128)(2,1)S(1)}, bf16[128,2048]{1,0:T(8,128)(2,1)S(1)}, u32[]{:S(2)}, u32[]{:S(2)}) %collective-permute-start.27) | collective-permute-done | bytes 524320 | tf_op jit(solution)/shard_map/ppermute | solution.py:40
  200.4 10.4 %collective-permute-done.29 = bf16[128,2048]{1,0:T(8,128)(2,1)S(1)} collective-permute-done((bf16[128,2048]{1,0:T(8,128)(2,1)}, bf16[128,2048]{1,0:T(8,128)(2,1)S(1)}, u32[]{:S(2)}, u32[]{:S(2)}) %collective-permute-start.29) | collective-permute-done | bytes 524320 | tf_op jit(solution)/shard_map/ppermute | solution.py:40
  218.0 24.8 %all-gather.6.cloned.1.call-done = bf16[2048,1536]{1,0:T(8,128)(2,1)} async-done(((bf16[512,1536]{1,0:T(8,128)(2,1)}), bf16[2048,1536]{1,0:T(8,128)(2,1)}) %all-gather.6.cloned.1.call-update) | async-done | bytes 6291472 | tf_op jit(solution)/shard_map/all_gather | solution.py:75
  272.1 17.8 %fusion.86 = f32[2048,1536]{0,1:T(8,128)S(1)} fusion(bf16[2048,2048]{1,0:T(8,128)(2,1)} %constant_dynamic-update-slice_fusion.10, bf16[2048,1536]{1,0:T(8,128)(2,1)} %all-gather.6.cloned.1.call-done), kind=kOutput, calls=%fused_computation.210 | convolution fusion | flops 12884901888 | bytes 27262976 | tf_op jit(solution)/shard_map/dot_general | solution.py:308
  301.3 4.8 collective-permute-done.44
  314.1 10.5 %convolution_convert_fusion.6 = bf16[2048,768]{1,0:T(8,128)(2,1)} fusion(bf16[2048,2048]{1,0:T(8,128)(2,1)} %constant_dynamic-update-slice_fusion.20, bf16[2048,768]{0,1:T(8,128)(2,1)S(1)} %multiply_convert_fusion.2), kind=kOutput, calls=%fused_computation.16 | convolution fusion | flops 6444023808 | bytes 14680064 | tf_op jit(solution)/shard_map/dot_general | solution.py:312
  324.6 18.6 %multiply_convert_fusion.1 = (bf16[2048,768]{0,1:T(8,128)(2,1)S(1)}, bf16[2048,768]{0,1:T(8,128)(2,1)}) fusion(f32[2048,1536]{0,1:T(8,128)} %copy-done.47, bf16[2048,2048]{1,0:T(8,128)(2,1)} %constant_dynamic-update-slice_fusion.20, bf16[2048,768]{1,0:T(8,128)(2,1)} %all-gather.8.cloned.1.call-done), kind=kOutput, calls=%fused_computation.7 | convolution fusion | flops 6477053952 | bytes 30408704 | tf_op jit(solution)/shard_map/dot_general | solution.py:308
  344.9 18.5 %convolution_convert_fusion = bf16[2048,1536]{1,0:T(8,128)(2,1)} fusion(bf16[2048,2048]{1,0:T(8,128)(2,1)} %constant_dynamic-update-slice_fusion.10, bf16[2048,768]{0,1:T(8,128)(2,1)} %get-tuple-element.218, bf16[2048,768]{0,1:T(8,128)(2,1)S(1)} %get-tuple-element.217), kind=kOutput, calls=%fused_computation.4 | convolution fusion | flops 12900630528 | bytes 20971520 | tf_op jit(solution)/shard_map/dot_general | solution.py:312
  363.4 4.0 pad_maximum_fusion
  367.3 13.4 %convolution_convert_fusion.1 = bf16[1024,2048]{1,0:T(8,128)(2,1)} fusion(bf16[2048,1536]{1,0:T(8,128)(2,1)} %all-gather.6.cloned.1.call-done, bf16[2048,1536]{0,1:T(8,128)(2,1)S(1)} %pad_maximum_fusion), kind=kOutput, calls=%fused_computation.11 | convolution fusion | flops 6444548096 | bytes 13631488 | tf_op jit(solution)/shard_map/dot_general | solution.py:316
  381.3 7.0 collective-permute-done.51
  388.4 12.0 %convert_add_fusion.3 = f32[1024,2048]{1,0:T(8,128)S(1)} fusion(bf16[1024,2048]{1,0:T(8,128)(2,1)} %collective-permute-done.51, bf16[2048,1536]{1,0:T(8,128)(2,1)} %all-gather.6.cloned.1.call-done, bf16[2048,1536]{0,1:T(8,128)(2,1)} %copy-done.50), kind=kOutput, calls=%fused_computation.3 | convolution fusion | flops 6446645248 | bytes 22020096 | tf_op jit(solution)/shard_map/dot_general | solution.py:316
  400.4 5.0 convolution_convert_fusion.4
  410.7 10.7 %collective-permute-done.60 = bf16[128,2048]{1,0:T(8,128)(2,1)S(1)} collective-permute-done((bf16[128,2048]{1,0:T(8,128)(2,1)S(1)}, bf16[128,2048]{1,0:T(8,128)(2,1)S(1)}, u32[]{:S(2)}, u32[]{:S(2)}) %collective-permute-start.60) | collective-permute-done | bytes 524320 | tf_op jit(solution)/shard_map/ppermute | solution.py:40
  425.4 7.4 %collective-permute-done.59 = bf16[128,2048]{1,0:T(8,128)(2,1)S(1)} collective-permute-done((bf16[128,2048]{1,0:T(8,128)(2,1)S(1)}, bf16[128,2048]{1,0:T(8,128)(2,1)S(1)}, u32[]{:S(2)}, u32[]{:S(2)}) %collective-permute-start.59) | collective-permute-done | bytes 524320 | tf_op jit(solution)/shard_map/ppermute | solution.py:40
  432.8 10.4 %collective-permute-done.61 = bf16[128,2048]{1,0:T(8,128)(2,1)S(1)} collective-permute-done((bf16[128,2048]{1,0:T(8,128)(2,1)S(1)}, bf16[128,2048]{1,0:T(8,128)(2,1)S(1)}, u32[]{:S(2)}, u32[]{:S(2)}) %collective-permute-start.61) | collective-permute-done | bytes 524320 | tf_op jit(solution)/shard_map/ppermute | solution.py:40
  446.1 7.4 %convert_add_fusion.2 = f32[1024,2048]{1,0:T(8,128)} fusion(bf16[1024,2048]{1,0:T(8,128)(2,1)} %collective-permute-done.52, bf16[2048,768]{1,0:T(8,128)(2,1)S(1)} %copy-done.87, bf16[2048,768]{0,1:T(8,128)(2,1)S(1)} %copy-done.63), kind=kOutput, calls=%fused_computation.2 | convolution fusion | flops 3225419776 | bytes 17301504 | tf_op jit(solution)/shard_map/dot_general | solution.py:316
  456.5 21.6 %collective-permute-done.66 = bf16[256,2048]{1,0:T(8,128)(2,1)S(1)} collective-permute-done((bf16[256,2048]{1,0:T(8,128)(2,1)}, bf16[256,2048]{1,0:T(8,128)(2,1)S(1)}, u32[]{:S(2)}, u32[]{:S(2)}) %collective-permute-start.66) | collective-permute-done | bytes 1048608 | tf_op jit(solution)/shard_map/ppermute | solution.py:40
  483.1 7.5 %collective-permute-done.67 = bf16[128,2048]{1,0:T(8,128)(2,1)S(1)} collective-permute-done((bf16[128,2048]{1,0:T(8,128)(2,1)S(1)}, bf16[128,2048]{1,0:T(8,128)(2,1)S(1)}, u32[]{:S(2)}, u32[]{:S(2)}) %collective-permute-start.67) | collective-permute-done | bytes 524320 | tf_op jit(solution)/shard_map/ppermute | solution.py:40
  496.9 5.8 convolution_convert_fusion.7
  502.8 10.3 %fusion.42 = f32[2048,384]{1,0:T(8,128)} fusion(bf16[2048,2048]{1,0:T(8,128)(2,1)} %copy-done.78, bf16[2048,1152]{1,0:T(8,128)(2,1)} %all-gather.4.cloned.1.call-done), kind=kOutput, calls=%fused_computation.69 | convolution fusion | flops 3221225472 | bytes 13107200 | tf_op jit(solution)/shard_map/dot_general | solution.py:308
  513.1 29.3 %mixer_backward.1 = (bf16[8,256,768]{2,1,0:T(8,128)(2,1)S(1)}, bf16[192,768]{1,0:T(8,128)(2,1)S(1)}) custom-call(s32[1]{0:T(128)} %bitcast.place, f32[8,256,768]{2,1,0:T(8,128)} %bitcast.272, f32[8,256,768]{2,1,0:T(8,128)} %bitcast.273, f32[8,256,128]{2,1,0:T(8,128)S(1)} %copy-done.3, f32[8,256,128]{2,1,0:T(8,128)S(1)} %copy-done.3, ...), custom_call_target="tpu_custom_call" | custom-call | flops 3623878656 | bytes 18874368 | tf_op jit(solution)/shard_map/mixer_backward/pallas_call | solution.py:837
  544.0 11.4 %convolution_convert_fusion.5 = bf16[2048,768]{1,0:T(8,128)(2,1)} fusion(bf16[2048,2048]{1,0:T(8,128)(2,1)} %norm_rows.1, bf16[2048,768]{1,0:T(8,128)(2,1)} %bitcast.268), kind=kOutput, calls=%fused_computation.15 | convolution fusion | flops 6444023808 | bytes 14680064 | tf_op jit(solution)/shard_map/dot_general | solution.py:312
  555.4 7.8 %convolution_convert_fusion.3 = bf16[1024,2048]{1,0:T(8,128)(2,1)} fusion(bf16[2048,1152]{1,0:T(8,128)(2,1)} %all-gather.4.cloned.1.call-done, bf16[2048,768]{1,0:T(8,128)(2,1)} %bitcast.269), kind=kOutput, calls=%fused_computation.13 | convolution fusion | flops 3223322624 | bytes 8912896 | tf_op jit(solution)/shard_map/dot_general | solution.py:316
  563.2 4.0 convert.29
  570.9 8.4 %collective-permute-done.95 = bf16[48,768]{1,0:T(8,128)(2,1)S(1)} collective-permute-done((bf16[48,768]{1,0:T(8,128)(2,1)S(1)}, bf16[48,768]{1,0:T(8,128)(2,1)S(1)}, u32[]{:S(2)}, u32[]{:S(2)}) %collective-permute-start.95) | collective-permute-done | bytes 73760 | tf_op jit(solution)/shard_map/ppermute | solution.py:46
  579.3 4.4 collective-permute-done.96
  594.4 4.8 collective-permute-done.100
  600.2 8.2 %collective-permute-done.99 = bf16[48,768]{1,0:T(8,128)(2,1)S(1)} collective-permute-done((bf16[48,768]{1,0:T(8,128)(2,1)S(1)}, bf16[48,768]{1,0:T(8,128)(2,1)S(1)}, u32[]{:S(2)}, u32[]{:S(2)}) %collective-permute-start.99) | collective-permute-done | bytes 73760 | tf_op jit(solution)/shard_map/ppermute | solution.py:46
  608.6 7.1 convert_add_fusion.1
  630.4 5.1 collective-permute-done.103.refs_3_
  639.8 6.9 collective-permute-done.76
  670.1 4.4 gates_owner.1
  675.8 8.5 %copy.38 = f32[2,16,171,171]{3,1,2,0:T(8,128)} copy(f32[2,16,171,171]{3,2,1,0:T(8,128)} %get-tuple-element.204) | data formatting | bytes 7485696
  687.4 10.1 %collective-permute-done.94.refs_15_.refs_7_ = bf16[64,2688]{1,0:T(8,128)(2,1)S(1)} collective-permute-done((bf16[64,2688]{1,0:T(8,128)(2,1)S(1)}, bf16[64,2688]{1,0:T(8,128)(2,1)S(1)}, u32[]{:S(2)}, u32[]{:S(2)}) %collective-permute-start.94) | collective-permute-done | bytes 344096 | tf_op jit(solution)/shard_map/ppermute | solution.py:40
  713.5 7.3 fusion.13
  (533 shorter events, 250.6 us)
Async XLA Ops:
  7.2 120.9 %all-gather.4.cloned.1.call-start = ((), (), s32[]{:S(2)}) async-start(), calls=%async_computation.4 | async-start | bytes 5898240 | tf_op jit(solution)/shard_map/all_gather | solution.py:75
  36.7 206.1 %all-gather.6.cloned.1.call-start = ((), (), s32[]{:S(2)}) async-start(), calls=%async_computation.5 | async-start | bytes 7864320 | tf_op jit(solution)/shard_map/all_gather | solution.py:75
  36.7 28.5 %collective-permute-start = (bf16[256,2048]{1,0:T(8,128)(2,1)}, bf16[256,2048]{1,0:T(8,128)(2,1)}, u32[]{:S(2)}, u32[]{:S(2)}) collective-permute-start(bf16[256,2048]{1,0:T(8,128)(2,1)} %bitcast.276), channel_id=1, source_target_pairs={{0,2},{1,3},{2,0},{3,1},{4,6},{5,7},{6,4},{7,5},{8,10},{9,11},{10,... | collective-permute-start | bytes 3145736 | tf_op jit(solution)/shard_map/ppermute | solution.py:40
  36.8 25.6 %collective-permute-start.1 = (bf16[256,2048]{1,0:T(8,128)(2,1)}, bf16[256,2048]{1,0:T(8,128)(2,1)}, u32[]{:S(2)}, u32[]{:S(2)}) collective-permute-start(bf16[256,2048]{1,0:T(8,128)(2,1)} %bitcast.277), channel_id=1, source_target_pairs={{0,4},{1,5},{2,6},{3,7},{4,0},{5,1},{6,2},{7,3},{8,12},{9,13},{10,... | collective-permute-start | bytes 3145736 | tf_op jit(solution)/shard_map/ppermute | solution.py:40
  52.5 30.1 %collective-permute-start.4 = (bf16[256,2048]{1,0:T(8,128)(2,1)}, bf16[256,2048]{1,0:T(8,128)(2,1)}, u32[]{:S(2)}, u32[]{:S(2)}) collective-permute-start(bf16[256,2048]{1,0:T(8,128)(2,1)} %bitcast.278), channel_id=1, source_target_pairs={{0,1},{1,0},{2,3},{3,2},{4,5},{5,4},{6,7},{7,6},{8,9},{9,8},{10,11... | collective-permute-start | bytes 3145736 | tf_op jit(solution)/shard_map/ppermute | solution.py:40
  79.0 34.5 %collective-permute-start.5 = (bf16[256,2048]{1,0:T(8,128)(2,1)}, bf16[256,2048]{1,0:T(8,128)(2,1)S(1)}, u32[]{:S(2)}, u32[]{:S(2)}) collective-permute-start(bf16[256,2048]{1,0:T(8,128)(2,1)} %collective-permute-done), channel_id=1, source_target_pairs={{0,1},{1,0},{2,3},{3,2},{4,5},{5,4},{6,7},{7,6},{8,9},{9,8},{10,11... | collective-permute-start | bytes 3145736 | tf_op jit(solution)/shard_map/ppermute | solution.py:40
  79.6 35.1 %collective-permute-start.6 = (bf16[256,2048]{1,0:T(8,128)(2,1)}, bf16[256,2048]{1,0:T(8,128)(2,1)S(1)}, u32[]{:S(2)}, u32[]{:S(2)}) collective-permute-start(bf16[256,2048]{1,0:T(8,128)(2,1)} %collective-permute-done.1), channel_id=1, source_target_pairs={{0,1},{1,0},{2,3},{3,2},{4,5},{5,4},{6,7},{7,6},{8,9},{9,8},{10,11... | collective-permute-start | bytes 3145736 | tf_op jit(solution)/shard_map/ppermute | solution.py:40
  99.9 15.9 %collective-permute-start.7 = (bf16[128,2048]{1,0:T(8,128)(2,1)S(1)}, bf16[128,2048]{1,0:T(8,128)(2,1)S(1)}, u32[]{:S(2)}, u32[]{:S(2)}) collective-permute-start(bf16[128,2048]{1,0:T(8,128)(2,1)S(1)} %copy-done.73), channel_id=1, source_target_pairs={{0,1},{1,0},{2,3},{3,2},{4,5},{5,4},{6,7},{7,6},{8,9},{9,8},{10,11... | collective-permute-start | bytes 1572872 | tf_op jit(solution)/shard_map/ppermute | solution.py:40
  117.5 207.1 %all-gather.8.cloned.1.call-start = ((), (), s32[]{:S(2)}) async-start(), calls=%async_computation.6 | async-start | bytes 3932160 | tf_op jit(solution)/shard_map/all_gather | solution.py:75
  175.8 24.5 %collective-permute-start.27 = (bf16[128,2048]{1,0:T(8,128)(2,1)S(1)}, bf16[128,2048]{1,0:T(8,128)(2,1)S(1)}, u32[]{:S(2)}, u32[]{:S(2)}) collective-permute-start(bf16[128,2048]{1,0:T(8,128)(2,1)S(1)} %get-tuple-element.239), channel_id=1, source_target_pairs={{0,4},{1,5},{2,6},{3,7},{4,0},{5,1},{6,2},{7,3},{8,12},{9,13},{10,... | collective-permute-start | bytes 1572872 | tf_op jit(solution)/shard_map/ppermute | solution.py:40
  176.4 24.0 %collective-permute-start.32 = (bf16[128,2048]{1,0:T(8,128)(2,1)S(1)}, bf16[128,2048]{1,0:T(8,128)(2,1)S(1)}, u32[]{:S(2)}, u32[]{:S(2)}) collective-permute-start(bf16[128,2048]{1,0:T(8,128)(2,1)S(1)} %get-tuple-element.240), channel_id=1, source_target_pairs={{0,2},{1,3},{2,0},{3,1},{4,6},{5,7},{6,4},{7,5},{8,10},{9,11},{10,... | collective-permute-start | bytes 1572872 | tf_op jit(solution)/shard_map/ppermute | solution.py:40
  190.2 20.5 %collective-permute-start.29 = (bf16[128,2048]{1,0:T(8,128)(2,1)}, bf16[128,2048]{1,0:T(8,128)(2,1)S(1)}, u32[]{:S(2)}, u32[]{:S(2)}) collective-permute-start(bf16[128,2048]{1,0:T(8,128)(2,1)} %get-tuple-element.225), channel_id=1, source_target_pairs={{0,4},{1,5},{2,6},{3,7},{4,0},{5,1},{6,2},{7,3},{8,12},{9,13},{10,... | collective-permute-start | bytes 1572872 | tf_op jit(solution)/shard_map/ppermute | solution.py:40
  191.7 19.8 %collective-permute-start.31 = (bf16[128,2048]{1,0:T(8,128)(2,1)S(1)}, bf16[128,2048]{1,0:T(8,128)(2,1)}, u32[]{:S(2)}, u32[]{:S(2)}) collective-permute-start(bf16[128,2048]{1,0:T(8,128)(2,1)S(1)} %get-tuple-element.226), channel_id=1, source_target_pairs={{0,2},{1,3},{2,0},{3,1},{4,6},{5,7},{6,4},{7,5},{8,10},{9,11},{10,... | collective-permute-start | bytes 1572872 | tf_op jit(solution)/shard_map/ppermute | solution.py:40
  216.0 26.8 %collective-permute-start.33 = (bf16[256,2048]{1,0:T(8,128)(2,1)}, bf16[256,2048]{1,0:T(8,128)(2,1)}, u32[]{:S(2)}, u32[]{:S(2)}) collective-permute-start(bf16[256,2048]{1,0:T(8,128)(2,1)} %get-tuple-element.214), channel_id=1, source_target_pairs={{0,4},{1,5},{2,6},{3,7},{4,0},{5,1},{6,2},{7,3},{8,12},{9,13},{10,... | collective-permute-start | bytes 3145736 | tf_op jit(solution)/shard_map/ppermute | solution.py:40
  217.5 25.3 %collective-permute-start.34 = (bf16[256,2048]{1,0:T(8,128)(2,1)}, bf16[256,2048]{1,0:T(8,128)(2,1)}, u32[]{:S(2)}, u32[]{:S(2)}) collective-permute-start(bf16[256,2048]{1,0:T(8,128)(2,1)} %get-tuple-element.214), channel_id=1, source_target_pairs={{0,2},{1,3},{2,0},{3,1},{4,6},{5,7},{6,4},{7,5},{8,10},{9,11},{10,... | collective-permute-start | bytes 3145736 | tf_op jit(solution)/shard_map/ppermute | solution.py:40
  218.0 46.0 %collective-permute-start.37 = (bf16[256,2048]{1,0:T(8,128)(2,1)}, bf16[256,2048]{1,0:T(8,128)(2,1)}, u32[]{:S(2)}, u32[]{:S(2)}) collective-permute-start(bf16[256,2048]{1,0:T(8,128)(2,1)} %get-tuple-element.214), channel_id=1, source_target_pairs={{0,1},{1,0},{2,3},{3,2},{4,5},{5,4},{6,7},{7,6},{8,9},{9,8},{10,11... | collective-permute-start | bytes 3145736 | tf_op jit(solution)/shard_map/ppermute | solution.py:40
  251.8 201.6 %reduce-scatter.5.cloned.1.call-start = ((), (), s32[]{:S(2)}) async-start(), calls=%async_computation.7 | async-start | bytes 3932160 | tf_op jit(solution)/shard_map/reduce_scatter | solution.py:79
  258.7 50.5 %collective-permute-start.46 = (bf16[256,2048]{1,0:T(8,128)(2,1)}, bf16[256,2048]{1,0:T(8,128)(2,1)S(1)}, u32[]{:S(2)}, u32[]{:S(2)}) collective-permute-start(bf16[256,2048]{1,0:T(8,128)(2,1)} %bitcast.283), channel_id=1, source_target_pairs={{0,1},{1,0},{2,3},{3,2},{4,5},{5,4},{6,7},{7,6},{8,9},{9,8},{10,11... | collective-permute-start | bytes 3145736 | tf_op jit(solution)/shard_map/ppermute | solution.py:40
  261.8 32.8 %collective-permute-start.42 = (bf16[256,2048]{1,0:T(8,128)(2,1)}, bf16[256,2048]{1,0:T(8,128)(2,1)S(1)}, u32[]{:S(2)}, u32[]{:S(2)}) collective-permute-start(bf16[256,2048]{1,0:T(8,128)(2,1)} %bitcast.284), channel_id=1, source_target_pairs={{0,2},{1,3},{2,0},{3,1},{4,6},{5,7},{6,4},{7,5},{8,10},{9,11},{10,... | collective-permute-start | bytes 3145736 | tf_op jit(solution)/shard_map/ppermute | solution.py:40
  267.9 25.1 %collective-permute-start.43 = (bf16[256,2048]{1,0:T(8,128)(2,1)S(1)}, bf16[256,2048]{1,0:T(8,128)(2,1)S(1)}, u32[]{:S(2)}, u32[]{:S(2)}) collective-permute-start(bf16[256,2048]{1,0:T(8,128)(2,1)S(1)} %bitcast.285), channel_id=1, source_target_pairs={{0,4},{1,5},{2,6},{3,7},{4,0},{5,1},{6,2},{7,3},{8,12},{9,13},{10,... | collective-permute-start | bytes 3145736 | tf_op jit(solution)/shard_map/ppermute | solution.py:40
  324.5 188.5 %reduce-scatter.7.cloned.1.call-start = ((), (), s32[]{:S(2)}) async-start(), calls=%async_computation.8 | async-start | bytes 7864320 | tf_op jit(solution)/shard_map/reduce_scatter | solution.py:79
  381.2 162.8 %reduce-scatter.9.cloned.1.call-start = ((), (), s32[]{:S(2)}) async-start(), calls=%async_computation.9 | async-start | bytes 1966080 | tf_op jit(solution)/shard_map/reduce_scatter | solution.py:79
  405.4 40.6 %collective-permute-start.52 = (bf16[1024,2048]{1,0:T(8,128)(2,1)}, bf16[1024,2048]{1,0:T(8,128)(2,1)}, u32[]{:S(2)}, u32[]{:S(2)}) collective-permute-start(bf16[1024,2048]{1,0:T(8,128)(2,1)} %convolution_convert_fusion.4), channel_id=1, source_target_pairs={{0,1},{1,0},{2,3},{3,2},{4,5},{5,4},{6,7},{7,6},{8,9},{9,8},{10,11... | collective-permute-start | bytes 12582920 | tf_op jit(solution)/shard_map/ppermute | solution.py:40
  408.2 24.5 %collective-permute-start.59 = (bf16[128,2048]{1,0:T(8,128)(2,1)S(1)}, bf16[128,2048]{1,0:T(8,128)(2,1)S(1)}, u32[]{:S(2)}, u32[]{:S(2)}) collective-permute-start(bf16[128,2048]{1,0:T(8,128)(2,1)S(1)} %get-tuple-element.231), channel_id=1, source_target_pairs={{0,4},{1,5},{2,6},{3,7},{4,0},{5,1},{6,2},{7,3},{8,12},{9,13},{10,... | collective-permute-start | bytes 1572872 | tf_op jit(solution)/shard_map/ppermute | solution.py:40
  408.8 24.0 %collective-permute-start.64 = (bf16[128,2048]{1,0:T(8,128)(2,1)S(1)}, bf16[128,2048]{1,0:T(8,128)(2,1)S(1)}, u32[]{:S(2)}, u32[]{:S(2)}) collective-permute-start(bf16[128,2048]{1,0:T(8,128)(2,1)S(1)} %get-tuple-element.232), channel_id=1, source_target_pairs={{0,2},{1,3},{2,0},{3,1},{4,6},{5,7},{6,4},{7,5},{8,10},{9,11},{10,... | collective-permute-start | bytes 1572872 | tf_op jit(solution)/shard_map/ppermute | solution.py:40
  421.8 21.4 %collective-permute-start.61 = (bf16[128,2048]{1,0:T(8,128)(2,1)S(1)}, bf16[128,2048]{1,0:T(8,128)(2,1)S(1)}, u32[]{:S(2)}, u32[]{:S(2)}) collective-permute-start(bf16[128,2048]{1,0:T(8,128)(2,1)S(1)} %get-tuple-element.221), channel_id=1, source_target_pairs={{0,4},{1,5},{2,6},{3,7},{4,0},{5,1},{6,2},{7,3},{8,12},{9,13},{10,... | collective-permute-start | bytes 1572872 | tf_op jit(solution)/shard_map/ppermute | solution.py:40
  423.4 19.8 %collective-permute-start.63 = (bf16[128,2048]{1,0:T(8,128)(2,1)S(1)}, bf16[128,2048]{1,0:T(8,128)(2,1)S(1)}, u32[]{:S(2)}, u32[]{:S(2)}) collective-permute-start(bf16[128,2048]{1,0:T(8,128)(2,1)S(1)} %get-tuple-element.222), channel_id=1, source_target_pairs={{0,2},{1,3},{2,0},{3,1},{4,6},{5,7},{6,4},{7,5},{8,10},{9,11},{10,... | collective-permute-start | bytes 1572872 | tf_op jit(solution)/shard_map/ppermute | solution.py:40
  453.4 24.7 %collective-permute-start.66 = (bf16[256,2048]{1,0:T(8,128)(2,1)}, bf16[256,2048]{1,0:T(8,128)(2,1)S(1)}, u32[]{:S(2)}, u32[]{:S(2)}) collective-permute-start(bf16[256,2048]{1,0:T(8,128)(2,1)} %fusion.15), channel_id=1, source_target_pairs={{0,4},{1,5},{2,6},{3,7},{4,0},{5,1},{6,2},{7,3},{8,12},{9,13},{10,... | collective-permute-start | bytes 3145736 | tf_op jit(solution)/shard_map/ppermute | solution.py:40
  454.9 24.7 %collective-permute-start.65 = (bf16[256,2048]{1,0:T(8,128)(2,1)}, bf16[256,2048]{1,0:T(8,128)(2,1)S(1)}, u32[]{:S(2)}, u32[]{:S(2)}) collective-permute-start(bf16[256,2048]{1,0:T(8,128)(2,1)} %fusion.15), channel_id=1, source_target_pairs={{0,2},{1,3},{2,0},{3,1},{4,6},{5,7},{6,4},{7,5},{8,10},{9,11},{10,... | collective-permute-start | bytes 3145736 | tf_op jit(solution)/shard_map/ppermute | solution.py:40
  456.5 35.1 %collective-permute-start.69 = (bf16[256,2048]{1,0:T(8,128)(2,1)}, bf16[256,2048]{1,0:T(8,128)(2,1)S(1)}, u32[]{:S(2)}, u32[]{:S(2)}) collective-permute-start(bf16[256,2048]{1,0:T(8,128)(2,1)} %fusion.15), channel_id=1, source_target_pairs={{0,1},{1,0},{2,3},{3,2},{4,5},{5,4},{6,7},{7,6},{8,9},{9,8},{10,11... | collective-permute-start | bytes 3145736 | tf_op jit(solution)/shard_map/ppermute | solution.py:40
  502.7 201.5 %reduce-scatter.11.cloned.1.call-start = ((), (), s32[]{:S(2)}) async-start(), calls=%async_computation.10 | async-start | bytes 3932160 | tf_op jit(solution)/shard_map/reduce_scatter | solution.py:79
  563.2 45.3 %collective-permute-start.74 = (bf16[1024,2048]{1,0:T(8,128)(2,1)}, bf16[1024,2048]{1,0:T(8,128)(2,1)}, u32[]{:S(2)}, u32[]{:S(2)}) collective-permute-start(bf16[1024,2048]{1,0:T(8,128)(2,1)} %convolution_convert_fusion.3), channel_id=1, source_target_pairs={{0,1},{1,0},{2,3},{3,2},{4,5},{5,4},{6,7},{7,6},{8,9},{9,8},{10,11... | collective-permute-start | bytes 12582920 | tf_op jit(solution)/shard_map/ppermute | solution.py:40
  568.4 21.8 %collective-permute-start.54 = (bf16[128,2048]{1,0:T(8,128)(2,1)S(1)}, bf16[128,2048]{1,0:T(8,128)(2,1)S(1)}, u32[]{:S(2)}, u32[]{:S(2)}) collective-permute-start(bf16[128,2048]{1,0:T(8,128)(2,1)S(1)} %get-tuple-element.237), channel_id=1, source_target_pairs={{0,2},{1,3},{2,0},{3,1},{4,6},{5,7},{6,4},{7,5},{8,10},{9,11},{10,... | collective-permute-start | bytes 1572872 | tf_op jit(solution)/shard_map/ppermute | solution.py:40
  569.4 21.7 %collective-permute-start.56 = (bf16[128,2048]{1,0:T(8,128)(2,1)S(1)}, bf16[128,2048]{1,0:T(8,128)(2,1)S(1)}, u32[]{:S(2)}, u32[]{:S(2)}) collective-permute-start(bf16[128,2048]{1,0:T(8,128)(2,1)S(1)} %get-tuple-element.235), channel_id=1, source_target_pairs={{0,4},{1,5},{2,6},{3,7},{4,0},{5,1},{6,2},{7,3},{8,12},{9,13},{10,... | collective-permute-start | bytes 1572872 | tf_op jit(solution)/shard_map/ppermute | solution.py:40
  583.6 35.4 %collective-permute-start.53 = (bf16[128,2048]{1,0:T(8,128)(2,1)}, bf16[128,2048]{1,0:T(8,128)(2,1)S(1)}, u32[]{:S(2)}, u32[]{:S(2)}) collective-permute-start(bf16[128,2048]{1,0:T(8,128)(2,1)} %get-tuple-element.238), channel_id=1, source_target_pairs={{0,4},{1,5},{2,6},{3,7},{4,0},{5,1},{6,2},{7,3},{8,12},{9,13},{10,... | collective-permute-start | bytes 1572872 | tf_op jit(solution)/shard_map/ppermute | solution.py:40
  591.1 17.3 %collective-permute-start.99 = (bf16[48,768]{1,0:T(8,128)(2,1)S(1)}, bf16[48,768]{1,0:T(8,128)(2,1)S(1)}, u32[]{:S(2)}, u32[]{:S(2)}) collective-permute-start(bf16[48,768]{1,0:T(8,128)(2,1)S(1)} %fusion.66), channel_id=1, source_target_pairs={{0,16},{1,17},{2,18},{3,19},{4,20},{5,21},{6,22},{7,23},{8,24},{9,... | collective-permute-start | bytes 221192 | tf_op jit(solution)/shard_map/ppermute | solution.py:46
  599.2 21.9 %collective-permute-start.58 = (bf16[128,2048]{1,0:T(8,128)(2,1)}, bf16[128,2048]{1,0:T(8,128)(2,1)S(1)}, u32[]{:S(2)}, u32[]{:S(2)}) collective-permute-start(bf16[128,2048]{1,0:T(8,128)(2,1)} %get-tuple-element.236), channel_id=1, source_target_pairs={{0,2},{1,3},{2,0},{3,1},{4,6},{5,7},{6,4},{7,5},{8,10},{9,11},{10,... | collective-permute-start | bytes 1572872 | tf_op jit(solution)/shard_map/ppermute | solution.py:40
  599.2 23.5 %collective-permute-start.55 = (bf16[128,2048]{1,0:T(8,128)(2,1)S(1)}, bf16[128,2048]{1,0:T(8,128)(2,1)S(1)}, u32[]{:S(2)}, u32[]{:S(2)}) collective-permute-start(bf16[128,2048]{1,0:T(8,128)(2,1)S(1)} %get-tuple-element.224), channel_id=1, source_target_pairs={{0,4},{1,5},{2,6},{3,7},{4,0},{5,1},{6,2},{7,3},{8,12},{9,13},{10,... | collective-permute-start | bytes 1572872 | tf_op jit(solution)/shard_map/ppermute | solution.py:40
  608.4 16.2 %collective-permute-start.57 = (bf16[128,2048]{1,0:T(8,128)(2,1)S(1)}, bf16[128,2048]{1,0:T(8,128)(2,1)S(1)}, u32[]{:S(2)}, u32[]{:S(2)}) collective-permute-start(bf16[128,2048]{1,0:T(8,128)(2,1)S(1)} %get-tuple-element.223), channel_id=1, source_target_pairs={{0,2},{1,3},{2,0},{3,1},{4,6},{5,7},{6,4},{7,5},{8,10},{9,11},{10,... | collective-permute-start | bytes 1572872 | tf_op jit(solution)/shard_map/ppermute | solution.py:40
  622.7 24.0 %collective-permute-start.76 = (bf16[128,2048]{1,0:T(8,128)(2,1)}, bf16[128,2048]{1,0:T(8,128)(2,1)}, u32[]{:S(2)}, u32[]{:S(2)}) collective-permute-start(bf16[128,2048]{1,0:T(8,128)(2,1)} %get-tuple-element.229), channel_id=1, source_target_pairs={{0,2},{1,3},{2,0},{3,1},{4,6},{5,7},{6,4},{7,5},{8,10},{9,11},{10,... | collective-permute-start | bytes 1572872 | tf_op jit(solution)/shard_map/ppermute | solution.py:40
  624.6 23.4 %collective-permute-start.78 = (bf16[128,2048]{1,0:T(8,128)(2,1)}, bf16[128,2048]{1,0:T(8,128)(2,1)}, u32[]{:S(2)}, u32[]{:S(2)}) collective-permute-start(bf16[128,2048]{1,0:T(8,128)(2,1)} %get-tuple-element.227), channel_id=1, source_target_pairs={{0,4},{1,5},{2,6},{3,7},{4,0},{5,1},{6,2},{7,3},{8,12},{9,13},{10,... | collective-permute-start | bytes 1572872 | tf_op jit(solution)/shard_map/ppermute | solution.py:40
  637.9 16.1 %collective-permute-start.89 = (bf16[64,2688]{1,0:T(8,128)(2,1)S(1)}, bf16[64,2688]{1,0:T(8,128)(2,1)S(1)}, u32[]{:S(2)}, u32[]{:S(2)}) collective-permute-start(bf16[64,2688]{1,0:T(8,128)(2,1)S(1)} %get-tuple-element.159), channel_id=1, source_target_pairs={{0,2},{1,3},{2,0},{3,1},{4,6},{5,7},{6,4},{7,5},{8,10},{9,11},{10,... | collective-permute-start | bytes 1032200 | tf_op jit(solution)/shard_map/ppermute | solution.py:40
  639.8 18.2 %collective-permute-start.90 = (bf16[64,2688]{1,0:T(8,128)(2,1)S(1)}, bf16[64,2688]{1,0:T(8,128)(2,1)S(1)}, u32[]{:S(2)}, u32[]{:S(2)}) collective-permute-start(bf16[64,2688]{1,0:T(8,128)(2,1)S(1)} %get-tuple-element.160), channel_id=1, source_target_pairs={{0,3},{1,2},{2,1},{3,0},{4,7},{5,6},{6,5},{7,4},{8,11},{9,10},{10,... | collective-permute-start | bytes 1032200 | tf_op jit(solution)/shard_map/ppermute | solution.py:40
  651.1 33.2 %collective-permute-start.93 = (bf16[64,2688]{1,0:T(8,128)(2,1)S(1)}, bf16[64,2688]{1,0:T(8,128)(2,1)S(1)}, u32[]{:S(2)}, u32[]{:S(2)}) collective-permute-start(bf16[64,2688]{1,0:T(8,128)(2,1)S(1)} %get-tuple-element.163), channel_id=1, source_target_pairs={{0,6},{1,7},{2,4},{3,5},{4,2},{5,3},{6,0},{7,1},{8,14},{9,15},{10,... | collective-permute-start | bytes 1032200 | tf_op jit(solution)/shard_map/ppermute | solution.py:40
  654.0 46.9 %collective-permute-start.75 = (bf16[128,2048]{1,0:T(8,128)(2,1)}, bf16[128,2048]{1,0:T(8,128)(2,1)}, u32[]{:S(2)}, u32[]{:S(2)}) collective-permute-start(bf16[128,2048]{1,0:T(8,128)(2,1)} %get-tuple-element.230), channel_id=1, source_target_pairs={{0,4},{1,5},{2,6},{3,7},{4,0},{5,1},{6,2},{7,3},{8,12},{9,13},{10,... | collective-permute-start | bytes 1572872 | tf_op jit(solution)/shard_map/ppermute | solution.py:40
  658.0 42.9 %collective-permute-start.80 = (bf16[128,2048]{1,0:T(8,128)(2,1)}, bf16[128,2048]{1,0:T(8,128)(2,1)}, u32[]{:S(2)}, u32[]{:S(2)}) collective-permute-start(bf16[128,2048]{1,0:T(8,128)(2,1)} %get-tuple-element.228), channel_id=1, source_target_pairs={{0,2},{1,3},{2,0},{3,1},{4,6},{5,7},{6,4},{7,5},{8,10},{9,11},{10,... | collective-permute-start | bytes 1572872 | tf_op jit(solution)/shard_map/ppermute | solution.py:40
  658.7 42.2 %collective-permute-start.77 = (bf16[128,2048]{1,0:T(8,128)(2,1)}, bf16[128,2048]{1,0:T(8,128)(2,1)}, u32[]{:S(2)}, u32[]{:S(2)}) collective-permute-start(bf16[128,2048]{1,0:T(8,128)(2,1)} %get-tuple-element.220), channel_id=1, source_target_pairs={{0,4},{1,5},{2,6},{3,7},{4,0},{5,1},{6,2},{7,3},{8,12},{9,13},{10,... | collective-permute-start | bytes 1572872 | tf_op jit(solution)/shard_map/ppermute | solution.py:40
  663.5 37.3 %collective-permute-start.79 = (bf16[128,2048]{1,0:T(8,128)(2,1)}, bf16[128,2048]{1,0:T(8,128)(2,1)}, u32[]{:S(2)}, u32[]{:S(2)}) collective-permute-start(bf16[128,2048]{1,0:T(8,128)(2,1)} %get-tuple-element.219), channel_id=1, source_target_pairs={{0,2},{1,3},{2,0},{3,1},{4,6},{5,7},{6,4},{7,5},{8,10},{9,11},{10,... | collective-permute-start | bytes 1572872 | tf_op jit(solution)/shard_map/ppermute | solution.py:40
  (157 other events, 2326.5 us)
Sparse Core Ops, SparseCore 0:
  36.8 89.9 all-gather.3
  128.9 113.7 all-gather.5
  251.9 62.0 all-gather.7
  324.7 57.6 reduce-scatter.4
  384.5 110.7 reduce-scatter.6
  502.8 32.8 reduce-scatter.8
  563.4 67.1 reduce-scatter.10

commit v3 on v2

--- a/solution.py
+++ b/solution.py
@@ -81,12 +81,10 @@
     )
 
 
-def ring_stack(block, turn, groups, wait_for=()):
-    arrived = [onward(block, step) for step in range(1, groups)]
-    arrived, _ = lax.optimization_barrier((arrived, wait_for))
+def ring_stack(block, turn, groups):
     out = jnp.broadcast_to(block, (groups,) + block.shape)
     for step in range(1, groups):
-        out = put(out, arrived[step - 1], (turn + groups - step) % groups)
+        out = put(out, onward(block, step), (turn + groups - step) % groups)
     return out
 
 
@@ -96,6 +94,12 @@
     for step in range(1, groups):
         total = total + wide(onward(pick(chunks, (turn + step) % groups), step))
     return low(total)
+
+
+def exchange(pieces):
+    count = device_count()
+    sets = [list(range(i, i + GROUP)) for i in range(0, count, GROUP)]
+    return lax.all_to_all(pieces, AXES, 0, 0, axis_index_groups=sets)
 
 
 def all_swapped(parts):
@@ -238,42 +242,29 @@
         tiny[place[0] ^ bit] = wide(parts[bit][rows:])[:1, : tiny.shape[2]]
 
 
-def deal_kernel(place, *refs):
-    values, outs = refs[:-GROUP], refs[-GROUP:]
-    for bit in range(GROUP):
-        begin = 0
-        for ref in values:
-            outs[bit][:, begin : begin + ref.shape[2]] = ref[place[0] ^ bit]
-            begin += ref.shape[2]
-
-
-def hidden_owner_kernel(place, gate, linear, gain, *refs):
-    parts, outs = refs[:GROUP], refs[GROUP:]
+def hidden_owner_kernel(place, gate, linear, gain, grads, *outs):
     part = gate.shape[1] // GROUP
     total = jnp.zeros((gate.shape[0], 1), F32)
-    for bit in range(GROUP):
-        columns = pl.ds(pl.multiple_of((place[0] ^ bit) * part, 128), part)
-        d_gate, d_linear = wide(parts[bit][:, :part]), wide(parts[bit][:, part : 2 * part])
+    for device in range(GROUP):
+        columns = slice(device * part, device * part + part)
+        d_gate = wide(grads[device, :, :part])
+        d_linear = wide(grads[device, :, part : 2 * part])
         outs[0][:, columns] = d_gate
         outs[1][:, columns] = d_linear
-        outs[2][:, columns] = wide(parts[bit][:, 2 * part : 3 * part])
+        outs[2][:, columns] = wide(grads[device, :, 2 * part :])
         terms = d_gate * wide(gate[:, columns]) + d_linear * wide(linear[:, columns])
         total = total + jnp.sum(terms, axis=1, keepdims=True)
     outs[3][...] = total / gain[...]
 
 
-def mixer_owner_kernel(place, branch, gating, gain, *refs):
-    boths, lasts = refs[:GROUP], refs[GROUP : 2 * GROUP]
-    outs, held = refs[2 * GROUP : -1], refs[-1]
-    for bit in range(GROUP):
-        held[place[0] ^ bit, :, : 2 * WIDE] = wide(boths[bit][...])
-        held[place[0] ^ bit, :, 2 * WIDE :] = wide(lasts[bit][:, -WIDE:])
-    for slot in range(3):
-        for i in range(NBLK):
-            begin = slot * WIDE + (i % 2) * PAD
-            outs[slot][:, BEGINS[i] : BEGINS[i] + SIZES[i]] = held[
-                i // 2, :, begin : begin + SIZES[i]
-            ]
+def mixer_owner_kernel(place, branch, gating, gain, both, last, *outs):
+    for i in range(NBLK):
+        columns = slice(BEGINS[i], BEGINS[i] + SIZES[i])
+        begin = (i % 2) * PAD
+        values = wide(both[i // 2])
+        outs[0][:, columns] = values[:, begin : begin + SIZES[i]]
+        outs[1][:, columns] = values[:, WIDE + begin : WIDE + begin + SIZES[i]]
+        outs[2][:, columns] = wide(last[i // 2])[:, begin : begin + SIZES[i]]
     terms = outs[0][...] * wide(branch[...]) + outs[1][...] * wide(gating[...])
     outs[3][...] = jnp.sum(terms, axis=1, keepdims=True) / gain[...]
 
@@ -319,8 +310,10 @@
 def pair_product(left, right, first=None):
     half = left.shape[0] // 2
     far = low(contract_cols(left[half:], right))
-    near = left[:half] if first is None else after(left[:half], first)
-    return pair_total(contract_cols(near, right), far)
+    if first is None:
+        return pair_total(contract_cols(left[:half], right), far)
+    near, first = lax.optimization_barrier((left[:half], first))
+    return pair_total(contract_cols(near, right), far), first
 
 
 def sigmoid(values):
@@ -384,11 +377,13 @@
 
 def forward_kernel(
     place,
-    pre,
+    normed,
     segment,
+    both_weight,
     weight,
     bias,
     params,
+    pre,
     state_out,
     mixed_out,
     padded,
@@ -411,6 +406,7 @@
         padded[0:8] = padded[steps : steps + 8]
         numbers[0:8] = numbers[steps : steps + 8]
 
+    pre[0] = product(normed[0], both_weight[...])
     padded[8 : 8 + steps] = pre[0, :, :width]
     numbers[8 : 8 + steps] = segment[0]
     masks, fresh = same_masks(numbers, steps, width)
@@ -451,7 +447,8 @@
     segment_rim,
     state,
     state_rim,
-    d_mixed,
+    middle,
+    out_weight,
     weight,
     bias,
     params,
@@ -496,7 +493,7 @@
         conv, fresh, weight[...], bias[...], params[7:8]
     )
     value, slope = gelu_both(pre[0, :, width:])
-    d_out = d_mixed[0]
+    d_out = product(middle[0], out_weight[...])
     d_both[0, :, width:] = low(d_out * state[0] * slope)
     d_state = d_out * value
     for lane in range(width // 128):
@@ -568,7 +565,7 @@
         )
 
 
-def mixer_calls(rows, shards, steps, channels):
+def mixer_calls(rows, shards, steps, channels, model):
     blocks = rows * shards
 
     def position(row, shard, place):
@@ -588,15 +585,17 @@
             num_scalar_prefetch=1,
             grid=(rows, shards),
             in_specs=[
-                pl.BlockSpec(
-                    (1, steps, 2 * channels), lambda r, s, p: (position(r, s, p[0]), 0, 0)
-                ),
+                pl.BlockSpec((1, steps, model), lambda r, s, p: (position(r, s, p[0]), 0, 0)),
                 pl.BlockSpec((1, steps, 128), lambda r, s, p: (r * shards + s, 0, 0)),
+                whole(model, 2 * channels),
                 whole(channels, 2 * channels),
                 whole(1, 2 * channels),
                 whole(8, channels),
             ],
             out_specs=[
+                pl.BlockSpec(
+                    (1, steps, 2 * channels), lambda r, s, p: (position(r, s, p[0]), 0, 0)
+                ),
                 pl.BlockSpec((1, steps, channels), lambda r, s, p: (r * shards + s, 0, 0)),
                 pl.BlockSpec((1, steps, channels), lambda r, s, p: (position(r, s, p[0]), 0, 0)),
             ],
@@ -609,6 +608,7 @@
             ],
         ),
         out_shape=[
+            jax.ShapeDtypeStruct((blocks, steps, 2 * channels), F32),
             jax.ShapeDtypeStruct((blocks, steps, channels), F32),
             jax.ShapeDtypeStruct((blocks, steps, channels), BF16),
         ],
@@ -646,8 +646,9 @@
                     lambda r, s, p: (r * shards + before(s), steps // 8 - 1, 0),
                 ),
                 pl.BlockSpec(
-                    (1, steps, channels), lambda r, s, p: (position(r, turned(s), p[0]), 0, 0)
+                    (1, steps, model), lambda r, s, p: (position(r, turned(s), p[0]), 0, 0)
                 ),
+                pl.BlockSpec((model, channels), lambda r, s, p: (0, 2)),
                 whole(channels, 2 * channels),
                 whole(1, 2 * channels),
                 whole(8, channels),
@@ -676,7 +677,7 @@
         ],
         compiler_params=params,
         cost_estimate=pl.CostEstimate(
-            flops=blocks * steps * channels * channels * 12,
+            flops=blocks * steps * channels * (channels * 12 + model * 2),
             bytes_accessed=blocks * steps * channels * 24,
             transcendentals=blocks * steps * channels * 8,
         ),
@@ -770,7 +771,7 @@
         [((GROUP, own_rows, 2 * hidden_part), BF16), ((GROUP, own_rows, hidden_part), BF16)],
     )
     pair_weight = ring_gather(pair_rows.reshape(-1, 2 * hidden_part))
-    pre = product(after(normed, pair_rows), both_weight).reshape(GROUP, steps, 2 * WIDE)
+    normed_blocks = after(normed, pair_rows).reshape(GROUP, steps, model_width)
 
     rate = -8.0 * jax.nn.softplus(-decay_param)
     params = jnp.concatenate(
@@ -789,8 +790,10 @@
         ],
         axis=0,
     )
-    mixer_forward, mixer_backward = mixer_calls(rows, shards, steps, WIDE)
-    state, mixed = mixer_forward(where, pre, segments, gate_weight, bias, params)
+    mixer_forward, mixer_backward = mixer_calls(rows, shards, steps, WIDE, model_width)
+    pre, state, mixed = mixer_forward(
+        where, normed_blocks, segments, mixer_weight, gate_weight, bias, params
+    )
     mixed = mixed.reshape(tokens, WIDE)
     last_weight = ring_gather(after(last_rows, mixed).reshape(-1, hidden_part))
     middle = inputs + group_total(pair_product(mixed, out_weight))
@@ -805,43 +808,59 @@
     pair = product(normed_mid, pair_weight)
     gate_pre, linear_pre = pair[:, :hidden_part], pair[:, hidden_part:]
     value, slope = gelu_both(gate_pre)
-    hidden = low(value * linear_pre)
+    hidden, value, slope = lax.optimization_barrier(
+        (low(value * linear_pre), value, linear_pre * slope)
+    )
     grad_last_low = low(contract_rows(upstream_all, hidden))
     grad_last = ring_reduce(grad_last_low)
-    d_hidden = product(after(upstream_all, grad_last_low), last_weight)
+    half = tokens // 2
+    hidden_far = low(contract_cols(after(hidden[half:], grad_last_low), last_weight))
+    d_hidden = product(after(upstream_all, grad_last_low, hidden_far), last_weight)
     d_pair = jnp.concatenate(
-        [low(d_hidden * linear_pre * slope), low(d_hidden * value)], axis=1
-    )
-    grad_pair_low = low(contract_rows(normed_mid, d_pair))
+        [low(d_hidden * slope), low(d_hidden * value)], axis=1
+    )
+    hidden_near = contract_cols(after(hidden[:half], d_pair), last_weight)
+    hidden_out = pair_total(hidden_near, hidden_far)
+    hidden_sent = send_totals(hidden_out)
+    grad_pair_low = low(contract_rows(normed_mid, after(d_pair, hidden_out)))
     grad_pair = ring_reduce(grad_pair_low)
-    d_normed_mid = pair_product(after(d_pair, grad_pair_low), pair_weight)
-    hidden_out = pair_product(after(hidden, d_normed_mid), last_weight)
-    result = low(middle + group_total(hidden_out))
+    d_pair, hidden_sent = lax.optimization_barrier((after(d_pair, grad_pair_low), hidden_sent))
+    d_normed_mid, hidden_out = pair_product(
+        d_pair, pair_weight, join_totals(hidden_out, hidden_sent)
+    )
+    result = low(middle + hidden_out)
     d_middle = upstream + norm_back(
         middle, middle_scale, hidden_scale, group_total(d_normed_mid)
     )
 
-    def to_owner(name, *grads):
-        grads = [values.reshape(GROUP, own_rows, -1) for values in grads]
-        width = sum(values.shape[2] for values in grads)
-        parts = simple_call(
-            deal_kernel, name, where, grads, [((own_rows, width), BF16)] * GROUP
-        )
-        return all_swapped(parts)
-
-    middle_low = group_gather(after(low(d_middle), grad_last, hidden_out))
-    d_mixed = product(middle_low, out_weight).reshape(GROUP, steps, WIDE)
+    def to_owner(grads):
+        return exchange(grads.reshape(GROUP, own_rows, -1))
+
+    own = after(low(d_middle), grad_last)
+    middle_low = group_gather(own)
     grad_out_low = low(contract_rows(middle_low, mixed))
     grad_out = ring_reduce(grad_out_low)
-    d_mixed = after(d_mixed, grad_out_low, grad_pair)
+    middle_blocks = after(middle_low, grad_out_low, grad_pair).reshape(GROUP, steps, model_width)
+    hidden_grads = to_owner(jnp.concatenate([grad_pair, grad_last], axis=1))
     d_both, packed = mixer_backward(
-        where, pre, pre, segments, segments, state, state, d_mixed, gate_weight, bias, params
+        where,
+        pre,
+        pre,
+        segments,
+        segments,
+        state,
+        state,
+        middle_blocks,
+        mixer_weight,
+        gate_weight,
+        bias,
+        params,
     )
     d_both = d_both.reshape(tokens, 2 * WIDE)
-    grad_both_low = low(contract_rows(normed, after(d_both, grad_out)))
+    grad_both_low = low(contract_rows(normed, after(d_both, grad_out, hidden_grads)))
     grad_both = ring_reduce(grad_both_low)
-    early_parts = to_owner("deal_early", grad_pair, grad_last, grad_out)
-    d_normed = pair_product(after(d_both, grad_both_low), both_weight)
+    packed = ring_sum(packed, turn, groups)
+    d_normed, packed = pair_product(after(d_both, grad_both_low), both_weight, packed)
     d_normed = group_total(d_normed)
     stream_grad = low(d_middle + norm_back(inputs, inputs_scale, mixer_scale, d_normed))
 
@@ -850,22 +869,16 @@
         "hidden_owner",
         where,
         (hidden_gate, hidden_linear, wide(hidden_gain)[:, None])
-        + tuple(early_parts),
+        + (hidden_grads,),
         [((own_rows, hidden_width), F32)] * 3 + [((own_rows, 1), F32)],
     )
-    grad_branch, grad_gating, grad_output, grad_mgain = simple_call(
-        mixer_owner_kernel,
-        "mixer_owner",
-        where,
-        (branch_weight, gating_weight, wide(mixer_gain)[:, None])
-        + tuple(to_owner("deal_both", grad_both) + early_parts),
-        [((own_rows, R), F32)] * 3 + [((own_rows, 1), F32)],
-        [pltpu.VMEM((GROUP, own_rows, 3 * WIDE), F32)],
-    )
-
-    packed = ring_stack(ring_sum(packed, turn, groups), turn, groups).reshape(PAD, 2 * WIDE)
+    both_grads, out_grads = to_owner(grad_both), to_owner(grad_out)
+
+    packed = ring_stack(packed, turn, groups).reshape(PAD, 2 * WIDE)
+    packed, out_grads = lax.optimization_barrier((packed, out_grads))
     across, along = swap(packed, 4), swap(packed, 2)
     near = [packed, along, across, swap(across, 2)]
+    near, both_grads = lax.optimization_barrier((near, both_grads))
     grad_gblocks, small = simple_call(
         gates_owner_kernel,
         "gates_owner",
@@ -875,6 +888,15 @@
         [pltpu.VMEM((GROUP, 8, WIDE), F32)],
     )
     grad_decay = 8.0 * jax.nn.sigmoid(-decay_param) * small[7]
+
+    grad_branch, grad_gating, grad_output, grad_mgain = simple_call(
+        mixer_owner_kernel,
+        "mixer_owner",
+        where,
+        (branch_weight, gating_weight, wide(mixer_gain)[:, None])
+        + (both_grads, out_grads),
+        [((own_rows, R), F32)] * 3 + [((own_rows, 1), F32)],
+    )
 
     shape = (rows_here, steps, model_width)
     return (

time: 740 us -> 722 us (0.976)
  matrix products: 162 us -> 133 us
  Pallas kernels: 72.8 us -> 83.2 us
    dot_general x4 -> x2, matrix products: 58.3 us -> 31 us  [product(): return jnp.dot(left, right, preferred_element_type=F32)]
    ppermute x99 -> x85, starting transfers between devices: 87.2 us -> 71.8 us  [swap(): lax.ppermute(values, AXES, [(i, i ^ bit) for i in range(device_count())])]
    ppermute x9, waiting for transfers between devices: 29.7 us -> 14.7 us  [onward(): return lax.ppermute(values, AXES, pairs)]
    all_to_all x0 -> x3, starting transfers between devices: none -> 11.9 us  [exchange(): return lax.all_to_all(pieces, AXES, 0, 0, axis_index_groups=sets)]
    pallas_call x2, Pallas kernels: 49.5 us -> 60 us  [the longest x1 33.5 us: local(): mixer_backward(where, pre, pre, segments, segments, state, state, middle_...]
    ppermute x9, starting transfers between devices: 10.5 us -> 19.5 us  [onward(): return lax.ppermute(values, AXES, pairs)]
    convert_element_type x10 -> x8, other arithmetic: 22.7 us -> 17.2 us  [low(): return values.astype(BF16)]
    unnamed x220 -> x188, local copies, waits for them, and re-layouts: 65.3 us -> 63 us
  transfers between devices with their start and end apart: 115 -> 104, of which waited for: 47 -> 41; matrix products, arithmetic and copies ran while one was open for 34% -> 29% of each run, Pallas kernels for 10% -> 11%
where the time goes in v3:
time: 722 us; the launch traced here: 716 us
  waiting for transfers between devices  248 us (34%)
  matrix products  133 us (18%)
  starting transfers between devices  104 us (14%)
  local copies, waits for them, and re-layouts  88.2 us (12%)
  Pallas kernels  83.2 us (12%)
  other arithmetic  44.4 us (6%)
  between operations  15.8 us (2%)
    ppermute x85, waiting for transfers between devices, swap(): lax.ppermute(values, AXES, [(i, i ^ bit) for i in range(device_count())])  201 us
    ppermute x85, starting transfers between devices, swap(): lax.ppermute(values, AXES, [(i, i ^ bit) for i in range(device_count())])  71.8 us
    unnamed x188, local copies, waits for them, and re-layouts  63 us
    dot_general x8, matrix products, contract_cols(): lax.dot_general(left, right, (((1,), (1,)), ((), ())), preferred_element_...  56.5 us
    dot_general x4, matrix products, contract_rows(): lax.dot_general(left, right, (((0,), (0,)), ((), ())), preferred_element_...  45.4 us
    pallas_call x1, Pallas kernels, local(): mixer_backward(where, pre, pre, segments, segments, state, state, middle_...  33.5 us
    dot_general x2, matrix products, product(): return jnp.dot(left, right, preferred_element_type=F32)  31 us
    pallas_call x1, Pallas kernels, local(): mixer_forward(where, normed_blocks, segments, mixer_weight, gate_weight,...  26.4 us
  transfers between devices with their start and end apart: 104, of which 41 were waited for; matrix products, arithmetic and copies ran while one was open for 29% of the time, Pallas kernels for 11%

profile of v3, /device:TPU:0, one launch (start us, length us, event | category | flops | bytes accessed | tf_op | source)
XLA Modules:
  0.0 715.6 jit_solution(16304718241758884041)
XLA Ops:
  25.9 5.7 collective-permute-done.14.refs_6_
  31.6 3.9 collective-permute-done.15.refs_7_
  51.3 11.0 %collective-permute-done.1 = bf16[256,2048]{1,0:T(8,128)(2,1)} collective-permute-done((bf16[256,2048]{1,0:T(8,128)(2,1)}, bf16[256,2048]{1,0:T(8,128)(2,1)}, u32[]{:S(2)}, u32[]{:S(2)}) %collective-permute-start.1) | collective-permute-done | bytes 1048608 | tf_op jit(solution)/shard_map/ppermute | solution.py:40
  71.3 8.5 %collective-permute-done.2 = bf16[128,2048]{1,0:T(8,128)(2,1)S(1)} collective-permute-done((bf16[128,2048]{1,0:T(8,128)(2,1)S(1)}, bf16[128,2048]{1,0:T(8,128)(2,1)S(1)}, u32[]{:S(2)}, u32[]{:S(2)}) %collective-permute-start.2) | collective-permute-done | bytes 524320 | tf_op jit(solution)/shard_map/ppermute | solution.py:40
  93.9 4.1 collective-permute-done.21.refs_3_
  105.1 5.5 collective-permute-done.24.refs_6_
  110.6 5.2 collective-permute-done.25.refs_7_
  121.4 10.2 %norm_rows.1 = bf16[2048,2048]{1,0:T(8,128)(2,1)} custom-call(bf16[2048,2048]{1,0:T(8,128)(2,1)} %constant_dynamic-update-slice_fusion.values, f32[1,2048]{1,0:T(1,128)S(1)} %reshape.466.gain), custom_call_target="tpu_custom_call" | custom-call | flops 1 | bytes 1 | tf_op jit(solution)/shard_map/norm_rows/pallas_call | solution.py:172
  132.1 26.4 %mixer_forward.1 = (f32[8,256,768]{2,1,0:T(8,128)}, f32[8,256,384]{2,1,0:T(8,128)}, bf16[8,256,384]{2,1,0:T(8,128)(2,1)S(1)}) custom-call(s32[1]{0:T(128)} %bitcast.1.place, bf16[8,256,2048]{2,1,0:T(8,128)(2,1)} %bitcast.249, f32[8,256,128]{2,1,0:T(8,128)S(1)} %broadcast_in_dim.71.segment.segment_rim, ...), custom_call_target="tpu_custom_call" | custom-call | flops 1 | bytes 1 | tf_op jit(solution)/shard_map/mixer_forward/pallas_call | solution.py:794
  161.9 6.8 collective-permute-done.26
  176.4 10.7 %collective-permute-done.28 = bf16[128,2048]{1,0:T(8,128)(2,1)S(1)} collective-permute-done((bf16[128,2048]{1,0:T(8,128)(2,1)S(1)}, bf16[128,2048]{1,0:T(8,128)(2,1)S(1)}, u32[]{:S(2)}, u32[]{:S(2)}) %collective-permute-start.28) | collective-permute-done | bytes 524320 | tf_op jit(solution)/shard_map/ppermute | solution.py:40
  192.1 6.3 collective-permute-done.27
  198.4 10.7 %collective-permute-done.29 = bf16[128,2048]{1,0:T(8,128)(2,1)S(1)} collective-permute-done((bf16[128,2048]{1,0:T(8,128)(2,1)}, bf16[128,2048]{1,0:T(8,128)(2,1)S(1)}, u32[]{:S(2)}, u32[]{:S(2)}) %collective-permute-start.29) | collective-permute-done | bytes 524320 | tf_op jit(solution)/shard_map/ppermute | solution.py:40
  218.0 24.8 %all-gather.6.cloned.1.call-done = bf16[2048,1536]{1,0:T(8,128)(2,1)} async-done(((bf16[512,1536]{1,0:T(8,128)(2,1)}), bf16[2048,1536]{1,0:T(8,128)(2,1)}) %all-gather.6.cloned.1.call-update) | async-done | bytes 6291472 | tf_op jit(solution)/shard_map/all_gather | solution.py:75
  253.6 4.2 collective-permute-done.35
  272.3 17.6 %fusion.77 = f32[2048,1536]{1,0:T(8,128)S(1)} fusion(bf16[2048,2048]{1,0:T(8,128)(2,1)} %constant_dynamic-update-slice_fusion.20, bf16[2048,1536]{1,0:T(8,128)(2,1)} %all-gather.6.cloned.1.call-done), kind=kOutput, calls=%fused_computation.206 | convolution fusion | flops 12884901888 | bytes 27262976 | tf_op jit(solution)/shard_map/dot_general | solution.py:299
  289.9 7.1 add_multiply_fusion
  303.8 6.9 collective-permute-done.39
  318.6 10.7 %convolution_convert_fusion.6 = bf16[2048,768]{1,0:T(8,128)(2,1)} fusion(bf16[2048,2048]{1,0:T(8,128)(2,1)} %constant_dynamic-update-slice_fusion.10, bf16[2048,768]{1,0:T(8,128)(2,1)S(1)} %get-tuple-element.135), kind=kOutput, calls=%fused_computation.17 | convolution fusion | flops 6444023808 | bytes 14680064 | tf_op jit(solution)/shard_map/dot_general | solution.py:303
  329.2 7.3 %convolution_convert_fusion.4 = bf16[1024,2048]{1,0:T(8,128)(2,1)} fusion(bf16[1024,768]{1,0:T(8,128)(2,1)S(1)} %copy-done.54, bf16[2048,768]{1,0:T(8,128)(2,1)} %all-gather.8.cloned.1.call-done), kind=kOutput, calls=%fused_computation.15 | convolution fusion | flops 3223322624 | bytes 8912896 | tf_op jit(solution)/shard_map/dot_general | solution.py:307
  337.2 13.3 %multiply_convert_fusion.1 = (bf16[2048,768]{1,0:T(8,128)(2,1)S(1)}, bf16[2048,768]{1,0:T(8,128)(2,1)S(1)}) fusion(f32[2048,768]{1,0:T(8,128)} %get-tuple-element.140, f32[2048,768]{1,0:T(8,128)} %get-tuple-element.141, bf16[2048,2048]{1,0:T(8,128)(2,1)} %constant_dynamic-update-slice_fusion.10, bf16[2048,768]{1,0:T(8,128)(2,1)} %all-gather.8.cloned.1.call-done), kind=kOutput, calls=%fused_computation.7 | convolution fusion | flops 6448742400 | bytes 30408704 | tf_op jit(solution)/shard_map/dot_general | solution.py:299
  351.0 9.4 %convert_add_fusion.3 = f32[1024,2048]{1,0:T(8,128)S(1)} fusion(bf16[1024,2048]{1,0:T(8,128)(2,1)} %collective-permute-done.51, bf16[1024,768]{1,0:T(8,128)(2,1)} %get-tuple-element.142, bf16[2048,768]{1,0:T(8,128)(2,1)} %all-gather.8.cloned.1.call-done), kind=kOutput, calls=%fused_computation.3 | convolution fusion | flops 3225419776 | bytes 17301504 | tf_op jit(solution)/shard_map/dot_general | solution.py:307
  369.0 17.7 %convolution_convert_fusion = bf16[2048,1536]{1,0:T(8,128)(2,1)} fusion(bf16[2048,2048]{1,0:T(8,128)(2,1)} %constant_dynamic-update-slice_fusion.20, bf16[2048,1536]{1,0:T(8,128)(2,1)S(1)} %pad_maximum_fusion), kind=kOutput, calls=%fused_computation.4 | convolution fusion | flops 12888047616 | bytes 20971520 | tf_op jit(solution)/shard_map/dot_general | solution.py:303
  390.6 11.1 %convolution_convert_fusion.1 = bf16[1024,2048]{1,0:T(8,128)(2,1)} fusion(bf16[2048,1536]{1,0:T(8,128)(2,1)} %all-gather.6.cloned.1.call-done, bf16[2048,1536]{1,0:T(8,128)(2,1)} %copy-done.41), kind=kOutput, calls=%fused_computation.12 | convolution fusion | flops 6444548096 | bytes 13631488 | tf_op jit(solution)/shard_map/dot_general | solution.py:307
  405.7 12.2 %collective-permute-done.56 = bf16[128,2048]{1,0:T(8,128)(2,1)S(1)} collective-permute-done((bf16[128,2048]{1,0:T(8,128)(2,1)S(1)}, bf16[128,2048]{1,0:T(8,128)(2,1)S(1)}, u32[]{:S(2)}, u32[]{:S(2)}) %collective-permute-start.56) | collective-permute-done | bytes 524320 | tf_op jit(solution)/shard_map/ppermute | solution.py:40
  421.2 9.7 %convert_add_fusion.2 = f32[1024,2048]{1,0:T(8,128)S(1)} fusion(bf16[1024,2048]{1,0:T(8,128)(2,1)} %collective-permute-done.58, bf16[1024,1536]{1,0:T(8,128)(2,1)S(1)} %slice-done.2, bf16[2048,1536]{1,0:T(8,128)(2,1)} %all-gather.6.cloned.1.call-done), kind=kOutput, calls=%fused_computation.2 | convolution fusion | flops 6446645248 | bytes 22020096 | tf_op jit(solution)/shard_map/dot_general | solution.py:307
  435.8 10.8 %collective-permute-done.60 = bf16[128,2048]{1,0:T(8,128)(2,1)S(1)} collective-permute-done((bf16[128,2048]{1,0:T(8,128)(2,1)S(1)}, bf16[128,2048]{1,0:T(8,128)(2,1)S(1)}, u32[]{:S(2)}, u32[]{:S(2)}) %collective-permute-start.60) | collective-permute-done | bytes 524320 | tf_op jit(solution)/shard_map/ppermute | solution.py:40
  449.7 8.9 %collective-permute-done.59 = bf16[128,2048]{1,0:T(8,128)(2,1)S(1)} collective-permute-done((bf16[128,2048]{1,0:T(8,128)(2,1)S(1)}, bf16[128,2048]{1,0:T(8,128)(2,1)S(1)}, u32[]{:S(2)}, u32[]{:S(2)}) %collective-permute-start.59) | collective-permute-done | bytes 524320 | tf_op jit(solution)/shard_map/ppermute | solution.py:40
  458.5 9.4 %collective-permute-done.61 = bf16[128,2048]{1,0:T(8,128)(2,1)S(1)} collective-permute-done((bf16[128,2048]{1,0:T(8,128)(2,1)S(1)}, bf16[128,2048]{1,0:T(8,128)(2,1)S(1)}, u32[]{:S(2)}, u32[]{:S(2)}) %collective-permute-start.61) | collective-permute-done | bytes 524320 | tf_op jit(solution)/shard_map/ppermute | solution.py:40
  474.0 21.5 %collective-permute-done.66 = bf16[256,2048]{1,0:T(8,128)(2,1)S(1)} collective-permute-done((bf16[256,2048]{1,0:T(8,128)(2,1)S(1)}, bf16[256,2048]{1,0:T(8,128)(2,1)S(1)}, u32[]{:S(2)}, u32[]{:S(2)}) %collective-permute-start.66) | collective-permute-done | bytes 1048608 | tf_op jit(solution)/shard_map/ppermute | solution.py:40
  498.8 8.3 %collective-permute-done.67 = bf16[128,2048]{1,0:T(8,128)(2,1)S(1)} collective-permute-done((bf16[128,2048]{1,0:T(8,128)(2,1)S(1)}, bf16[128,2048]{1,0:T(8,128)(2,1)S(1)}, u32[]{:S(2)}, u32[]{:S(2)}) %collective-permute-start.67) | collective-permute-done | bytes 524320 | tf_op jit(solution)/shard_map/ppermute | solution.py:40
  513.5 5.6 convolution_convert_fusion.7
  527.0 33.5 %mixer_backward.1 = (bf16[8,256,768]{2,1,0:T(8,128)(2,1)S(1)}, bf16[192,768]{1,0:T(8,128)(2,1)S(1)}) custom-call(s32[1]{0:T(128)} %bitcast.1.place, f32[8,256,768]{2,1,0:T(8,128)} %get-tuple-element.152.pre.rim, f32[8,256,768]{2,1,0:T(8,128)} %get-tuple-element.152.pre.rim, f32[8,256,128]{2,1,0:T(8,128)S(1)} %copy-done.3, f32[8,256,128]{2,1,0:T(8,128)S(1)} %copy-done.3, ...), custom_call_target="tpu_custom_call" | custom-call | flops 6845104128 | bytes 18874368 | tf_op jit(solution)/shard_map/mixer_backward/pallas_call | solution.py:845
  562.9 11.4 %convolution_convert_fusion.5 = bf16[2048,768]{1,0:T(8,128)(2,1)} fusion(bf16[2048,2048]{1,0:T(8,128)(2,1)} %norm_rows.1, bf16[2048,768]{1,0:T(8,128)(2,1)} %bitcast.242), kind=kOutput, calls=%fused_computation.16 | convolution fusion | flops 6444023808 | bytes 14680064 | tf_op jit(solution)/shard_map/dot_general | solution.py:303
  574.3 7.9 %convolution_convert_fusion.3 = bf16[1024,2048]{1,0:T(8,128)(2,1)} fusion(bf16[2048,1152]{1,0:T(8,128)(2,1)} %all-gather.4.cloned.1.call-done.both_weight.out_weight, bf16[2048,768]{1,0:T(8,128)(2,1)} %bitcast.243), kind=kOutput, calls=%fused_computation.14 | convolution fusion | flops 3223322624 | bytes 8912896 | tf_op jit(solution)/shard_map/dot_general | solution.py:307
  589.6 5.5 collective-permute-done.75
  596.7 5.3 collective-permute-start.84
  602.0 6.4 convert_add_fusion.1
  616.3 4.1 all-to-all-start.1
  624.3 6.1 collective-permute-done.85
  640.8 6.9 reduce-scatter.11.cloned.1.call-done
  647.6 4.2 all-to-all-start.2
  656.5 7.1 collective-permute-done.88.refs_2_
  669.0 6.8 collective-permute-done.87.refs_1_
  675.7 6.2 collective-permute-done.89.refs_3_
  683.0 6.7 fusion.10
  693.4 4.1 gates_owner.1
  699.5 8.5 %copy.42 = f32[2,16,171,171]{3,1,2,0:T(8,128)} copy(f32[2,16,171,171]{3,2,1,0:T(8,128)} %get-tuple-element.204) | data formatting | bytes 7485696
  (480 shorter events, 237.8 us)
Async XLA Ops:
  7.2 124.5 %all-gather.4.cloned.1.call-start = ((), (), s32[]{:S(2)}) async-start(), calls=%async_computation.7 | async-start | bytes 5898240 | tf_op jit(solution)/shard_map/all_gather | solution.py:75
  36.7 206.1 %all-gather.6.cloned.1.call-start = ((), (), s32[]{:S(2)}) async-start(), calls=%async_computation.8 | async-start | bytes 7864320 | tf_op jit(solution)/shard_map/all_gather | solution.py:75
  36.7 25.6 %collective-permute-start.1 = (bf16[256,2048]{1,0:T(8,128)(2,1)}, bf16[256,2048]{1,0:T(8,128)(2,1)}, u32[]{:S(2)}, u32[]{:S(2)}) collective-permute-start(bf16[256,2048]{1,0:T(8,128)(2,1)} %bitcast.258), channel_id=1, source_target_pairs={{0,4},{1,5},{2,6},{3,7},{4,0},{5,1},{6,2},{7,3},{8,12},{9,13},{10,... | collective-permute-start | bytes 3145736 | tf_op jit(solution)/shard_map/ppermute | solution.py:40
  38.3 28.7 %collective-permute-start = (bf16[256,2048]{1,0:T(8,128)(2,1)}, bf16[256,2048]{1,0:T(8,128)(2,1)}, u32[]{:S(2)}, u32[]{:S(2)}) collective-permute-start(bf16[256,2048]{1,0:T(8,128)(2,1)} %bitcast.259), channel_id=1, source_target_pairs={{0,2},{1,3},{2,0},{3,1},{4,6},{5,7},{6,4},{7,5},{8,10},{9,11},{10,... | collective-permute-start | bytes 3145736 | tf_op jit(solution)/shard_map/ppermute | solution.py:40
  38.5 48.1 %collective-permute-start.4 = (bf16[256,2048]{1,0:T(8,128)(2,1)}, bf16[256,2048]{1,0:T(8,128)(2,1)}, u32[]{:S(2)}, u32[]{:S(2)}) collective-permute-start(bf16[256,2048]{1,0:T(8,128)(2,1)} %bitcast.260), channel_id=1, source_target_pairs={{0,1},{1,0},{2,3},{3,2},{4,5},{5,4},{6,7},{7,6},{8,9},{9,8},{10,11... | collective-permute-start | bytes 3145736 | tf_op jit(solution)/shard_map/ppermute | solution.py:40
  45.0 23.4 %collective-permute-start.16 = (f32[8,128]{1,0:T(8,128)}, f32[8,128]{1,0:T(8,128)}, u32[]{:S(2)}, u32[]{:S(2)}) collective-permute-start(f32[8,128]{1,0:T(8,128)} %slice.362), channel_id=1, source_target_pairs={{0,8},{1,9},{2,10},{3,11},{4,12},{5,13},{6,14},{7,15},{8,16},{9,17... | collective-permute-start | bytes 12296 | tf_op jit(solution)/shard_map/ppermute | solution.py:46
  48.0 23.3 %collective-permute-start.17 = (f32[8,128]{1,0:T(8,128)}, f32[8,128]{1,0:T(8,128)S(1)}, u32[]{:S(2)}, u32[]{:S(2)}) collective-permute-start(f32[8,128]{1,0:T(8,128)} %slice.362), channel_id=1, source_target_pairs={{0,16},{1,17},{2,18},{3,19},{4,20},{5,21},{6,22},{7,23},{8,24},{9,... | collective-permute-start | bytes 12296 | tf_op jit(solution)/shard_map/ppermute | solution.py:46
  82.0 35.3 %collective-permute-start.5 = (bf16[256,2048]{1,0:T(8,128)(2,1)}, bf16[256,2048]{1,0:T(8,128)(2,1)S(1)}, u32[]{:S(2)}, u32[]{:S(2)}) collective-permute-start(bf16[256,2048]{1,0:T(8,128)(2,1)} %collective-permute-done), channel_id=1, source_target_pairs={{0,1},{1,0},{2,3},{3,2},{4,5},{5,4},{6,7},{7,6},{8,9},{9,8},{10,11... | collective-permute-start | bytes 3145736 | tf_op jit(solution)/shard_map/ppermute | solution.py:40
  82.5 36.0 %collective-permute-start.6 = (bf16[256,2048]{1,0:T(8,128)(2,1)}, bf16[256,2048]{1,0:T(8,128)(2,1)S(1)}, u32[]{:S(2)}, u32[]{:S(2)}) collective-permute-start(bf16[256,2048]{1,0:T(8,128)(2,1)} %collective-permute-done.1), channel_id=1, source_target_pairs={{0,1},{1,0},{2,3},{3,2},{4,5},{5,4},{6,7},{7,6},{8,9},{9,8},{10,11... | collective-permute-start | bytes 3145736 | tf_op jit(solution)/shard_map/ppermute | solution.py:40
  121.2 208.0 %all-gather.8.cloned.1.call-start = ((), (), s32[]{:S(2)}) async-start(), calls=%async_computation.9 | async-start | bytes 3932160 | tf_op jit(solution)/shard_map/all_gather | solution.py:75
  173.9 24.5 %collective-permute-start.27 = (bf16[128,2048]{1,0:T(8,128)(2,1)}, bf16[128,2048]{1,0:T(8,128)(2,1)S(1)}, u32[]{:S(2)}, u32[]{:S(2)}) collective-permute-start(bf16[128,2048]{1,0:T(8,128)(2,1)} %get-tuple-element.242), channel_id=1, source_target_pairs={{0,4},{1,5},{2,6},{3,7},{4,0},{5,1},{6,2},{7,3},{8,12},{9,13},{10,... | collective-permute-start | bytes 1572872 | tf_op jit(solution)/shard_map/ppermute | solution.py:40
  174.4 24.0 %collective-permute-start.32 = (bf16[128,2048]{1,0:T(8,128)(2,1)}, bf16[128,2048]{1,0:T(8,128)(2,1)S(1)}, u32[]{:S(2)}, u32[]{:S(2)}) collective-permute-start(bf16[128,2048]{1,0:T(8,128)(2,1)} %get-tuple-element.243), channel_id=1, source_target_pairs={{0,2},{1,3},{2,0},{3,1},{4,6},{5,7},{6,4},{7,5},{8,10},{9,11},{10,... | collective-permute-start | bytes 1572872 | tf_op jit(solution)/shard_map/ppermute | solution.py:40
  188.4 20.6 %collective-permute-start.29 = (bf16[128,2048]{1,0:T(8,128)(2,1)}, bf16[128,2048]{1,0:T(8,128)(2,1)S(1)}, u32[]{:S(2)}, u32[]{:S(2)}) collective-permute-start(bf16[128,2048]{1,0:T(8,128)(2,1)} %get-tuple-element.226), channel_id=1, source_target_pairs={{0,4},{1,5},{2,6},{3,7},{4,0},{5,1},{6,2},{7,3},{8,12},{9,13},{10,... | collective-permute-start | bytes 1572872 | tf_op jit(solution)/shard_map/ppermute | solution.py:40
  189.9 19.1 %collective-permute-start.31 = (bf16[128,2048]{1,0:T(8,128)(2,1)}, bf16[128,2048]{1,0:T(8,128)(2,1)S(1)}, u32[]{:S(2)}, u32[]{:S(2)}) collective-permute-start(bf16[128,2048]{1,0:T(8,128)(2,1)} %get-tuple-element.227), channel_id=1, source_target_pairs={{0,2},{1,3},{2,0},{3,1},{4,6},{5,7},{6,4},{7,5},{8,10},{9,11},{10,... | collective-permute-start | bytes 1572872 | tf_op jit(solution)/shard_map/ppermute | solution.py:40
  214.7 28.1 %collective-permute-start.33 = (bf16[256,2048]{1,0:T(8,128)(2,1)}, bf16[256,2048]{1,0:T(8,128)(2,1)S(1)}, u32[]{:S(2)}, u32[]{:S(2)}) collective-permute-start(bf16[256,2048]{1,0:T(8,128)(2,1)} %get-tuple-element.214), channel_id=1, source_target_pairs={{0,4},{1,5},{2,6},{3,7},{4,0},{5,1},{6,2},{7,3},{8,12},{9,13},{10,... | collective-permute-start | bytes 3145736 | tf_op jit(solution)/shard_map/ppermute | solution.py:40
  216.2 26.6 %collective-permute-start.34 = (bf16[256,2048]{1,0:T(8,128)(2,1)}, bf16[256,2048]{1,0:T(8,128)(2,1)}, u32[]{:S(2)}, u32[]{:S(2)}) collective-permute-start(bf16[256,2048]{1,0:T(8,128)(2,1)} %get-tuple-element.214), channel_id=1, source_target_pairs={{0,2},{1,3},{2,0},{3,1},{4,6},{5,7},{6,4},{7,5},{8,10},{9,11},{10,... | collective-permute-start | bytes 3145736 | tf_op jit(solution)/shard_map/ppermute | solution.py:40
  218.0 46.1 %collective-permute-start.46 = (bf16[256,2048]{1,0:T(8,128)(2,1)}, bf16[256,2048]{1,0:T(8,128)(2,1)}, u32[]{:S(2)}, u32[]{:S(2)}) collective-permute-start(bf16[256,2048]{1,0:T(8,128)(2,1)} %get-tuple-element.214), channel_id=1, source_target_pairs={{0,1},{1,0},{2,3},{3,2},{4,5},{5,4},{6,7},{7,6},{8,9},{9,8},{10,11... | collective-permute-start | bytes 3145736 | tf_op jit(solution)/shard_map/ppermute | solution.py:40
  249.6 222.4 %reduce-scatter.5.cloned.1.call-start = ((), (), s32[]{:S(2)}) async-start(), calls=%async_computation.10 | async-start | bytes 3932160 | tf_op jit(solution)/shard_map/reduce_scatter | solution.py:79
  257.8 55.8 %collective-permute-start.41 = (bf16[256,2048]{1,0:T(8,128)(2,1)S(1)}, bf16[256,2048]{1,0:T(8,128)(2,1)S(1)}, u32[]{:S(2)}, u32[]{:S(2)}) collective-permute-start(bf16[256,2048]{1,0:T(8,128)(2,1)S(1)} %bitcast.263), channel_id=1, source_target_pairs={{0,1},{1,0},{2,3},{3,2},{4,5},{5,4},{6,7},{7,6},{8,9},{9,8},{10,11... | collective-permute-start | bytes 3145736 | tf_op jit(solution)/shard_map/ppermute | solution.py:40
  260.8 37.8 %collective-permute-start.37 = (bf16[256,2048]{1,0:T(8,128)(2,1)S(1)}, bf16[256,2048]{1,0:T(8,128)(2,1)S(1)}, u32[]{:S(2)}, u32[]{:S(2)}) collective-permute-start(bf16[256,2048]{1,0:T(8,128)(2,1)S(1)} %bitcast.264), channel_id=1, source_target_pairs={{0,2},{1,3},{2,0},{3,1},{4,6},{5,7},{6,4},{7,5},{8,10},{9,11},{10,... | collective-permute-start | bytes 3145736 | tf_op jit(solution)/shard_map/ppermute | solution.py:40
  268.0 29.0 %collective-permute-start.38 = (bf16[256,2048]{1,0:T(8,128)(2,1)S(1)}, bf16[256,2048]{1,0:T(8,128)(2,1)S(1)}, u32[]{:S(2)}, u32[]{:S(2)}) collective-permute-start(bf16[256,2048]{1,0:T(8,128)(2,1)S(1)} %bitcast.265), channel_id=1, source_target_pairs={{0,4},{1,5},{2,6},{3,7},{4,0},{5,1},{6,2},{7,3},{8,12},{9,13},{10,... | collective-permute-start | bytes 3145736 | tf_op jit(solution)/shard_map/ppermute | solution.py:40
  337.2 182.0 %reduce-scatter.7.cloned.1.call-start = ((), (), s32[]{:S(2)}) async-start(), calls=%async_computation.11 | async-start | bytes 7864320 | tf_op jit(solution)/shard_map/reduce_scatter | solution.py:79
  365.0 21.8 %collective-permute-start.52 = (bf16[128,2048]{1,0:T(8,128)(2,1)}, bf16[128,2048]{1,0:T(8,128)(2,1)S(1)}, u32[]{:S(2)}, u32[]{:S(2)}) collective-permute-start(bf16[128,2048]{1,0:T(8,128)(2,1)} %get-tuple-element.241), channel_id=1, source_target_pairs={{0,4},{1,5},{2,6},{3,7},{4,0},{5,1},{6,2},{7,3},{8,12},{9,13},{10,... | collective-permute-start | bytes 1572872 | tf_op jit(solution)/shard_map/ppermute | solution.py:40
  365.5 21.2 %collective-permute-start.53 = (bf16[128,2048]{1,0:T(8,128)(2,1)}, bf16[128,2048]{1,0:T(8,128)(2,1)S(1)}, u32[]{:S(2)}, u32[]{:S(2)}) collective-permute-start(bf16[128,2048]{1,0:T(8,128)(2,1)} %get-tuple-element.240), channel_id=1, source_target_pairs={{0,2},{1,3},{2,0},{3,1},{4,6},{5,7},{6,4},{7,5},{8,10},{9,11},{10,... | collective-permute-start | bytes 1572872 | tf_op jit(solution)/shard_map/ppermute | solution.py:40
  366.1 24.2 %collective-permute-start.54 = (bf16[128,2048]{1,0:T(8,128)(2,1)S(1)}, bf16[128,2048]{1,0:T(8,128)(2,1)S(1)}, u32[]{:S(2)}, u32[]{:S(2)}) collective-permute-start(bf16[128,2048]{1,0:T(8,128)(2,1)S(1)} %get-tuple-element.239), channel_id=1, source_target_pairs={{0,4},{1,5},{2,6},{3,7},{4,0},{5,1},{6,2},{7,3},{8,12},{9,13},{10,... | collective-permute-start | bytes 1572872 | tf_op jit(solution)/shard_map/ppermute | solution.py:40
  367.5 23.1 %collective-permute-start.55 = (bf16[128,2048]{1,0:T(8,128)(2,1)S(1)}, bf16[128,2048]{1,0:T(8,128)(2,1)S(1)}, u32[]{:S(2)}, u32[]{:S(2)}) collective-permute-start(bf16[128,2048]{1,0:T(8,128)(2,1)S(1)} %get-tuple-element.238), channel_id=1, source_target_pairs={{0,2},{1,3},{2,0},{3,1},{4,6},{5,7},{6,4},{7,5},{8,10},{9,11},{10,... | collective-permute-start | bytes 1572872 | tf_op jit(solution)/shard_map/ppermute | solution.py:40
  401.6 19.5 %collective-permute-start.58 = (bf16[1024,2048]{1,0:T(8,128)(2,1)}, bf16[1024,2048]{1,0:T(8,128)(2,1)}, u32[]{:S(2)}, u32[]{:S(2)}) collective-permute-start(bf16[1024,2048]{1,0:T(8,128)(2,1)} %convolution_convert_fusion.1), channel_id=1, source_target_pairs={{0,1},{1,0},{2,3},{3,2},{4,5},{5,4},{6,7},{7,6},{8,9},{9,8},{10,11... | collective-permute-start | bytes 12582920 | tf_op jit(solution)/shard_map/ppermute | solution.py:40
  401.7 161.2 %reduce-scatter.9.cloned.1.call-start = ((), (), s32[]{:S(2)}) async-start(), calls=%async_computation.12 | async-start | bytes 1966080 | tf_op jit(solution)/shard_map/reduce_scatter | solution.py:79
  433.0 25.5 %collective-permute-start.59 = (bf16[128,2048]{1,0:T(8,128)(2,1)S(1)}, bf16[128,2048]{1,0:T(8,128)(2,1)S(1)}, u32[]{:S(2)}, u32[]{:S(2)}) collective-permute-start(bf16[128,2048]{1,0:T(8,128)(2,1)S(1)} %get-tuple-element.234), channel_id=1, source_target_pairs={{0,4},{1,5},{2,6},{3,7},{4,0},{5,1},{6,2},{7,3},{8,12},{9,13},{10,... | collective-permute-start | bytes 1572872 | tf_op jit(solution)/shard_map/ppermute | solution.py:40
  434.4 24.1 %collective-permute-start.64 = (bf16[128,2048]{1,0:T(8,128)(2,1)S(1)}, bf16[128,2048]{1,0:T(8,128)(2,1)S(1)}, u32[]{:S(2)}, u32[]{:S(2)}) collective-permute-start(bf16[128,2048]{1,0:T(8,128)(2,1)S(1)} %get-tuple-element.235), channel_id=1, source_target_pairs={{0,2},{1,3},{2,0},{3,1},{4,6},{5,7},{6,4},{7,5},{8,10},{9,11},{10,... | collective-permute-start | bytes 1572872 | tf_op jit(solution)/shard_map/ppermute | solution.py:40
  447.6 20.3 %collective-permute-start.61 = (bf16[128,2048]{1,0:T(8,128)(2,1)S(1)}, bf16[128,2048]{1,0:T(8,128)(2,1)S(1)}, u32[]{:S(2)}, u32[]{:S(2)}) collective-permute-start(bf16[128,2048]{1,0:T(8,128)(2,1)S(1)} %get-tuple-element.222), channel_id=1, source_target_pairs={{0,4},{1,5},{2,6},{3,7},{4,0},{5,1},{6,2},{7,3},{8,12},{9,13},{10,... | collective-permute-start | bytes 1572872 | tf_op jit(solution)/shard_map/ppermute | solution.py:40
  448.3 19.7 %collective-permute-start.63 = (bf16[128,2048]{1,0:T(8,128)(2,1)S(1)}, bf16[128,2048]{1,0:T(8,128)(2,1)S(1)}, u32[]{:S(2)}, u32[]{:S(2)}) collective-permute-start(bf16[128,2048]{1,0:T(8,128)(2,1)S(1)} %get-tuple-element.223), channel_id=1, source_target_pairs={{0,2},{1,3},{2,0},{3,1},{4,6},{5,7},{6,4},{7,5},{8,10},{9,11},{10,... | collective-permute-start | bytes 1572872 | tf_op jit(solution)/shard_map/ppermute | solution.py:40
  472.0 23.5 %collective-permute-start.66 = (bf16[256,2048]{1,0:T(8,128)(2,1)S(1)}, bf16[256,2048]{1,0:T(8,128)(2,1)S(1)}, u32[]{:S(2)}, u32[]{:S(2)}) collective-permute-start(bf16[256,2048]{1,0:T(8,128)(2,1)S(1)} %get-tuple-element.154), channel_id=1, source_target_pairs={{0,4},{1,5},{2,6},{3,7},{4,0},{5,1},{6,2},{7,3},{8,12},{9,13},{10,... | collective-permute-start | bytes 3145736 | tf_op jit(solution)/shard_map/ppermute | solution.py:40
  472.6 24.3 %collective-permute-start.65 = (bf16[256,2048]{1,0:T(8,128)(2,1)S(1)}, bf16[256,2048]{1,0:T(8,128)(2,1)S(1)}, u32[]{:S(2)}, u32[]{:S(2)}) collective-permute-start(bf16[256,2048]{1,0:T(8,128)(2,1)S(1)} %get-tuple-element.154), channel_id=1, source_target_pairs={{0,2},{1,3},{2,0},{3,1},{4,6},{5,7},{6,4},{7,5},{8,10},{9,11},{10,... | collective-permute-start | bytes 3145736 | tf_op jit(solution)/shard_map/ppermute | solution.py:40
  474.0 34.4 %collective-permute-start.69 = (bf16[256,2048]{1,0:T(8,128)(2,1)S(1)}, bf16[256,2048]{1,0:T(8,128)(2,1)S(1)}, u32[]{:S(2)}, u32[]{:S(2)}) collective-permute-start(bf16[256,2048]{1,0:T(8,128)(2,1)S(1)} %get-tuple-element.154), channel_id=1, source_target_pairs={{0,1},{1,0},{2,3},{3,2},{4,5},{5,4},{6,7},{7,6},{8,9},{9,8},{10,11... | collective-permute-start | bytes 3145736 | tf_op jit(solution)/shard_map/ppermute | solution.py:40
  522.2 40.7 %all-to-all-start = ((bf16[8,64,2304]{2,1,0:T(8,128)(2,1)}), bf16[8,64,2304]{2,1,0:T(8,128)(2,1)S(1)}, u32[]{:S(2)}, u32[]{:S(2)}) async-start(bf16[8,64,2304]{2,1,0:T(8,128)(2,1)} %bitcast.262), calls=%async_computation.3 | async-start | bytes 4718592 | tf_op jit(solution)/shard_map/all_to_all | solution.py:102
  525.8 121.8 %reduce-scatter.11.cloned.1.call-start = ((), (), s32[]{:S(2)}) async-start(), calls=%async_computation.13 | async-start | bytes 3932160 | tf_op jit(solution)/shard_map/reduce_scatter | solution.py:79
  582.1 19.8 %collective-permute-start.77 = (bf16[1024,2048]{1,0:T(8,128)(2,1)}, bf16[1024,2048]{1,0:T(8,128)(2,1)}, u32[]{:S(2)}, u32[]{:S(2)}) collective-permute-start(bf16[1024,2048]{1,0:T(8,128)(2,1)} %convolution_convert_fusion.3), channel_id=1, source_target_pairs={{0,1},{1,0},{2,3},{3,2},{4,5},{5,4},{6,7},{7,6},{8,9},{9,8},{10,11... | collective-permute-start | bytes 12582920 | tf_op jit(solution)/shard_map/ppermute | solution.py:40
  596.7 26.2 %collective-permute-start.84 = (bf16[48,768]{1,0:T(8,128)(2,1)S(1)}, bf16[48,768]{1,0:T(8,128)(2,1)S(1)}, u32[]{:S(2)}, u32[]{:S(2)}) collective-permute-start(bf16[48,768]{1,0:T(8,128)(2,1)S(1)} %fusion.56), channel_id=1, source_target_pairs={{0,8},{1,9},{2,10},{3,11},{4,12},{5,13},{6,14},{7,15},{8,16},{9,17... | collective-permute-start | bytes 221192 | tf_op jit(solution)/shard_map/ppermute | solution.py:46
  613.0 21.4 %collective-permute-start.79 = (bf16[128,2048]{1,0:T(8,128)(2,1)}, bf16[128,2048]{1,0:T(8,128)(2,1)}, u32[]{:S(2)}, u32[]{:S(2)}) collective-permute-start(bf16[128,2048]{1,0:T(8,128)(2,1)} %get-tuple-element.232), channel_id=1, source_target_pairs={{0,2},{1,3},{2,0},{3,1},{4,6},{5,7},{6,4},{7,5},{8,10},{9,11},{10,... | collective-permute-start | bytes 1572872 | tf_op jit(solution)/shard_map/ppermute | solution.py:40
  614.8 19.6 %collective-permute-start.81 = (bf16[128,2048]{1,0:T(8,128)(2,1)}, bf16[128,2048]{1,0:T(8,128)(2,1)}, u32[]{:S(2)}, u32[]{:S(2)}) collective-permute-start(bf16[128,2048]{1,0:T(8,128)(2,1)} %get-tuple-element.230), channel_id=1, source_target_pairs={{0,4},{1,5},{2,6},{3,7},{4,0},{5,1},{6,2},{7,3},{8,12},{9,13},{10,... | collective-permute-start | bytes 1572872 | tf_op jit(solution)/shard_map/ppermute | solution.py:40
  616.3 22.5 %all-to-all-start.1 = ((bf16[8,64,384]{2,1,0:T(8,128)(2,1)}), bf16[8,64,384]{2,1,0:T(8,128)(2,1)}, u32[]{:S(2)}, u32[]{:S(2)}) async-start(bf16[8,64,384]{2,1,0:T(8,128)(2,1)} %bitcast.277), calls=%async_computation.4 | async-start | bytes 786432 | tf_op jit(solution)/shard_map/all_to_all | solution.py:102
  631.0 34.6 %collective-permute-start.78 = (bf16[128,2048]{1,0:T(8,128)(2,1)}, bf16[128,2048]{1,0:T(8,128)(2,1)}, u32[]{:S(2)}, u32[]{:S(2)}) collective-permute-start(bf16[128,2048]{1,0:T(8,128)(2,1)} %get-tuple-element.233), channel_id=1, source_target_pairs={{0,4},{1,5},{2,6},{3,7},{4,0},{5,1},{6,2},{7,3},{8,12},{9,13},{10,... | collective-permute-start | bytes 1572872 | tf_op jit(solution)/shard_map/ppermute | solution.py:40
  632.9 32.7 %collective-permute-start.83 = (bf16[128,2048]{1,0:T(8,128)(2,1)}, bf16[128,2048]{1,0:T(8,128)(2,1)}, u32[]{:S(2)}, u32[]{:S(2)}) collective-permute-start(bf16[128,2048]{1,0:T(8,128)(2,1)} %get-tuple-element.231), channel_id=1, source_target_pairs={{0,2},{1,3},{2,0},{3,1},{4,6},{5,7},{6,4},{7,5},{8,10},{9,11},{10,... | collective-permute-start | bytes 1572872 | tf_op jit(solution)/shard_map/ppermute | solution.py:40
  637.6 28.1 %collective-permute-start.80 = (bf16[128,2048]{1,0:T(8,128)(2,1)}, bf16[128,2048]{1,0:T(8,128)(2,1)}, u32[]{:S(2)}, u32[]{:S(2)}) collective-permute-start(bf16[128,2048]{1,0:T(8,128)(2,1)} %get-tuple-element.221), channel_id=1, source_target_pairs={{0,4},{1,5},{2,6},{3,7},{4,0},{5,1},{6,2},{7,3},{8,12},{9,13},{10,... | collective-permute-start | bytes 1572872 | tf_op jit(solution)/shard_map/ppermute | solution.py:40
  638.1 27.6 %collective-permute-start.82 = (bf16[128,2048]{1,0:T(8,128)(2,1)}, bf16[128,2048]{1,0:T(8,128)(2,1)}, u32[]{:S(2)}, u32[]{:S(2)}) collective-permute-start(bf16[128,2048]{1,0:T(8,128)(2,1)} %get-tuple-element.220), channel_id=1, source_target_pairs={{0,2},{1,3},{2,0},{3,1},{4,6},{5,7},{6,4},{7,5},{8,10},{9,11},{10,... | collective-permute-start | bytes 1572872 | tf_op jit(solution)/shard_map/ppermute | solution.py:40
  638.8 24.8 %collective-permute-start.88 = (bf16[192,768]{1,0:T(8,128)(2,1)}, bf16[192,768]{1,0:T(8,128)(2,1)}, u32[]{:S(2)}, u32[]{:S(2)}) collective-permute-start(bf16[192,768]{1,0:T(8,128)(2,1)} %bitcast.81.refs_0_), channel_id=1, source_target_pairs={{0,4},{1,5},{2,6},{3,7},{4,0},{5,1},{6,2},{7,3},{8,12},{9,13},{10,... | collective-permute-start | bytes 884744 | tf_op jit(solution)/shard_map/ppermute | solution.py:40
  647.6 34.3 %all-to-all-start.2 = ((bf16[8,64,768]{2,1,0:T(8,128)(2,1)}), bf16[8,64,768]{2,1,0:T(8,128)(2,1)}, u32[]{:S(2)}, u32[]{:S(2)}) async-start(bf16[8,64,768]{2,1,0:T(8,128)(2,1)} %bitcast.275), calls=%async_computation.6 | async-start | bytes 1572864 | tf_op jit(solution)/shard_map/all_to_all | solution.py:102
  (131 other events, 2064.7 us)
Sparse Core Ops, SparseCore 0:
  36.8 89.9 all-gather.3
  129.0 113.7 all-gather.5
  249.7 59.9 all-gather.7
  337.3 56.6 reduce-scatter.4
  401.8 108.2 reduce-scatter.6
  519.2 32.8 reduce-scatter.8
  582.7 64.9 reduce-scatter.10

commit v4 on v3

--- a/solution.py
+++ b/solution.py
@@ -137,11 +137,16 @@
     )
 
 
-def join_totals(total, arrived):
+def rest_totals(total, arrived):
     first, second, across, along = arrived
     half = total.shape[1] // 2
-    across_rest = swap(low(total[2, half:] + wide(second)), 4)
-    along_rest = swap(low(total[1, :half] + wide(first)), 2)
+    return low(total[2, half:] + wide(second)), low(total[1, :half] + wide(first))
+
+
+def join_totals(total, arrived, rest=None):
+    first, second, across, along = arrived
+    across_rest, along_rest = rest or rest_totals(total, arrived)
+    across_rest, along_rest = swap(across_rest, 4), swap(along_rest, 2)
     return (
         total[0]
         + wide(jnp.concatenate([across, across_rest], axis=0))
@@ -613,7 +618,11 @@
             jax.ShapeDtypeStruct((blocks, steps, channels), BF16),
         ],
         compiler_params=params,
-        cost_estimate=pl.CostEstimate(flops=1, bytes_accessed=1, transcendentals=0),
+        cost_estimate=pl.CostEstimate(
+            flops=blocks * steps * channels * (channels * 4 + model * 4),
+            bytes_accessed=blocks * steps * channels * 14,
+            transcendentals=blocks * steps * channels * 6,
+        ),
         name="mixer_forward",
     )
 
@@ -754,7 +763,8 @@
     inputs = wide(stream_in).reshape(steps, model_width)
     inputs_scale = rms_scale(inputs)
     parts = group_parts(stream_in.reshape(steps, model_width))
-    normed = norm_rows(jnp.concatenate(parts, axis=0), mixer_scale, steps)
+    raw = jnp.concatenate(parts, axis=0)
+    normed = norm_rows(raw, mixer_scale, steps)
     upstream = wide(out_grad).reshape(steps, model_width)
     hidden_parts = simple_call(
         split_hidden_kernel,
@@ -767,7 +777,12 @@
         collect_kernel,
         "collect_hidden",
         where,
-        all_swapped(lax.optimization_barrier((hidden_parts, parts[3:5]))[0]),
+        lax.optimization_barrier(
+            (
+                all_swapped(lax.optimization_barrier((hidden_parts, parts[3:5]))[0]),
+                (raw, mixer_scale),
+            )
+        )[0],
         [((GROUP, own_rows, 2 * hidden_part), BF16), ((GROUP, own_rows, hidden_part), BF16)],
     )
     pair_weight = ring_gather(pair_rows.reshape(-1, 2 * hidden_part))
@@ -791,20 +806,21 @@
         axis=0,
     )
     mixer_forward, mixer_backward = mixer_calls(rows, shards, steps, WIDE, model_width)
+    own = after(out_grad.reshape(steps, model_width), normed)
+    swapped = first_swaps(own)
     pre, state, mixed = mixer_forward(
         where, normed_blocks, segments, mixer_weight, gate_weight, bias, params
     )
-    mixed = mixed.reshape(tokens, WIDE)
+    mixed, swapped = lax.optimization_barrier((mixed.reshape(tokens, WIDE), swapped))
+    upstream_parts = group_parts(own, swapped)
     last_weight = ring_gather(after(last_rows, mixed).reshape(-1, hidden_part))
     middle = inputs + group_total(pair_product(mixed, out_weight))
 
     middle_scale = rms_scale(middle)
     own = low(middle * middle_scale * hidden_scale)
     parts = group_parts(own, lax.optimization_barrier((first_swaps(own), pair_weight))[0])
-    own = out_grad.reshape(steps, model_width)
-    swapped = first_swaps(lax.optimization_barrier((own, parts[3:5]))[0])
     normed_mid = jnp.concatenate(parts, axis=0)
-    upstream_all = jnp.concatenate(group_parts(own, swapped), axis=0)
+    upstream_all = jnp.concatenate(upstream_parts, axis=0)
     pair = product(normed_mid, pair_weight)
     gate_pre, linear_pre = pair[:, :hidden_part], pair[:, hidden_part:]
     value, slope = gelu_both(gate_pre)
@@ -824,9 +840,12 @@
     hidden_sent = send_totals(hidden_out)
     grad_pair_low = low(contract_rows(normed_mid, after(d_pair, hidden_out)))
     grad_pair = ring_reduce(grad_pair_low)
-    d_pair, hidden_sent = lax.optimization_barrier((after(d_pair, grad_pair_low), hidden_sent))
+    hidden_rest = rest_totals(hidden_out, hidden_sent)
+    d_pair, hidden_rest, hidden_sent = lax.optimization_barrier(
+        (after(d_pair, grad_pair_low), hidden_rest, hidden_sent)
+    )
     d_normed_mid, hidden_out = pair_product(
-        d_pair, pair_weight, join_totals(hidden_out, hidden_sent)
+        d_pair, pair_weight, join_totals(hidden_out, hidden_sent, hidden_rest)
     )
     result = low(middle + hidden_out)
     d_middle = upstream + norm_back(

time: 722 us -> 704 us (0.975)
  waiting for transfers between devices: 248 us -> 223 us
  local copies, waits for them, and re-layouts: 88.2 us -> 98.9 us
    all_gather x3, waiting for transfers between devices: 24.8 us -> 0.02 us  [ring_gather(): lax.all_gather(block, AXES, axis=0, tiled=True, axis_index_groups=ring_gr...]
    unnamed x188 -> x192, local copies, waits for them, and re-layouts: 63 us -> 74.7 us
  transfers between devices with their start and end apart: 104 -> 104, of which waited for: 41 -> 44; matrix products, arithmetic and copies ran while one was open for 29% -> 31% of each run, Pallas kernels for 11% -> 11%
where the time goes in v4:
time: 704 us; the launch traced here: 697 us
  waiting for transfers between devices  223 us (32%)
  matrix products  134 us (19%)
  local copies, waits for them, and re-layouts  98.9 us (14%)
  starting transfers between devices  97.5 us (14%)
  Pallas kernels  81.5 us (12%)
  other arithmetic  46.4 us (7%)
  between operations  15.8 us (2%)
    ppermute x85, waiting for transfers between devices, swap(): lax.ppermute(values, AXES, [(i, i ^ bit) for i in range(device_count())])  197 us
    unnamed x192, local copies, waits for them, and re-layouts  74.7 us
    ppermute x85, starting transfers between devices, swap(): lax.ppermute(values, AXES, [(i, i ^ bit) for i in range(device_count())])  67.5 us
    dot_general x8, matrix products, contract_cols(): lax.dot_general(left, right, (((1,), (1,)), ((), ())), preferred_element_...  59.5 us
    dot_general x4, matrix products, contract_rows(): lax.dot_general(left, right, (((0,), (0,)), ((), ())), preferred_element_...  45.2 us
    pallas_call x1, Pallas kernels, local(): mixer_backward(where, pre, pre, segments, segments, state, state, middle_...  33.5 us
    dot_general x2, matrix products, product(): return jnp.dot(left, right, preferred_element_type=F32)  29.1 us
    pallas_call x1, Pallas kernels, local(): mixer_forward(where, normed_blocks, segments, mixer_weight, gate_weight,...  26 us
  transfers between devices with their start and end apart: 104, of which 44 were waited for; matrix products, arithmetic and copies ran while one was open for 31% of the time, Pallas kernels for 11%

profile of v4, /device:TPU:0, one launch (start us, length us, event | category | flops | bytes accessed | tf_op | source)
XLA Modules:
  0.0 696.8 jit_solution(10171888745059024415)
XLA Ops:
  26.0 5.7 collective-permute-done.14.refs_6_
  31.6 3.9 collective-permute-done.15.refs_7_
  53.5 8.8 %collective-permute-done.1 = bf16[256,2048]{1,0:T(8,128)(2,1)} collective-permute-done((bf16[256,2048]{1,0:T(8,128)(2,1)}, bf16[256,2048]{1,0:T(8,128)(2,1)}, u32[]{:S(2)}, u32[]{:S(2)}) %collective-permute-start.1) | collective-permute-done | bytes 1048608 | tf_op jit(solution)/shard_map/ppermute | solution.py:40
  73.3 4.3 collective-permute-done.2
  92.0 4.2 collective-permute-done.20.refs_2_
  101.8 3.9 collective-permute-done.23.refs_5_
  105.7 8.5 %collective-permute-done.24.refs_6_ = bf16[64,2304]{1,0:T(8,128)(2,1)S(1)} collective-permute-done((bf16[64,2304]{1,0:T(8,128)(2,1)S(1)}, bf16[64,2304]{1,0:T(8,128)(2,1)S(1)}, u32[]{:S(2)}, u32[]{:S(2)}) %collective-permute-start.24) | collective-permute-done | bytes 294944 | tf_op jit(solution)/shard_map/ppermute | solution.py:40
  114.1 5.2 collective-permute-done.25.refs_7_
  122.2 10.2 %norm_rows.1 = bf16[2048,2048]{1,0:T(8,128)(2,1)} custom-call(bf16[2048,2048]{1,0:T(8,128)(2,1)} %constant_dynamic-update-slice_fusion.values, f32[1,2048]{1,0:T(1,128)S(1)} %reshape.460.gain), custom_call_target="tpu_custom_call" | custom-call | flops 1 | bytes 1 | tf_op jit(solution)/shard_map/norm_rows/pallas_call | solution.py:177
  135.6 26.0 %mixer_forward.1 = (f32[8,256,768]{2,1,0:T(8,128)}, f32[8,256,384]{2,1,0:T(8,128)}, bf16[8,256,384]{2,1,0:T(8,128)(2,1)S(1)}) custom-call(s32[1]{0:T(128)} %bitcast.1.place, bf16[8,256,2048]{2,1,0:T(8,128)(2,1)} %bitcast.252, f32[8,256,128]{2,1,0:T(8,128)S(1)} %broadcast_in_dim.71.segment.segment_rim, ...), custom_call_target="tpu_custom_call" | custom-call | flops 7650410496 | bytes 11010048 | tf_op jit(solution)/shard_map/mixer_forward/pallas_call | solution.py:811
  161.7 4.3 convolution_convert_fusion.2
  166.3 7.0 %collective-permute-done.28 = bf16[1024,2048]{1,0:T(8,128)(2,1)S(1)} collective-permute-done((bf16[1024,2048]{1,0:T(8,128)(2,1)S(1)}, bf16[1024,2048]{1,0:T(8,128)(2,1)S(1)}, u32[]{:S(2)}, u32[]{:S(2)}) %collective-permute-start.28) | collective-permute-done | bytes 4194336 | tf_op jit(solution)/shard_map/ppermute | solution.py:40
  192.5 4.5 collective-permute-done.30
  211.8 7.7 %collective-permute-done.34 = bf16[128,2048]{1,0:T(8,128)(2,1)S(1)} collective-permute-done((bf16[128,2048]{1,0:T(8,128)(2,1)}, bf16[128,2048]{1,0:T(8,128)(2,1)S(1)}, u32[]{:S(2)}, u32[]{:S(2)}) %collective-permute-start.34) | collective-permute-done | bytes 524320 | tf_op jit(solution)/shard_map/ppermute | solution.py:40
  221.0 9.1 %collective-permute-done.33 = bf16[128,2048]{1,0:T(8,128)(2,1)S(1)} collective-permute-done((bf16[128,2048]{1,0:T(8,128)(2,1)}, bf16[128,2048]{1,0:T(8,128)(2,1)S(1)}, u32[]{:S(2)}, u32[]{:S(2)}) %collective-permute-start.33) | collective-permute-done | bytes 524320 | tf_op jit(solution)/shard_map/ppermute | solution.py:40
  243.3 15.9 %collective-permute-done.42 = bf16[256,2048]{1,0:T(8,128)(2,1)S(1)} collective-permute-done((bf16[256,2048]{1,0:T(8,128)(2,1)}, bf16[256,2048]{1,0:T(8,128)(2,1)S(1)}, u32[]{:S(2)}, u32[]{:S(2)}) %collective-permute-start.42) | collective-permute-done | bytes 1048608 | tf_op jit(solution)/shard_map/ppermute | solution.py:40
  267.4 4.8 collective-permute-done.44
  280.2 15.7 %fusion.74 = f32[2048,1536]{1,0:T(8,128)S(1)} fusion(bf16[2048,2048]{1,0:T(8,128)(2,1)} %constant_dynamic-update-slice_fusion.20, bf16[2048,1536]{1,0:T(8,128)(2,1)S(1)} %bitcast.269), kind=kOutput, calls=%fused_computation.205 | convolution fusion | flops 12884901888 | bytes 27262976 | tf_op jit(solution)/shard_map/dot_general | solution.py:304
  296.0 7.1 %add_multiply_fusion = (f32[2048,768]{1,0:T(8,128)}, bf16[2048,768]{1,0:T(8,128)(2,1)S(1)}, f32[2048,768]{1,0:T(8,128)}) fusion(f32[2048,1536]{1,0:T(8,128)S(1)} %fusion.74), kind=kLoop, calls=%fused_computation.8 | loop fusion | flops 31457280 | bytes 28311552 | tf_op jit(solution)/shard_map/mul | solution.py:828
  304.4 10.5 %convolution_convert_fusion.6 = bf16[2048,768]{1,0:T(8,128)(2,1)} fusion(bf16[2048,2048]{1,0:T(8,128)(2,1)} %constant_dynamic-update-slice_fusion.10, bf16[2048,768]{1,0:T(8,128)(2,1)S(1)} %get-tuple-element.157), kind=kOutput, calls=%fused_computation.17 | convolution fusion | flops 6444023808 | bytes 14680064 | tf_op jit(solution)/shard_map/dot_general | solution.py:308
  315.0 6.9 convolution_convert_fusion.4
  322.4 13.3 %multiply_convert_fusion.1 = (bf16[2048,768]{1,0:T(8,128)(2,1)S(1)}, bf16[2048,768]{1,0:T(8,128)(2,1)S(1)}) fusion(f32[2048,768]{1,0:T(8,128)} %get-tuple-element.162, f32[2048,768]{1,0:T(8,128)} %get-tuple-element.163, bf16[2048,2048]{1,0:T(8,128)(2,1)} %constant_dynamic-update-slice_fusion.10, bf16[2048,768]{1,0:T(8,128)(2,1)} %all-gather.8.cloned.1.call-done), kind=kOutput, calls=%fused_computation.7 | convolution fusion | flops 6448742400 | bytes 30408704 | tf_op jit(solution)/shard_map/dot_general | solution.py:304
  336.3 9.4 %convert_add_fusion.2 = f32[1024,2048]{1,0:T(8,128)S(1)} fusion(bf16[1024,2048]{1,0:T(8,128)(2,1)} %collective-permute-done.51, bf16[1024,768]{1,0:T(8,128)(2,1)} %get-tuple-element.164, bf16[2048,768]{1,0:T(8,128)(2,1)} %all-gather.8.cloned.1.call-done), kind=kOutput, calls=%fused_computation.2 | convolution fusion | flops 3225419776 | bytes 17301504 | tf_op jit(solution)/shard_map/dot_general | solution.py:312
  354.0 17.7 %convolution_convert_fusion = bf16[2048,1536]{1,0:T(8,128)(2,1)} fusion(bf16[2048,2048]{1,0:T(8,128)(2,1)} %constant_dynamic-update-slice_fusion.20, bf16[2048,1536]{1,0:T(8,128)(2,1)S(1)} %pad_maximum_fusion), kind=kOutput, calls=%fused_computation.4 | convolution fusion | flops 12888047616 | bytes 20971520 | tf_op jit(solution)/shard_map/dot_general | solution.py:308
  375.2 11.1 %convolution_convert_fusion.1 = bf16[1024,2048]{1,0:T(8,128)(2,1)} fusion(bf16[2048,1536]{1,0:T(8,128)(2,1)} %all-gather.6.cloned.1.call-done, bf16[2048,1536]{1,0:T(8,128)(2,1)} %copy-done.47), kind=kOutput, calls=%fused_computation.12 | convolution fusion | flops 6444548096 | bytes 13631488 | tf_op jit(solution)/shard_map/dot_general | solution.py:312
  388.8 11.9 %collective-permute-done.56 = bf16[128,2048]{1,0:T(8,128)(2,1)S(1)} collective-permute-done((bf16[128,2048]{1,0:T(8,128)(2,1)S(1)}, bf16[128,2048]{1,0:T(8,128)(2,1)S(1)}, u32[]{:S(2)}, u32[]{:S(2)}) %collective-permute-start.56) | collective-permute-done | bytes 524320 | tf_op jit(solution)/shard_map/ppermute | solution.py:40
  403.6 9.8 %convert_add_fusion.1 = f32[1024,2048]{1,0:T(8,128)S(1)} fusion(bf16[1024,2048]{1,0:T(8,128)(2,1)} %collective-permute-done.58, bf16[1024,1536]{1,0:T(8,128)(2,1)S(1)} %slice-done, bf16[2048,1536]{1,0:T(8,128)(2,1)} %all-gather.6.cloned.1.call-done), kind=kOutput, calls=%fused_computation.1 | convolution fusion | flops 6446645248 | bytes 22020096 | tf_op jit(solution)/shard_map/dot_general | solution.py:312
  418.3 10.8 %collective-permute-done.60 = bf16[128,2048]{1,0:T(8,128)(2,1)S(1)} collective-permute-done((bf16[128,2048]{1,0:T(8,128)(2,1)S(1)}, bf16[128,2048]{1,0:T(8,128)(2,1)S(1)}, u32[]{:S(2)}, u32[]{:S(2)}) %collective-permute-start.60) | collective-permute-done | bytes 524320 | tf_op jit(solution)/shard_map/ppermute | solution.py:40
  432.5 9.3 %collective-permute-done.59 = bf16[128,2048]{1,0:T(8,128)(2,1)S(1)} collective-permute-done((bf16[128,2048]{1,0:T(8,128)(2,1)S(1)}, bf16[128,2048]{1,0:T(8,128)(2,1)S(1)}, u32[]{:S(2)}, u32[]{:S(2)}) %collective-permute-start.59) | collective-permute-done | bytes 524320 | tf_op jit(solution)/shard_map/ppermute | solution.py:40
  441.8 9.4 %collective-permute-done.61 = bf16[128,2048]{1,0:T(8,128)(2,1)S(1)} collective-permute-done((bf16[128,2048]{1,0:T(8,128)(2,1)S(1)}, bf16[128,2048]{1,0:T(8,128)(2,1)S(1)}, u32[]{:S(2)}, u32[]{:S(2)}) %collective-permute-start.61) | collective-permute-done | bytes 524320 | tf_op jit(solution)/shard_map/ppermute | solution.py:40
  452.1 4.0 fusion.12
  457.7 21.9 %collective-permute-done.66 = bf16[256,2048]{1,0:T(8,128)(2,1)S(1)} collective-permute-done((bf16[256,2048]{1,0:T(8,128)(2,1)S(1)}, bf16[256,2048]{1,0:T(8,128)(2,1)S(1)}, u32[]{:S(2)}, u32[]{:S(2)}) %collective-permute-start.66) | collective-permute-done | bytes 1048608 | tf_op jit(solution)/shard_map/ppermute | solution.py:40
  482.9 8.6 %collective-permute-done.67 = bf16[128,2048]{1,0:T(8,128)(2,1)S(1)} collective-permute-done((bf16[128,2048]{1,0:T(8,128)(2,1)S(1)}, bf16[128,2048]{1,0:T(8,128)(2,1)S(1)}, u32[]{:S(2)}, u32[]{:S(2)}) %collective-permute-start.67) | collective-permute-done | bytes 524320 | tf_op jit(solution)/shard_map/ppermute | solution.py:40
  497.5 5.6 convolution_convert_fusion.7
  511.1 33.5 %mixer_backward.1 = (bf16[8,256,768]{2,1,0:T(8,128)(2,1)S(1)}, bf16[192,768]{1,0:T(8,128)(2,1)S(1)}) custom-call(s32[1]{0:T(128)} %bitcast.1.place, f32[8,256,768]{2,1,0:T(8,128)} %get-tuple-element.174.pre.rim, f32[8,256,768]{2,1,0:T(8,128)} %get-tuple-element.174.pre.rim, f32[8,256,128]{2,1,0:T(8,128)S(1)} %copy-done.3, f32[8,256,128]{2,1,0:T(8,128)S(1)} %copy-done.3, ...), custom_call_target="tpu_custom_call" | custom-call | flops 6845104128 | bytes 18874368 | tf_op jit(solution)/shard_map/mixer_backward/pallas_call | solution.py:864
  546.9 11.4 %convolution_convert_fusion.5 = bf16[2048,768]{1,0:T(8,128)(2,1)} fusion(bf16[2048,2048]{1,0:T(8,128)(2,1)} %norm_rows.1, bf16[2048,768]{1,0:T(8,128)(2,1)} %bitcast.232), kind=kOutput, calls=%fused_computation.16 | convolution fusion | flops 6444023808 | bytes 14680064 | tf_op jit(solution)/shard_map/dot_general | solution.py:308
  558.3 7.9 %convolution_convert_fusion.3 = bf16[1024,2048]{1,0:T(8,128)(2,1)} fusion(bf16[2048,1152]{1,0:T(8,128)(2,1)} %all-gather.4.cloned.1.call-done.both_weight.out_weight, bf16[2048,768]{1,0:T(8,128)(2,1)} %bitcast.233), kind=kOutput, calls=%fused_computation.14 | convolution fusion | flops 3223322624 | bytes 8912896 | tf_op jit(solution)/shard_map/dot_general | solution.py:312
  578.1 4.3 collective-permute-start.84
  582.4 6.4 convert_add_fusion
  597.2 4.1 all-to-all-start.1
  605.2 6.7 collective-permute-done.85
  621.9 11.0 %reduce-scatter.11.cloned.1.call-done = bf16[512,768]{1,0:T(8,128)(2,1)} async-done(((bf16[2048,768]{1,0:T(8,128)(2,1)}), bf16[512,768]{1,0:T(8,128)(2,1)}) %reduce-scatter.11.cloned.1.call-update) | async-done | bytes 786448 | tf_op jit(solution)/shard_map/reduce_scatter | solution.py:79
  632.9 4.2 all-to-all-start.2
  650.5 6.5 collective-permute-done.87.refs_1_
  657.0 6.2 collective-permute-done.89.refs_3_
  664.2 6.7 fusion.10
  674.6 4.1 gates_owner.1
  680.7 8.5 %copy.42 = f32[2,16,171,171]{3,1,2,0:T(8,128)} copy(f32[2,16,171,171]{3,2,1,0:T(8,128)} %get-tuple-element.226) | data formatting | bytes 7485696
  (484 shorter events, 242.5 us)
Async XLA Ops:
  7.2 128.1 %all-gather.4.cloned.1.call-start = ((), (), s32[]{:S(2)}) async-start(), calls=%async_computation.7 | async-start | bytes 5898240 | tf_op jit(solution)/shard_map/all_gather | solution.py:75
  36.7 206.7 %all-gather.6.cloned.1.call-start = ((), (), s32[]{:S(2)}) async-start(), calls=%async_computation.8 | async-start | bytes 7864320 | tf_op jit(solution)/shard_map/all_gather | solution.py:75
  36.7 25.6 %collective-permute-start.1 = (bf16[256,2048]{1,0:T(8,128)(2,1)}, bf16[256,2048]{1,0:T(8,128)(2,1)}, u32[]{:S(2)}, u32[]{:S(2)}) collective-permute-start(bf16[256,2048]{1,0:T(8,128)(2,1)} %bitcast.247), channel_id=1, source_target_pairs={{0,4},{1,5},{2,6},{3,7},{4,0},{5,1},{6,2},{7,3},{8,12},{9,13},{10,... | collective-permute-start | bytes 3145736 | tf_op jit(solution)/shard_map/ppermute | solution.py:40
  38.3 25.9 %collective-permute-start = (bf16[256,2048]{1,0:T(8,128)(2,1)}, bf16[256,2048]{1,0:T(8,128)(2,1)}, u32[]{:S(2)}, u32[]{:S(2)}) collective-permute-start(bf16[256,2048]{1,0:T(8,128)(2,1)} %bitcast.248), channel_id=1, source_target_pairs={{0,2},{1,3},{2,0},{3,1},{4,6},{5,7},{6,4},{7,5},{8,10},{9,11},{10,... | collective-permute-start | bytes 3145736 | tf_op jit(solution)/shard_map/ppermute | solution.py:40
  38.5 45.4 %collective-permute-start.4 = (bf16[256,2048]{1,0:T(8,128)(2,1)}, bf16[256,2048]{1,0:T(8,128)(2,1)}, u32[]{:S(2)}, u32[]{:S(2)}) collective-permute-start(bf16[256,2048]{1,0:T(8,128)(2,1)} %bitcast.249), channel_id=1, source_target_pairs={{0,1},{1,0},{2,3},{3,2},{4,5},{5,4},{6,7},{7,6},{8,9},{9,8},{10,11... | collective-permute-start | bytes 3145736 | tf_op jit(solution)/shard_map/ppermute | solution.py:40
  68.1 21.2 %collective-permute-start.6 = (bf16[256,2048]{1,0:T(8,128)(2,1)}, bf16[256,2048]{1,0:T(8,128)(2,1)S(1)}, u32[]{:S(2)}, u32[]{:S(2)}) collective-permute-start(bf16[256,2048]{1,0:T(8,128)(2,1)} %collective-permute-done.1), channel_id=1, source_target_pairs={{0,1},{1,0},{2,3},{3,2},{4,5},{5,4},{6,7},{7,6},{8,9},{9,8},{10,11... | collective-permute-start | bytes 3145736 | tf_op jit(solution)/shard_map/ppermute | solution.py:40
  99.0 20.4 %collective-permute-start.25 = (bf16[64,2304]{1,0:T(8,128)(2,1)S(1)}, bf16[64,2304]{1,0:T(8,128)(2,1)S(1)}, u32[]{:S(2)}, u32[]{:S(2)}) collective-permute-start(bf16[64,2304]{1,0:T(8,128)(2,1)S(1)} %get-tuple-element.138), channel_id=1, source_target_pairs={{0,7},{1,6},{2,5},{3,4},{4,3},{5,2},{6,1},{7,0},{8,15},{9,14},{10,... | collective-permute-start | bytes 884744 | tf_op jit(solution)/shard_map/ppermute | solution.py:40
  121.5 193.4 %all-gather.8.cloned.1.call-start = ((), (), s32[]{:S(2)}) async-start(), calls=%async_computation.9 | async-start | bytes 3932160 | tf_op jit(solution)/shard_map/all_gather | solution.py:75
  132.4 29.3 %collective-permute-start.26 = (bf16[256,2048]{1,0:T(8,128)(2,1)}, bf16[256,2048]{1,0:T(8,128)(2,1)}, u32[]{:S(2)}, u32[]{:S(2)}) collective-permute-start(bf16[256,2048]{1,0:T(8,128)(2,1)} %bitcast.19), channel_id=1, source_target_pairs={{0,4},{1,5},{2,6},{3,7},{4,0},{5,1},{6,2},{7,3},{8,12},{9,13},{10,... | collective-permute-start | bytes 3145736 | tf_op jit(solution)/shard_map/ppermute | solution.py:40
  134.0 27.7 %collective-permute-start.27 = (bf16[256,2048]{1,0:T(8,128)(2,1)}, bf16[256,2048]{1,0:T(8,128)(2,1)}, u32[]{:S(2)}, u32[]{:S(2)}) collective-permute-start(bf16[256,2048]{1,0:T(8,128)(2,1)} %bitcast.19), channel_id=1, source_target_pairs={{0,2},{1,3},{2,0},{3,1},{4,6},{5,7},{6,4},{7,5},{8,10},{9,11},{10,... | collective-permute-start | bytes 3145736 | tf_op jit(solution)/shard_map/ppermute | solution.py:40
  189.0 20.3 %collective-permute-start.35 = (bf16[128,2048]{1,0:T(8,128)(2,1)}, bf16[128,2048]{1,0:T(8,128)(2,1)}, u32[]{:S(2)}, u32[]{:S(2)}) collective-permute-start(bf16[128,2048]{1,0:T(8,128)(2,1)} %slice.315), channel_id=1, source_target_pairs={{0,2},{1,3},{2,0},{3,1},{4,6},{5,7},{6,4},{7,5},{8,10},{9,11},{10,... | collective-permute-start | bytes 1572872 | tf_op jit(solution)/shard_map/ppermute | solution.py:40
  189.4 21.9 %collective-permute-start.29 = (bf16[128,2048]{1,0:T(8,128)(2,1)}, bf16[128,2048]{1,0:T(8,128)(2,1)S(1)}, u32[]{:S(2)}, u32[]{:S(2)}) collective-permute-start(bf16[128,2048]{1,0:T(8,128)(2,1)} %get-tuple-element.264), channel_id=1, source_target_pairs={{0,4},{1,5},{2,6},{3,7},{4,0},{5,1},{6,2},{7,3},{8,12},{9,13},{10,... | collective-permute-start | bytes 1572872 | tf_op jit(solution)/shard_map/ppermute | solution.py:40
  190.7 28.9 %collective-permute-start.34 = (bf16[128,2048]{1,0:T(8,128)(2,1)}, bf16[128,2048]{1,0:T(8,128)(2,1)S(1)}, u32[]{:S(2)}, u32[]{:S(2)}) collective-permute-start(bf16[128,2048]{1,0:T(8,128)(2,1)} %get-tuple-element.265), channel_id=1, source_target_pairs={{0,2},{1,3},{2,0},{3,1},{4,6},{5,7},{6,4},{7,5},{8,10},{9,11},{10,... | collective-permute-start | bytes 1572872 | tf_op jit(solution)/shard_map/ppermute | solution.py:40
  201.8 18.6 %collective-permute-start.31 = (bf16[128,2048]{1,0:T(8,128)(2,1)}, bf16[128,2048]{1,0:T(8,128)(2,1)S(1)}, u32[]{:S(2)}, u32[]{:S(2)}) collective-permute-start(bf16[128,2048]{1,0:T(8,128)(2,1)} %get-tuple-element.248), channel_id=1, source_target_pairs={{0,4},{1,5},{2,6},{3,7},{4,0},{5,1},{6,2},{7,3},{8,12},{9,13},{10,... | collective-permute-start | bytes 1572872 | tf_op jit(solution)/shard_map/ppermute | solution.py:40
  202.3 27.8 %collective-permute-start.33 = (bf16[128,2048]{1,0:T(8,128)(2,1)}, bf16[128,2048]{1,0:T(8,128)(2,1)S(1)}, u32[]{:S(2)}, u32[]{:S(2)}) collective-permute-start(bf16[128,2048]{1,0:T(8,128)(2,1)} %get-tuple-element.249), channel_id=1, source_target_pairs={{0,2},{1,3},{2,0},{3,1},{4,6},{5,7},{6,4},{7,5},{8,10},{9,11},{10,... | collective-permute-start | bytes 1572872 | tf_op jit(solution)/shard_map/ppermute | solution.py:40
  207.0 249.2 %reduce-scatter.5.cloned.1.call-start = ((), (), s32[]{:S(2)}) async-start(), calls=%async_computation.10 | async-start | bytes 3932160 | tf_op jit(solution)/shard_map/reduce_scatter | solution.py:79
  209.3 29.4 %collective-permute-start.37 = (bf16[256,2048]{1,0:T(8,128)(2,1)}, bf16[256,2048]{1,0:T(8,128)(2,1)S(1)}, u32[]{:S(2)}, u32[]{:S(2)}) collective-permute-start(bf16[256,2048]{1,0:T(8,128)(2,1)} %bitcast.19), channel_id=1, source_target_pairs={{0,1},{1,0},{2,3},{3,2},{4,5},{5,4},{6,7},{7,6},{8,9},{9,8},{10,11... | collective-permute-start | bytes 3145736 | tf_op jit(solution)/shard_map/ppermute | solution.py:40
  211.3 28.6 %collective-permute-start.38 = (bf16[256,2048]{1,0:T(8,128)(2,1)}, bf16[256,2048]{1,0:T(8,128)(2,1)S(1)}, u32[]{:S(2)}, u32[]{:S(2)}) collective-permute-start(bf16[256,2048]{1,0:T(8,128)(2,1)} %collective-permute-done.27), channel_id=1, source_target_pairs={{0,1},{1,0},{2,3},{3,2},{4,5},{5,4},{6,7},{7,6},{8,9},{9,8},{10,11... | collective-permute-start | bytes 3145736 | tf_op jit(solution)/shard_map/ppermute | solution.py:40
  219.5 21.9 %collective-permute-start.39 = (bf16[256,2048]{1,0:T(8,128)(2,1)}, bf16[256,2048]{1,0:T(8,128)(2,1)S(1)}, u32[]{:S(2)}, u32[]{:S(2)}) collective-permute-start(bf16[256,2048]{1,0:T(8,128)(2,1)} %collective-permute-done.26), channel_id=1, source_target_pairs={{0,1},{1,0},{2,3},{3,2},{4,5},{5,4},{6,7},{7,6},{8,9},{9,8},{10,11... | collective-permute-start | bytes 3145736 | tf_op jit(solution)/shard_map/ppermute | solution.py:40
  234.4 24.9 %collective-permute-start.42 = (bf16[256,2048]{1,0:T(8,128)(2,1)}, bf16[256,2048]{1,0:T(8,128)(2,1)S(1)}, u32[]{:S(2)}, u32[]{:S(2)}) collective-permute-start(bf16[256,2048]{1,0:T(8,128)(2,1)} %get-tuple-element.236), channel_id=1, source_target_pairs={{0,4},{1,5},{2,6},{3,7},{4,0},{5,1},{6,2},{7,3},{8,12},{9,13},{10,... | collective-permute-start | bytes 3145736 | tf_op jit(solution)/shard_map/ppermute | solution.py:40
  235.2 24.6 %collective-permute-start.43 = (bf16[256,2048]{1,0:T(8,128)(2,1)}, bf16[256,2048]{1,0:T(8,128)(2,1)S(1)}, u32[]{:S(2)}, u32[]{:S(2)}) collective-permute-start(bf16[256,2048]{1,0:T(8,128)(2,1)} %get-tuple-element.236), channel_id=1, source_target_pairs={{0,2},{1,3},{2,0},{3,1},{4,6},{5,7},{6,4},{7,5},{8,10},{9,11},{10,... | collective-permute-start | bytes 3145736 | tf_op jit(solution)/shard_map/ppermute | solution.py:40
  239.8 23.0 %collective-permute-start.41 = (bf16[128,2048]{1,0:T(8,128)(2,1)}, bf16[128,2048]{1,0:T(8,128)(2,1)}, u32[]{:S(2)}, u32[]{:S(2)}) collective-permute-start(bf16[128,2048]{1,0:T(8,128)(2,1)} %collective-permute-done.36), channel_id=1, source_target_pairs={{0,1},{1,0},{2,3},{3,2},{4,5},{5,4},{6,7},{7,6},{8,9},{9,8},{10,11... | collective-permute-start | bytes 1572872 | tf_op jit(solution)/shard_map/ppermute | solution.py:40
  243.3 32.0 %collective-permute-start.46 = (bf16[256,2048]{1,0:T(8,128)(2,1)}, bf16[256,2048]{1,0:T(8,128)(2,1)S(1)}, u32[]{:S(2)}, u32[]{:S(2)}) collective-permute-start(bf16[256,2048]{1,0:T(8,128)(2,1)} %get-tuple-element.236), channel_id=1, source_target_pairs={{0,1},{1,0},{2,3},{3,2},{4,5},{5,4},{6,7},{7,6},{8,9},{9,8},{10,11... | collective-permute-start | bytes 3145736 | tf_op jit(solution)/shard_map/ppermute | solution.py:40
  322.4 180.8 %reduce-scatter.7.cloned.1.call-start = ((), (), s32[]{:S(2)}) async-start(), calls=%async_computation.11 | async-start | bytes 7864320 | tf_op jit(solution)/shard_map/reduce_scatter | solution.py:79
  350.0 21.7 %collective-permute-start.52 = (bf16[128,2048]{1,0:T(8,128)(2,1)}, bf16[128,2048]{1,0:T(8,128)(2,1)S(1)}, u32[]{:S(2)}, u32[]{:S(2)}) collective-permute-start(bf16[128,2048]{1,0:T(8,128)(2,1)} %get-tuple-element.263), channel_id=1, source_target_pairs={{0,2},{1,3},{2,0},{3,1},{4,6},{5,7},{6,4},{7,5},{8,10},{9,11},{10,... | collective-permute-start | bytes 1572872 | tf_op jit(solution)/shard_map/ppermute | solution.py:40
  350.0 22.5 %collective-permute-start.53 = (bf16[128,2048]{1,0:T(8,128)(2,1)S(1)}, bf16[128,2048]{1,0:T(8,128)(2,1)}, u32[]{:S(2)}, u32[]{:S(2)}) collective-permute-start(bf16[128,2048]{1,0:T(8,128)(2,1)S(1)} %get-tuple-element.262), channel_id=1, source_target_pairs={{0,4},{1,5},{2,6},{3,7},{4,0},{5,1},{6,2},{7,3},{8,12},{9,13},{10,... | collective-permute-start | bytes 1572872 | tf_op jit(solution)/shard_map/ppermute | solution.py:40
  351.2 23.9 %collective-permute-start.54 = (bf16[128,2048]{1,0:T(8,128)(2,1)S(1)}, bf16[128,2048]{1,0:T(8,128)(2,1)S(1)}, u32[]{:S(2)}, u32[]{:S(2)}) collective-permute-start(bf16[128,2048]{1,0:T(8,128)(2,1)S(1)} %get-tuple-element.261), channel_id=1, source_target_pairs={{0,4},{1,5},{2,6},{3,7},{4,0},{5,1},{6,2},{7,3},{8,12},{9,13},{10,... | collective-permute-start | bytes 1572872 | tf_op jit(solution)/shard_map/ppermute | solution.py:40
  352.1 23.1 %collective-permute-start.55 = (bf16[128,2048]{1,0:T(8,128)(2,1)S(1)}, bf16[128,2048]{1,0:T(8,128)(2,1)S(1)}, u32[]{:S(2)}, u32[]{:S(2)}) collective-permute-start(bf16[128,2048]{1,0:T(8,128)(2,1)S(1)} %get-tuple-element.260), channel_id=1, source_target_pairs={{0,2},{1,3},{2,0},{3,1},{4,6},{5,7},{6,4},{7,5},{8,10},{9,11},{10,... | collective-permute-start | bytes 1572872 | tf_op jit(solution)/shard_map/ppermute | solution.py:40
  386.3 160.7 %reduce-scatter.9.cloned.1.call-start = ((), (), s32[]{:S(2)}) async-start(), calls=%async_computation.12 | async-start | bytes 1966080 | tf_op jit(solution)/shard_map/reduce_scatter | solution.py:79
  416.5 25.2 %collective-permute-start.59 = (bf16[128,2048]{1,0:T(8,128)(2,1)S(1)}, bf16[128,2048]{1,0:T(8,128)(2,1)S(1)}, u32[]{:S(2)}, u32[]{:S(2)}) collective-permute-start(bf16[128,2048]{1,0:T(8,128)(2,1)S(1)} %get-tuple-element.256), channel_id=1, source_target_pairs={{0,4},{1,5},{2,6},{3,7},{4,0},{5,1},{6,2},{7,3},{8,12},{9,13},{10,... | collective-permute-start | bytes 1572872 | tf_op jit(solution)/shard_map/ppermute | solution.py:40
  417.7 24.1 %collective-permute-start.64 = (bf16[128,2048]{1,0:T(8,128)(2,1)S(1)}, bf16[128,2048]{1,0:T(8,128)(2,1)S(1)}, u32[]{:S(2)}, u32[]{:S(2)}) collective-permute-start(bf16[128,2048]{1,0:T(8,128)(2,1)S(1)} %get-tuple-element.257), channel_id=1, source_target_pairs={{0,2},{1,3},{2,0},{3,1},{4,6},{5,7},{6,4},{7,5},{8,10},{9,11},{10,... | collective-permute-start | bytes 1572872 | tf_op jit(solution)/shard_map/ppermute | solution.py:40
  430.9 20.3 %collective-permute-start.61 = (bf16[128,2048]{1,0:T(8,128)(2,1)S(1)}, bf16[128,2048]{1,0:T(8,128)(2,1)S(1)}, u32[]{:S(2)}, u32[]{:S(2)}) collective-permute-start(bf16[128,2048]{1,0:T(8,128)(2,1)S(1)} %get-tuple-element.244), channel_id=1, source_target_pairs={{0,4},{1,5},{2,6},{3,7},{4,0},{5,1},{6,2},{7,3},{8,12},{9,13},{10,... | collective-permute-start | bytes 1572872 | tf_op jit(solution)/shard_map/ppermute | solution.py:40
  431.8 19.3 %collective-permute-start.63 = (bf16[128,2048]{1,0:T(8,128)(2,1)S(1)}, bf16[128,2048]{1,0:T(8,128)(2,1)S(1)}, u32[]{:S(2)}, u32[]{:S(2)}) collective-permute-start(bf16[128,2048]{1,0:T(8,128)(2,1)S(1)} %get-tuple-element.245), channel_id=1, source_target_pairs={{0,2},{1,3},{2,0},{3,1},{4,6},{5,7},{6,4},{7,5},{8,10},{9,11},{10,... | collective-permute-start | bytes 1572872 | tf_op jit(solution)/shard_map/ppermute | solution.py:40
  456.2 23.5 %collective-permute-start.66 = (bf16[256,2048]{1,0:T(8,128)(2,1)S(1)}, bf16[256,2048]{1,0:T(8,128)(2,1)S(1)}, u32[]{:S(2)}, u32[]{:S(2)}) collective-permute-start(bf16[256,2048]{1,0:T(8,128)(2,1)S(1)} %get-tuple-element.176), channel_id=1, source_target_pairs={{0,4},{1,5},{2,6},{3,7},{4,0},{5,1},{6,2},{7,3},{8,12},{9,13},{10,... | collective-permute-start | bytes 3145736 | tf_op jit(solution)/shard_map/ppermute | solution.py:40
  457.1 23.5 %collective-permute-start.65 = (bf16[256,2048]{1,0:T(8,128)(2,1)S(1)}, bf16[256,2048]{1,0:T(8,128)(2,1)S(1)}, u32[]{:S(2)}, u32[]{:S(2)}) collective-permute-start(bf16[256,2048]{1,0:T(8,128)(2,1)S(1)} %get-tuple-element.176), channel_id=1, source_target_pairs={{0,2},{1,3},{2,0},{3,1},{4,6},{5,7},{6,4},{7,5},{8,10},{9,11},{10,... | collective-permute-start | bytes 3145736 | tf_op jit(solution)/shard_map/ppermute | solution.py:40
  457.7 34.4 %collective-permute-start.69 = (bf16[256,2048]{1,0:T(8,128)(2,1)S(1)}, bf16[256,2048]{1,0:T(8,128)(2,1)S(1)}, u32[]{:S(2)}, u32[]{:S(2)}) collective-permute-start(bf16[256,2048]{1,0:T(8,128)(2,1)S(1)} %get-tuple-element.176), channel_id=1, source_target_pairs={{0,1},{1,0},{2,3},{3,2},{4,5},{5,4},{6,7},{7,6},{8,9},{9,8},{10,11... | collective-permute-start | bytes 3145736 | tf_op jit(solution)/shard_map/ppermute | solution.py:40
  506.3 40.7 %all-to-all-start = ((bf16[8,64,2304]{2,1,0:T(8,128)(2,1)}), bf16[8,64,2304]{2,1,0:T(8,128)(2,1)S(1)}, u32[]{:S(2)}, u32[]{:S(2)}) async-start(bf16[8,64,2304]{2,1,0:T(8,128)(2,1)} %bitcast.251), calls=%async_computation.3 | async-start | bytes 4718592 | tf_op jit(solution)/shard_map/all_to_all | solution.py:102
  509.9 123.0 %reduce-scatter.11.cloned.1.call-start = ((), (), s32[]{:S(2)}) async-start(), calls=%async_computation.13 | async-start | bytes 3932160 | tf_op jit(solution)/shard_map/reduce_scatter | solution.py:79
  578.1 25.7 %collective-permute-start.84 = (bf16[48,768]{1,0:T(8,128)(2,1)S(1)}, bf16[48,768]{1,0:T(8,128)(2,1)S(1)}, u32[]{:S(2)}, u32[]{:S(2)}) collective-permute-start(bf16[48,768]{1,0:T(8,128)(2,1)S(1)} %fusion.54), channel_id=1, source_target_pairs={{0,8},{1,9},{2,10},{3,11},{4,12},{5,13},{6,14},{7,15},{8,16},{9,17... | collective-permute-start | bytes 221192 | tf_op jit(solution)/shard_map/ppermute | solution.py:46
  593.4 22.1 %collective-permute-start.79 = (bf16[128,2048]{1,0:T(8,128)(2,1)}, bf16[128,2048]{1,0:T(8,128)(2,1)}, u32[]{:S(2)}, u32[]{:S(2)}) collective-permute-start(bf16[128,2048]{1,0:T(8,128)(2,1)} %get-tuple-element.254), channel_id=1, source_target_pairs={{0,2},{1,3},{2,0},{3,1},{4,6},{5,7},{6,4},{7,5},{8,10},{9,11},{10,... | collective-permute-start | bytes 1572872 | tf_op jit(solution)/shard_map/ppermute | solution.py:40
  595.7 19.8 %collective-permute-start.81 = (bf16[128,2048]{1,0:T(8,128)(2,1)}, bf16[128,2048]{1,0:T(8,128)(2,1)}, u32[]{:S(2)}, u32[]{:S(2)}) collective-permute-start(bf16[128,2048]{1,0:T(8,128)(2,1)} %get-tuple-element.252), channel_id=1, source_target_pairs={{0,4},{1,5},{2,6},{3,7},{4,0},{5,1},{6,2},{7,3},{8,12},{9,13},{10,... | collective-permute-start | bytes 1572872 | tf_op jit(solution)/shard_map/ppermute | solution.py:40
  597.2 23.1 %all-to-all-start.1 = ((bf16[8,64,384]{2,1,0:T(8,128)(2,1)}), bf16[8,64,384]{2,1,0:T(8,128)(2,1)}, u32[]{:S(2)}, u32[]{:S(2)}) async-start(bf16[8,64,384]{2,1,0:T(8,128)(2,1)} %bitcast.262), calls=%async_computation.4 | async-start | bytes 786432 | tf_op jit(solution)/shard_map/all_to_all | solution.py:102
  612.5 34.2 %collective-permute-start.78 = (bf16[128,2048]{1,0:T(8,128)(2,1)}, bf16[128,2048]{1,0:T(8,128)(2,1)}, u32[]{:S(2)}, u32[]{:S(2)}) collective-permute-start(bf16[128,2048]{1,0:T(8,128)(2,1)} %get-tuple-element.255), channel_id=1, source_target_pairs={{0,4},{1,5},{2,6},{3,7},{4,0},{5,1},{6,2},{7,3},{8,12},{9,13},{10,... | collective-permute-start | bytes 1572872 | tf_op jit(solution)/shard_map/ppermute | solution.py:40
  614.1 33.1 %collective-permute-start.83 = (bf16[128,2048]{1,0:T(8,128)(2,1)}, bf16[128,2048]{1,0:T(8,128)(2,1)}, u32[]{:S(2)}, u32[]{:S(2)}) collective-permute-start(bf16[128,2048]{1,0:T(8,128)(2,1)} %get-tuple-element.253), channel_id=1, source_target_pairs={{0,2},{1,3},{2,0},{3,1},{4,6},{5,7},{6,4},{7,5},{8,10},{9,11},{10,... | collective-permute-start | bytes 1572872 | tf_op jit(solution)/shard_map/ppermute | solution.py:40
  618.7 28.5 %collective-permute-start.80 = (bf16[128,2048]{1,0:T(8,128)(2,1)}, bf16[128,2048]{1,0:T(8,128)(2,1)}, u32[]{:S(2)}, u32[]{:S(2)}) collective-permute-start(bf16[128,2048]{1,0:T(8,128)(2,1)} %get-tuple-element.243), channel_id=1, source_target_pairs={{0,4},{1,5},{2,6},{3,7},{4,0},{5,1},{6,2},{7,3},{8,12},{9,13},{10,... | collective-permute-start | bytes 1572872 | tf_op jit(solution)/shard_map/ppermute | solution.py:40
  619.2 28.0 %collective-permute-start.82 = (bf16[128,2048]{1,0:T(8,128)(2,1)}, bf16[128,2048]{1,0:T(8,128)(2,1)}, u32[]{:S(2)}, u32[]{:S(2)}) collective-permute-start(bf16[128,2048]{1,0:T(8,128)(2,1)} %get-tuple-element.242), channel_id=1, source_target_pairs={{0,2},{1,3},{2,0},{3,1},{4,6},{5,7},{6,4},{7,5},{8,10},{9,11},{10,... | collective-permute-start | bytes 1572872 | tf_op jit(solution)/shard_map/ppermute | solution.py:40
  620.3 24.8 %collective-permute-start.88 = (bf16[192,768]{1,0:T(8,128)(2,1)}, bf16[192,768]{1,0:T(8,128)(2,1)}, u32[]{:S(2)}, u32[]{:S(2)}) collective-permute-start(bf16[192,768]{1,0:T(8,128)(2,1)} %bitcast.79.refs_0_), channel_id=1, source_target_pairs={{0,4},{1,5},{2,6},{3,7},{4,0},{5,1},{6,2},{7,3},{8,12},{9,13},{10,... | collective-permute-start | bytes 884744 | tf_op jit(solution)/shard_map/ppermute | solution.py:40
  632.9 30.3 %all-to-all-start.2 = ((bf16[8,64,768]{2,1,0:T(8,128)(2,1)}), bf16[8,64,768]{2,1,0:T(8,128)(2,1)}, u32[]{:S(2)}, u32[]{:S(2)}) async-start(bf16[8,64,768]{2,1,0:T(8,128)(2,1)} %bitcast.261), calls=%async_computation.6 | async-start | bytes 1572864 | tf_op jit(solution)/shard_map/all_to_all | solution.py:102
  (133 other events, 1953.3 us)
Sparse Core Ops, SparseCore 0:
  36.8 89.9 all-gather.3
  129.0 113.6 all-gather.5
  244.8 61.7 all-gather.7
  322.5 60.1 reduce-scatter.4
  386.4 111.5 reduce-scatter.6
  503.3 35.3 reduce-scatter.8
  566.7 66.1 reduce-scatter.10

commit v5 on v4

--- a/solution.py
+++ b/solution.py
@@ -895,7 +895,7 @@
 
     packed = ring_stack(packed, turn, groups).reshape(PAD, 2 * WIDE)
     packed, out_grads = lax.optimization_barrier((packed, out_grads))
-    across, along = swap(packed, 4), swap(packed, 2)
+    across, along = lax.optimization_barrier((swap(packed, 4), swap(packed, 2)))
     near = [packed, along, across, swap(across, 2)]
     near, both_grads = lax.optimization_barrier((near, both_grads))
     grad_gblocks, small = simple_call(

time: 704 us -> 696 us (0.989)
  waiting for transfers between devices: 223 us -> 215 us
    ppermute x9, waiting for transfers between devices: 14.2 us -> 3.41 us  [onward(): return lax.ppermute(values, AXES, pairs)]
  transfers between devices with their start and end apart: 104 -> 104, of which waited for: 44 -> 42; matrix products, arithmetic and copies ran while one was open for 31% -> 31% of each run, Pallas kernels for 11% -> 11%
where the time goes in v5:
time: 696 us; the launch traced here: 689 us
  waiting for transfers between devices  215 us (31%)
  matrix products  134 us (19%)
  local copies, waits for them, and re-layouts  98.9 us (14%)
  starting transfers between devices  96.7 us (14%)
  Pallas kernels  81.6 us (12%)
  other arithmetic  46.5 us (7%)
  between operations  15.8 us (2%)
    ppermute x85, waiting for transfers between devices, swap(): lax.ppermute(values, AXES, [(i, i ^ bit) for i in range(device_count())])  199 us
    unnamed x192, local copies, waits for them, and re-layouts  74.7 us
    ppermute x85, starting transfers between devices, swap(): lax.ppermute(values, AXES, [(i, i ^ bit) for i in range(device_count())])  66.7 us
    dot_general x8, matrix products, contract_cols(): lax.dot_general(left, right, (((1,), (1,)), ((), ())), preferred_element_...  59.5 us
    dot_general x4, matrix products, contract_rows(): lax.dot_general(left, right, (((0,), (0,)), ((), ())), preferred_element_...  45.2 us
    pallas_call x1, Pallas kernels, local(): mixer_backward(where, pre, pre, segments, segments, state, state, middle_...  33.5 us
    dot_general x2, matrix products, product(): return jnp.dot(left, right, preferred_element_type=F32)  29.1 us
    pallas_call x1, Pallas kernels, local(): mixer_forward(where, normed_blocks, segments, mixer_weight, gate_weight,...  26 us
  transfers between devices with their start and end apart: 104, of which 42 were waited for; matrix products, arithmetic and copies ran while one was open for 31% of the time, Pallas kernels for 11%

profile of v5, /device:TPU:0, one launch (start us, length us, event | category | flops | bytes accessed | tf_op | source)
XLA Modules:
  0.0 688.7 jit_solution(16712056219853328732)
XLA Ops:
  26.0 5.7 collective-permute-done.14.refs_6_
  31.6 3.9 collective-permute-done.15.refs_7_
  53.5 8.8 %collective-permute-done.1 = bf16[256,2048]{1,0:T(8,128)(2,1)} collective-permute-done((bf16[256,2048]{1,0:T(8,128)(2,1)}, bf16[256,2048]{1,0:T(8,128)(2,1)}, u32[]{:S(2)}, u32[]{:S(2)}) %collective-permute-start.1) | collective-permute-done | bytes 1048608 | tf_op jit(solution)/shard_map/ppermute | solution.py:40
  73.3 4.3 collective-permute-done.2
  92.0 4.2 collective-permute-done.20.refs_2_
  101.8 3.9 collective-permute-done.23.refs_5_
  105.7 8.5 %collective-permute-done.24.refs_6_ = bf16[64,2304]{1,0:T(8,128)(2,1)S(1)} collective-permute-done((bf16[64,2304]{1,0:T(8,128)(2,1)S(1)}, bf16[64,2304]{1,0:T(8,128)(2,1)S(1)}, u32[]{:S(2)}, u32[]{:S(2)}) %collective-permute-start.24) | collective-permute-done | bytes 294944 | tf_op jit(solution)/shard_map/ppermute | solution.py:40
  114.1 5.2 collective-permute-done.25.refs_7_
  122.2 10.2 %norm_rows.1 = bf16[2048,2048]{1,0:T(8,128)(2,1)} custom-call(bf16[2048,2048]{1,0:T(8,128)(2,1)} %constant_dynamic-update-slice_fusion.values, f32[1,2048]{1,0:T(1,128)S(1)} %reshape.460.gain), custom_call_target="tpu_custom_call" | custom-call | flops 1 | bytes 1 | tf_op jit(solution)/shard_map/norm_rows/pallas_call | solution.py:177
  135.6 26.0 %mixer_forward.1 = (f32[8,256,768]{2,1,0:T(8,128)}, f32[8,256,384]{2,1,0:T(8,128)}, bf16[8,256,384]{2,1,0:T(8,128)(2,1)S(1)}) custom-call(s32[1]{0:T(128)} %bitcast.1.place, bf16[8,256,2048]{2,1,0:T(8,128)(2,1)} %bitcast.252, f32[8,256,128]{2,1,0:T(8,128)S(1)} %broadcast_in_dim.71.segment.segment_rim, ...), custom_call_target="tpu_custom_call" | custom-call | flops 7650410496 | bytes 11010048 | tf_op jit(solution)/shard_map/mixer_forward/pallas_call | solution.py:811
  161.7 4.3 convolution_convert_fusion.2
  166.3 7.0 %collective-permute-done.28 = bf16[1024,2048]{1,0:T(8,128)(2,1)S(1)} collective-permute-done((bf16[1024,2048]{1,0:T(8,128)(2,1)S(1)}, bf16[1024,2048]{1,0:T(8,128)(2,1)S(1)}, u32[]{:S(2)}, u32[]{:S(2)}) %collective-permute-start.28) | collective-permute-done | bytes 4194336 | tf_op jit(solution)/shard_map/ppermute | solution.py:40
  173.3 3.8 convert_add_fusion.3
  192.5 4.5 collective-permute-done.30
  211.8 7.7 %collective-permute-done.34 = bf16[128,2048]{1,0:T(8,128)(2,1)S(1)} collective-permute-done((bf16[128,2048]{1,0:T(8,128)(2,1)}, bf16[128,2048]{1,0:T(8,128)(2,1)S(1)}, u32[]{:S(2)}, u32[]{:S(2)}) %collective-permute-start.34) | collective-permute-done | bytes 524320 | tf_op jit(solution)/shard_map/ppermute | solution.py:40
  221.0 9.1 %collective-permute-done.33 = bf16[128,2048]{1,0:T(8,128)(2,1)S(1)} collective-permute-done((bf16[128,2048]{1,0:T(8,128)(2,1)}, bf16[128,2048]{1,0:T(8,128)(2,1)S(1)}, u32[]{:S(2)}, u32[]{:S(2)}) %collective-permute-start.33) | collective-permute-done | bytes 524320 | tf_op jit(solution)/shard_map/ppermute | solution.py:40
  243.3 15.9 %collective-permute-done.42 = bf16[256,2048]{1,0:T(8,128)(2,1)S(1)} collective-permute-done((bf16[256,2048]{1,0:T(8,128)(2,1)}, bf16[256,2048]{1,0:T(8,128)(2,1)S(1)}, u32[]{:S(2)}, u32[]{:S(2)}) %collective-permute-start.42) | collective-permute-done | bytes 1048608 | tf_op jit(solution)/shard_map/ppermute | solution.py:40
  267.4 4.8 collective-permute-done.44
  280.2 15.7 %fusion.74 = f32[2048,1536]{1,0:T(8,128)S(1)} fusion(bf16[2048,2048]{1,0:T(8,128)(2,1)} %constant_dynamic-update-slice_fusion.20, bf16[2048,1536]{1,0:T(8,128)(2,1)S(1)} %bitcast.268), kind=kOutput, calls=%fused_computation.205 | convolution fusion | flops 12884901888 | bytes 27262976 | tf_op jit(solution)/shard_map/dot_general | solution.py:304
  296.0 7.1 %add_multiply_fusion = (f32[2048,768]{1,0:T(8,128)}, bf16[2048,768]{1,0:T(8,128)(2,1)S(1)}, f32[2048,768]{1,0:T(8,128)}) fusion(f32[2048,1536]{1,0:T(8,128)S(1)} %fusion.74), kind=kLoop, calls=%fused_computation.8 | loop fusion | flops 31457280 | bytes 28311552 | tf_op jit(solution)/shard_map/mul | solution.py:828
  304.4 10.5 %convolution_convert_fusion.6 = bf16[2048,768]{1,0:T(8,128)(2,1)} fusion(bf16[2048,2048]{1,0:T(8,128)(2,1)} %constant_dynamic-update-slice_fusion.10, bf16[2048,768]{1,0:T(8,128)(2,1)S(1)} %get-tuple-element.159), kind=kOutput, calls=%fused_computation.17 | convolution fusion | flops 6444023808 | bytes 14680064 | tf_op jit(solution)/shard_map/dot_general | solution.py:308
  315.0 6.9 convolution_convert_fusion.4
  322.4 13.3 %multiply_convert_fusion.1 = (bf16[2048,768]{1,0:T(8,128)(2,1)S(1)}, bf16[2048,768]{1,0:T(8,128)(2,1)S(1)}) fusion(f32[2048,768]{1,0:T(8,128)} %get-tuple-element.164, f32[2048,768]{1,0:T(8,128)} %get-tuple-element.165, bf16[2048,2048]{1,0:T(8,128)(2,1)} %constant_dynamic-update-slice_fusion.10, bf16[2048,768]{1,0:T(8,128)(2,1)} %all-gather.8.cloned.1.call-done), kind=kOutput, calls=%fused_computation.7 | convolution fusion | flops 6448742400 | bytes 30408704 | tf_op jit(solution)/shard_map/dot_general | solution.py:304
  336.3 9.4 %convert_add_fusion.2 = f32[1024,2048]{1,0:T(8,128)S(1)} fusion(bf16[1024,2048]{1,0:T(8,128)(2,1)} %collective-permute-done.51, bf16[1024,768]{1,0:T(8,128)(2,1)} %get-tuple-element.166, bf16[2048,768]{1,0:T(8,128)(2,1)} %all-gather.8.cloned.1.call-done), kind=kOutput, calls=%fused_computation.2 | convolution fusion | flops 3225419776 | bytes 17301504 | tf_op jit(solution)/shard_map/dot_general | solution.py:312
  354.0 17.7 %convolution_convert_fusion = bf16[2048,1536]{1,0:T(8,128)(2,1)} fusion(bf16[2048,2048]{1,0:T(8,128)(2,1)} %constant_dynamic-update-slice_fusion.20, bf16[2048,1536]{1,0:T(8,128)(2,1)S(1)} %pad_maximum_fusion), kind=kOutput, calls=%fused_computation.4 | convolution fusion | flops 12888047616 | bytes 20971520 | tf_op jit(solution)/shard_map/dot_general | solution.py:308
  375.2 11.1 %convolution_convert_fusion.1 = bf16[1024,2048]{1,0:T(8,128)(2,1)} fusion(bf16[2048,1536]{1,0:T(8,128)(2,1)} %all-gather.6.cloned.1.call-done, bf16[2048,1536]{1,0:T(8,128)(2,1)} %copy-done.47), kind=kOutput, calls=%fused_computation.12 | convolution fusion | flops 6444548096 | bytes 13631488 | tf_op jit(solution)/shard_map/dot_general | solution.py:312
  388.8 11.9 %collective-permute-done.56 = bf16[128,2048]{1,0:T(8,128)(2,1)S(1)} collective-permute-done((bf16[128,2048]{1,0:T(8,128)(2,1)S(1)}, bf16[128,2048]{1,0:T(8,128)(2,1)S(1)}, u32[]{:S(2)}, u32[]{:S(2)}) %collective-permute-start.56) | collective-permute-done | bytes 524320 | tf_op jit(solution)/shard_map/ppermute | solution.py:40
  403.6 9.8 %convert_add_fusion.1 = f32[1024,2048]{1,0:T(8,128)S(1)} fusion(bf16[1024,2048]{1,0:T(8,128)(2,1)} %collective-permute-done.58, bf16[1024,1536]{1,0:T(8,128)(2,1)S(1)} %slice-done, bf16[2048,1536]{1,0:T(8,128)(2,1)} %all-gather.6.cloned.1.call-done), kind=kOutput, calls=%fused_computation.1 | convolution fusion | flops 6446645248 | bytes 22020096 | tf_op jit(solution)/shard_map/dot_general | solution.py:312
  418.3 10.8 %collective-permute-done.60 = bf16[128,2048]{1,0:T(8,128)(2,1)S(1)} collective-permute-done((bf16[128,2048]{1,0:T(8,128)(2,1)S(1)}, bf16[128,2048]{1,0:T(8,128)(2,1)S(1)}, u32[]{:S(2)}, u32[]{:S(2)}) %collective-permute-start.60) | collective-permute-done | bytes 524320 | tf_op jit(solution)/shard_map/ppermute | solution.py:40
  432.5 9.3 %collective-permute-done.59 = bf16[128,2048]{1,0:T(8,128)(2,1)S(1)} collective-permute-done((bf16[128,2048]{1,0:T(8,128)(2,1)S(1)}, bf16[128,2048]{1,0:T(8,128)(2,1)S(1)}, u32[]{:S(2)}, u32[]{:S(2)}) %collective-permute-start.59) | collective-permute-done | bytes 524320 | tf_op jit(solution)/shard_map/ppermute | solution.py:40
  441.8 9.4 %collective-permute-done.61 = bf16[128,2048]{1,0:T(8,128)(2,1)S(1)} collective-permute-done((bf16[128,2048]{1,0:T(8,128)(2,1)S(1)}, bf16[128,2048]{1,0:T(8,128)(2,1)S(1)}, u32[]{:S(2)}, u32[]{:S(2)}) %collective-permute-start.61) | collective-permute-done | bytes 524320 | tf_op jit(solution)/shard_map/ppermute | solution.py:40
  452.1 4.0 fusion.12
  457.7 21.9 %collective-permute-done.66 = bf16[256,2048]{1,0:T(8,128)(2,1)S(1)} collective-permute-done((bf16[256,2048]{1,0:T(8,128)(2,1)S(1)}, bf16[256,2048]{1,0:T(8,128)(2,1)S(1)}, u32[]{:S(2)}, u32[]{:S(2)}) %collective-permute-start.66) | collective-permute-done | bytes 1048608 | tf_op jit(solution)/shard_map/ppermute | solution.py:40
  482.9 8.6 %collective-permute-done.67 = bf16[128,2048]{1,0:T(8,128)(2,1)S(1)} collective-permute-done((bf16[128,2048]{1,0:T(8,128)(2,1)S(1)}, bf16[128,2048]{1,0:T(8,128)(2,1)S(1)}, u32[]{:S(2)}, u32[]{:S(2)}) %collective-permute-start.67) | collective-permute-done | bytes 524320 | tf_op jit(solution)/shard_map/ppermute | solution.py:40
  497.5 5.6 convolution_convert_fusion.7
  511.1 33.5 %mixer_backward.1 = (bf16[8,256,768]{2,1,0:T(8,128)(2,1)S(1)}, bf16[192,768]{1,0:T(8,128)(2,1)S(1)}) custom-call(s32[1]{0:T(128)} %bitcast.1.place, f32[8,256,768]{2,1,0:T(8,128)} %get-tuple-element.176.pre.rim, f32[8,256,768]{2,1,0:T(8,128)} %get-tuple-element.176.pre.rim, f32[8,256,128]{2,1,0:T(8,128)S(1)} %copy-done.3, f32[8,256,128]{2,1,0:T(8,128)S(1)} %copy-done.3, ...), custom_call_target="tpu_custom_call" | custom-call | flops 6845104128 | bytes 18874368 | tf_op jit(solution)/shard_map/mixer_backward/pallas_call | solution.py:864
  546.9 11.4 %convolution_convert_fusion.5 = bf16[2048,768]{1,0:T(8,128)(2,1)} fusion(bf16[2048,2048]{1,0:T(8,128)(2,1)} %norm_rows.1, bf16[2048,768]{1,0:T(8,128)(2,1)} %bitcast.232), kind=kOutput, calls=%fused_computation.16 | convolution fusion | flops 6444023808 | bytes 14680064 | tf_op jit(solution)/shard_map/dot_general | solution.py:308
  558.3 7.9 %convolution_convert_fusion.3 = bf16[1024,2048]{1,0:T(8,128)(2,1)} fusion(bf16[2048,1152]{1,0:T(8,128)(2,1)} %all-gather.4.cloned.1.call-done.both_weight.out_weight, bf16[2048,768]{1,0:T(8,128)(2,1)} %bitcast.233), kind=kOutput, calls=%fused_computation.14 | convolution fusion | flops 3223322624 | bytes 8912896 | tf_op jit(solution)/shard_map/dot_general | solution.py:312
  572.0 4.1 all-to-all-start.1
  578.1 4.3 collective-permute-start.84
  584.9 6.4 convert_add_fusion
  604.9 6.4 collective-permute-done.79
  620.0 12.9 %reduce-scatter.11.cloned.1.call-done = bf16[512,768]{1,0:T(8,128)(2,1)} async-done(((bf16[2048,768]{1,0:T(8,128)(2,1)}), bf16[512,768]{1,0:T(8,128)(2,1)}) %reduce-scatter.11.cloned.1.call-update) | async-done | bytes 786448 | tf_op jit(solution)/shard_map/reduce_scatter | solution.py:79
  632.9 4.2 all-to-all-start.2
  647.0 7.9 %collective-permute-done.89.refs_3_ = bf16[192,768]{1,0:T(8,128)(2,1)S(1)} collective-permute-done((bf16[192,768]{1,0:T(8,128)(2,1)}, bf16[192,768]{1,0:T(8,128)(2,1)S(1)}, u32[]{:S(2)}, u32[]{:S(2)}) %collective-permute-start.89) | collective-permute-done | bytes 294944 | tf_op jit(solution)/shard_map/ppermute | solution.py:40
  656.0 6.7 fusion.10
  666.5 4.2 gates_owner.1
  672.6 8.5 %copy.42 = f32[2,16,171,171]{3,1,2,0:T(8,128)} copy(f32[2,16,171,171]{3,2,1,0:T(8,128)} %get-tuple-element.230) | data formatting | bytes 7485696
  (484 shorter events, 233.6 us)
Async XLA Ops:
  7.2 128.1 %all-gather.4.cloned.1.call-start = ((), (), s32[]{:S(2)}) async-start(), calls=%async_computation.7 | async-start | bytes 5898240 | tf_op jit(solution)/shard_map/all_gather | solution.py:75
  36.7 206.7 %all-gather.6.cloned.1.call-start = ((), (), s32[]{:S(2)}) async-start(), calls=%async_computation.8 | async-start | bytes 7864320 | tf_op jit(solution)/shard_map/all_gather | solution.py:75
  36.7 25.6 %collective-permute-start.1 = (bf16[256,2048]{1,0:T(8,128)(2,1)}, bf16[256,2048]{1,0:T(8,128)(2,1)}, u32[]{:S(2)}, u32[]{:S(2)}) collective-permute-start(bf16[256,2048]{1,0:T(8,128)(2,1)} %bitcast.247), channel_id=1, source_target_pairs={{0,4},{1,5},{2,6},{3,7},{4,0},{5,1},{6,2},{7,3},{8,12},{9,13},{10,... | collective-permute-start | bytes 3145736 | tf_op jit(solution)/shard_map/ppermute | solution.py:40
  38.3 25.9 %collective-permute-start = (bf16[256,2048]{1,0:T(8,128)(2,1)}, bf16[256,2048]{1,0:T(8,128)(2,1)}, u32[]{:S(2)}, u32[]{:S(2)}) collective-permute-start(bf16[256,2048]{1,0:T(8,128)(2,1)} %bitcast.248), channel_id=1, source_target_pairs={{0,2},{1,3},{2,0},{3,1},{4,6},{5,7},{6,4},{7,5},{8,10},{9,11},{10,... | collective-permute-start | bytes 3145736 | tf_op jit(solution)/shard_map/ppermute | solution.py:40
  38.5 45.4 %collective-permute-start.4 = (bf16[256,2048]{1,0:T(8,128)(2,1)}, bf16[256,2048]{1,0:T(8,128)(2,1)}, u32[]{:S(2)}, u32[]{:S(2)}) collective-permute-start(bf16[256,2048]{1,0:T(8,128)(2,1)} %bitcast.249), channel_id=1, source_target_pairs={{0,1},{1,0},{2,3},{3,2},{4,5},{5,4},{6,7},{7,6},{8,9},{9,8},{10,11... | collective-permute-start | bytes 3145736 | tf_op jit(solution)/shard_map/ppermute | solution.py:40
  68.1 21.2 %collective-permute-start.6 = (bf16[256,2048]{1,0:T(8,128)(2,1)}, bf16[256,2048]{1,0:T(8,128)(2,1)S(1)}, u32[]{:S(2)}, u32[]{:S(2)}) collective-permute-start(bf16[256,2048]{1,0:T(8,128)(2,1)} %collective-permute-done.1), channel_id=1, source_target_pairs={{0,1},{1,0},{2,3},{3,2},{4,5},{5,4},{6,7},{7,6},{8,9},{9,8},{10,11... | collective-permute-start | bytes 3145736 | tf_op jit(solution)/shard_map/ppermute | solution.py:40
  99.0 20.4 %collective-permute-start.25 = (bf16[64,2304]{1,0:T(8,128)(2,1)S(1)}, bf16[64,2304]{1,0:T(8,128)(2,1)S(1)}, u32[]{:S(2)}, u32[]{:S(2)}) collective-permute-start(bf16[64,2304]{1,0:T(8,128)(2,1)S(1)} %get-tuple-element.140), channel_id=1, source_target_pairs={{0,7},{1,6},{2,5},{3,4},{4,3},{5,2},{6,1},{7,0},{8,15},{9,14},{10,... | collective-permute-start | bytes 884744 | tf_op jit(solution)/shard_map/ppermute | solution.py:40
  121.5 193.4 %all-gather.8.cloned.1.call-start = ((), (), s32[]{:S(2)}) async-start(), calls=%async_computation.9 | async-start | bytes 3932160 | tf_op jit(solution)/shard_map/all_gather | solution.py:75
  132.4 29.3 %collective-permute-start.26 = (bf16[256,2048]{1,0:T(8,128)(2,1)}, bf16[256,2048]{1,0:T(8,128)(2,1)}, u32[]{:S(2)}, u32[]{:S(2)}) collective-permute-start(bf16[256,2048]{1,0:T(8,128)(2,1)} %bitcast.19), channel_id=1, source_target_pairs={{0,4},{1,5},{2,6},{3,7},{4,0},{5,1},{6,2},{7,3},{8,12},{9,13},{10,... | collective-permute-start | bytes 3145736 | tf_op jit(solution)/shard_map/ppermute | solution.py:40
  134.0 27.7 %collective-permute-start.27 = (bf16[256,2048]{1,0:T(8,128)(2,1)}, bf16[256,2048]{1,0:T(8,128)(2,1)}, u32[]{:S(2)}, u32[]{:S(2)}) collective-permute-start(bf16[256,2048]{1,0:T(8,128)(2,1)} %bitcast.19), channel_id=1, source_target_pairs={{0,2},{1,3},{2,0},{3,1},{4,6},{5,7},{6,4},{7,5},{8,10},{9,11},{10,... | collective-permute-start | bytes 3145736 | tf_op jit(solution)/shard_map/ppermute | solution.py:40
  189.0 20.3 %collective-permute-start.35 = (bf16[128,2048]{1,0:T(8,128)(2,1)}, bf16[128,2048]{1,0:T(8,128)(2,1)}, u32[]{:S(2)}, u32[]{:S(2)}) collective-permute-start(bf16[128,2048]{1,0:T(8,128)(2,1)} %slice.315), channel_id=1, source_target_pairs={{0,2},{1,3},{2,0},{3,1},{4,6},{5,7},{6,4},{7,5},{8,10},{9,11},{10,... | collective-permute-start | bytes 1572872 | tf_op jit(solution)/shard_map/ppermute | solution.py:40
  189.4 21.9 %collective-permute-start.29 = (bf16[128,2048]{1,0:T(8,128)(2,1)}, bf16[128,2048]{1,0:T(8,128)(2,1)S(1)}, u32[]{:S(2)}, u32[]{:S(2)}) collective-permute-start(bf16[128,2048]{1,0:T(8,128)(2,1)} %get-tuple-element.268), channel_id=1, source_target_pairs={{0,4},{1,5},{2,6},{3,7},{4,0},{5,1},{6,2},{7,3},{8,12},{9,13},{10,... | collective-permute-start | bytes 1572872 | tf_op jit(solution)/shard_map/ppermute | solution.py:40
  190.7 28.9 %collective-permute-start.34 = (bf16[128,2048]{1,0:T(8,128)(2,1)}, bf16[128,2048]{1,0:T(8,128)(2,1)S(1)}, u32[]{:S(2)}, u32[]{:S(2)}) collective-permute-start(bf16[128,2048]{1,0:T(8,128)(2,1)} %get-tuple-element.269), channel_id=1, source_target_pairs={{0,2},{1,3},{2,0},{3,1},{4,6},{5,7},{6,4},{7,5},{8,10},{9,11},{10,... | collective-permute-start | bytes 1572872 | tf_op jit(solution)/shard_map/ppermute | solution.py:40
  202.3 27.8 %collective-permute-start.33 = (bf16[128,2048]{1,0:T(8,128)(2,1)}, bf16[128,2048]{1,0:T(8,128)(2,1)S(1)}, u32[]{:S(2)}, u32[]{:S(2)}) collective-permute-start(bf16[128,2048]{1,0:T(8,128)(2,1)} %get-tuple-element.253), channel_id=1, source_target_pairs={{0,2},{1,3},{2,0},{3,1},{4,6},{5,7},{6,4},{7,5},{8,10},{9,11},{10,... | collective-permute-start | bytes 1572872 | tf_op jit(solution)/shard_map/ppermute | solution.py:40
  207.0 249.2 %reduce-scatter.5.cloned.1.call-start = ((), (), s32[]{:S(2)}) async-start(), calls=%async_computation.10 | async-start | bytes 3932160 | tf_op jit(solution)/shard_map/reduce_scatter | solution.py:79
  209.3 29.4 %collective-permute-start.37 = (bf16[256,2048]{1,0:T(8,128)(2,1)}, bf16[256,2048]{1,0:T(8,128)(2,1)S(1)}, u32[]{:S(2)}, u32[]{:S(2)}) collective-permute-start(bf16[256,2048]{1,0:T(8,128)(2,1)} %bitcast.19), channel_id=1, source_target_pairs={{0,1},{1,0},{2,3},{3,2},{4,5},{5,4},{6,7},{7,6},{8,9},{9,8},{10,11... | collective-permute-start | bytes 3145736 | tf_op jit(solution)/shard_map/ppermute | solution.py:40
  211.3 28.6 %collective-permute-start.38 = (bf16[256,2048]{1,0:T(8,128)(2,1)}, bf16[256,2048]{1,0:T(8,128)(2,1)S(1)}, u32[]{:S(2)}, u32[]{:S(2)}) collective-permute-start(bf16[256,2048]{1,0:T(8,128)(2,1)} %collective-permute-done.27), channel_id=1, source_target_pairs={{0,1},{1,0},{2,3},{3,2},{4,5},{5,4},{6,7},{7,6},{8,9},{9,8},{10,11... | collective-permute-start | bytes 3145736 | tf_op jit(solution)/shard_map/ppermute | solution.py:40
  219.5 21.9 %collective-permute-start.39 = (bf16[256,2048]{1,0:T(8,128)(2,1)}, bf16[256,2048]{1,0:T(8,128)(2,1)S(1)}, u32[]{:S(2)}, u32[]{:S(2)}) collective-permute-start(bf16[256,2048]{1,0:T(8,128)(2,1)} %collective-permute-done.26), channel_id=1, source_target_pairs={{0,1},{1,0},{2,3},{3,2},{4,5},{5,4},{6,7},{7,6},{8,9},{9,8},{10,11... | collective-permute-start | bytes 3145736 | tf_op jit(solution)/shard_map/ppermute | solution.py:40
  234.4 24.9 %collective-permute-start.42 = (bf16[256,2048]{1,0:T(8,128)(2,1)}, bf16[256,2048]{1,0:T(8,128)(2,1)S(1)}, u32[]{:S(2)}, u32[]{:S(2)}) collective-permute-start(bf16[256,2048]{1,0:T(8,128)(2,1)} %get-tuple-element.240), channel_id=1, source_target_pairs={{0,4},{1,5},{2,6},{3,7},{4,0},{5,1},{6,2},{7,3},{8,12},{9,13},{10,... | collective-permute-start | bytes 3145736 | tf_op jit(solution)/shard_map/ppermute | solution.py:40
  235.2 24.6 %collective-permute-start.43 = (bf16[256,2048]{1,0:T(8,128)(2,1)}, bf16[256,2048]{1,0:T(8,128)(2,1)S(1)}, u32[]{:S(2)}, u32[]{:S(2)}) collective-permute-start(bf16[256,2048]{1,0:T(8,128)(2,1)} %get-tuple-element.240), channel_id=1, source_target_pairs={{0,2},{1,3},{2,0},{3,1},{4,6},{5,7},{6,4},{7,5},{8,10},{9,11},{10,... | collective-permute-start | bytes 3145736 | tf_op jit(solution)/shard_map/ppermute | solution.py:40
  239.8 23.0 %collective-permute-start.41 = (bf16[128,2048]{1,0:T(8,128)(2,1)}, bf16[128,2048]{1,0:T(8,128)(2,1)}, u32[]{:S(2)}, u32[]{:S(2)}) collective-permute-start(bf16[128,2048]{1,0:T(8,128)(2,1)} %collective-permute-done.36), channel_id=1, source_target_pairs={{0,1},{1,0},{2,3},{3,2},{4,5},{5,4},{6,7},{7,6},{8,9},{9,8},{10,11... | collective-permute-start | bytes 1572872 | tf_op jit(solution)/shard_map/ppermute | solution.py:40
  243.3 32.0 %collective-permute-start.46 = (bf16[256,2048]{1,0:T(8,128)(2,1)}, bf16[256,2048]{1,0:T(8,128)(2,1)S(1)}, u32[]{:S(2)}, u32[]{:S(2)}) collective-permute-start(bf16[256,2048]{1,0:T(8,128)(2,1)} %get-tuple-element.240), channel_id=1, source_target_pairs={{0,1},{1,0},{2,3},{3,2},{4,5},{5,4},{6,7},{7,6},{8,9},{9,8},{10,11... | collective-permute-start | bytes 3145736 | tf_op jit(solution)/shard_map/ppermute | solution.py:40
  322.4 180.8 %reduce-scatter.7.cloned.1.call-start = ((), (), s32[]{:S(2)}) async-start(), calls=%async_computation.11 | async-start | bytes 7864320 | tf_op jit(solution)/shard_map/reduce_scatter | solution.py:79
  350.0 21.7 %collective-permute-start.52 = (bf16[128,2048]{1,0:T(8,128)(2,1)}, bf16[128,2048]{1,0:T(8,128)(2,1)S(1)}, u32[]{:S(2)}, u32[]{:S(2)}) collective-permute-start(bf16[128,2048]{1,0:T(8,128)(2,1)} %get-tuple-element.267), channel_id=1, source_target_pairs={{0,2},{1,3},{2,0},{3,1},{4,6},{5,7},{6,4},{7,5},{8,10},{9,11},{10,... | collective-permute-start | bytes 1572872 | tf_op jit(solution)/shard_map/ppermute | solution.py:40
  350.0 22.5 %collective-permute-start.53 = (bf16[128,2048]{1,0:T(8,128)(2,1)S(1)}, bf16[128,2048]{1,0:T(8,128)(2,1)}, u32[]{:S(2)}, u32[]{:S(2)}) collective-permute-start(bf16[128,2048]{1,0:T(8,128)(2,1)S(1)} %get-tuple-element.266), channel_id=1, source_target_pairs={{0,4},{1,5},{2,6},{3,7},{4,0},{5,1},{6,2},{7,3},{8,12},{9,13},{10,... | collective-permute-start | bytes 1572872 | tf_op jit(solution)/shard_map/ppermute | solution.py:40
  351.2 23.9 %collective-permute-start.54 = (bf16[128,2048]{1,0:T(8,128)(2,1)S(1)}, bf16[128,2048]{1,0:T(8,128)(2,1)S(1)}, u32[]{:S(2)}, u32[]{:S(2)}) collective-permute-start(bf16[128,2048]{1,0:T(8,128)(2,1)S(1)} %get-tuple-element.265), channel_id=1, source_target_pairs={{0,4},{1,5},{2,6},{3,7},{4,0},{5,1},{6,2},{7,3},{8,12},{9,13},{10,... | collective-permute-start | bytes 1572872 | tf_op jit(solution)/shard_map/ppermute | solution.py:40
  352.1 23.1 %collective-permute-start.55 = (bf16[128,2048]{1,0:T(8,128)(2,1)S(1)}, bf16[128,2048]{1,0:T(8,128)(2,1)S(1)}, u32[]{:S(2)}, u32[]{:S(2)}) collective-permute-start(bf16[128,2048]{1,0:T(8,128)(2,1)S(1)} %get-tuple-element.264), channel_id=1, source_target_pairs={{0,2},{1,3},{2,0},{3,1},{4,6},{5,7},{6,4},{7,5},{8,10},{9,11},{10,... | collective-permute-start | bytes 1572872 | tf_op jit(solution)/shard_map/ppermute | solution.py:40
  386.3 160.7 %reduce-scatter.9.cloned.1.call-start = ((), (), s32[]{:S(2)}) async-start(), calls=%async_computation.12 | async-start | bytes 1966080 | tf_op jit(solution)/shard_map/reduce_scatter | solution.py:79
  416.5 25.2 %collective-permute-start.59 = (bf16[128,2048]{1,0:T(8,128)(2,1)S(1)}, bf16[128,2048]{1,0:T(8,128)(2,1)S(1)}, u32[]{:S(2)}, u32[]{:S(2)}) collective-permute-start(bf16[128,2048]{1,0:T(8,128)(2,1)S(1)} %get-tuple-element.260), channel_id=1, source_target_pairs={{0,4},{1,5},{2,6},{3,7},{4,0},{5,1},{6,2},{7,3},{8,12},{9,13},{10,... | collective-permute-start | bytes 1572872 | tf_op jit(solution)/shard_map/ppermute | solution.py:40
  417.7 24.1 %collective-permute-start.64 = (bf16[128,2048]{1,0:T(8,128)(2,1)S(1)}, bf16[128,2048]{1,0:T(8,128)(2,1)S(1)}, u32[]{:S(2)}, u32[]{:S(2)}) collective-permute-start(bf16[128,2048]{1,0:T(8,128)(2,1)S(1)} %get-tuple-element.261), channel_id=1, source_target_pairs={{0,2},{1,3},{2,0},{3,1},{4,6},{5,7},{6,4},{7,5},{8,10},{9,11},{10,... | collective-permute-start | bytes 1572872 | tf_op jit(solution)/shard_map/ppermute | solution.py:40
  430.9 20.3 %collective-permute-start.61 = (bf16[128,2048]{1,0:T(8,128)(2,1)S(1)}, bf16[128,2048]{1,0:T(8,128)(2,1)S(1)}, u32[]{:S(2)}, u32[]{:S(2)}) collective-permute-start(bf16[128,2048]{1,0:T(8,128)(2,1)S(1)} %get-tuple-element.248), channel_id=1, source_target_pairs={{0,4},{1,5},{2,6},{3,7},{4,0},{5,1},{6,2},{7,3},{8,12},{9,13},{10,... | collective-permute-start | bytes 1572872 | tf_op jit(solution)/shard_map/ppermute | solution.py:40
  431.8 19.3 %collective-permute-start.63 = (bf16[128,2048]{1,0:T(8,128)(2,1)S(1)}, bf16[128,2048]{1,0:T(8,128)(2,1)S(1)}, u32[]{:S(2)}, u32[]{:S(2)}) collective-permute-start(bf16[128,2048]{1,0:T(8,128)(2,1)S(1)} %get-tuple-element.249), channel_id=1, source_target_pairs={{0,2},{1,3},{2,0},{3,1},{4,6},{5,7},{6,4},{7,5},{8,10},{9,11},{10,... | collective-permute-start | bytes 1572872 | tf_op jit(solution)/shard_map/ppermute | solution.py:40
  456.2 23.5 %collective-permute-start.66 = (bf16[256,2048]{1,0:T(8,128)(2,1)S(1)}, bf16[256,2048]{1,0:T(8,128)(2,1)S(1)}, u32[]{:S(2)}, u32[]{:S(2)}) collective-permute-start(bf16[256,2048]{1,0:T(8,128)(2,1)S(1)} %get-tuple-element.178), channel_id=1, source_target_pairs={{0,4},{1,5},{2,6},{3,7},{4,0},{5,1},{6,2},{7,3},{8,12},{9,13},{10,... | collective-permute-start | bytes 3145736 | tf_op jit(solution)/shard_map/ppermute | solution.py:40
  457.1 23.5 %collective-permute-start.65 = (bf16[256,2048]{1,0:T(8,128)(2,1)S(1)}, bf16[256,2048]{1,0:T(8,128)(2,1)S(1)}, u32[]{:S(2)}, u32[]{:S(2)}) collective-permute-start(bf16[256,2048]{1,0:T(8,128)(2,1)S(1)} %get-tuple-element.178), channel_id=1, source_target_pairs={{0,2},{1,3},{2,0},{3,1},{4,6},{5,7},{6,4},{7,5},{8,10},{9,11},{10,... | collective-permute-start | bytes 3145736 | tf_op jit(solution)/shard_map/ppermute | solution.py:40
  457.7 34.4 %collective-permute-start.69 = (bf16[256,2048]{1,0:T(8,128)(2,1)S(1)}, bf16[256,2048]{1,0:T(8,128)(2,1)S(1)}, u32[]{:S(2)}, u32[]{:S(2)}) collective-permute-start(bf16[256,2048]{1,0:T(8,128)(2,1)S(1)} %get-tuple-element.178), channel_id=1, source_target_pairs={{0,1},{1,0},{2,3},{3,2},{4,5},{5,4},{6,7},{7,6},{8,9},{9,8},{10,11... | collective-permute-start | bytes 3145736 | tf_op jit(solution)/shard_map/ppermute | solution.py:40
  506.3 40.7 %all-to-all-start = ((bf16[8,64,2304]{2,1,0:T(8,128)(2,1)}), bf16[8,64,2304]{2,1,0:T(8,128)(2,1)S(1)}, u32[]{:S(2)}, u32[]{:S(2)}) async-start(bf16[8,64,2304]{2,1,0:T(8,128)(2,1)} %bitcast.251), calls=%async_computation.3 | async-start | bytes 4718592 | tf_op jit(solution)/shard_map/all_to_all | solution.py:102
  509.9 123.0 %reduce-scatter.11.cloned.1.call-start = ((), (), s32[]{:S(2)}) async-start(), calls=%async_computation.13 | async-start | bytes 3932160 | tf_op jit(solution)/shard_map/reduce_scatter | solution.py:79
  566.2 18.7 %collective-permute-start.77 = (bf16[1024,2048]{1,0:T(8,128)(2,1)}, bf16[1024,2048]{1,0:T(8,128)(2,1)}, u32[]{:S(2)}, u32[]{:S(2)}) collective-permute-start(bf16[1024,2048]{1,0:T(8,128)(2,1)} %convolution_convert_fusion.3), channel_id=1, source_target_pairs={{0,1},{1,0},{2,3},{3,2},{4,5},{5,4},{6,7},{7,6},{8,9},{9,8},{10,11... | collective-permute-start | bytes 12582920 | tf_op jit(solution)/shard_map/ppermute | solution.py:40
  572.0 30.3 %all-to-all-start.1 = ((bf16[8,64,384]{2,1,0:T(8,128)(2,1)}), bf16[8,64,384]{2,1,0:T(8,128)(2,1)}, u32[]{:S(2)}, u32[]{:S(2)}) async-start(bf16[8,64,384]{2,1,0:T(8,128)(2,1)} %bitcast.80), calls=%async_computation.4 | async-start | bytes 786432 | tf_op jit(solution)/shard_map/all_to_all | solution.py:102
  578.1 21.5 %collective-permute-start.84 = (bf16[48,768]{1,0:T(8,128)(2,1)S(1)}, bf16[48,768]{1,0:T(8,128)(2,1)S(1)}, u32[]{:S(2)}, u32[]{:S(2)}) collective-permute-start(bf16[48,768]{1,0:T(8,128)(2,1)S(1)} %fusion.54), channel_id=1, source_target_pairs={{0,8},{1,9},{2,10},{3,11},{4,12},{5,13},{6,14},{7,15},{8,16},{9,17... | collective-permute-start | bytes 221192 | tf_op jit(solution)/shard_map/ppermute | solution.py:46
  582.4 18.6 %collective-permute-start.85 = (bf16[48,768]{1,0:T(8,128)(2,1)S(1)}, bf16[48,768]{1,0:T(8,128)(2,1)S(1)}, u32[]{:S(2)}, u32[]{:S(2)}) collective-permute-start(bf16[48,768]{1,0:T(8,128)(2,1)S(1)} %fusion.54), channel_id=1, source_target_pairs={{0,16},{1,17},{2,18},{3,19},{4,20},{5,21},{6,22},{7,23},{8,24},{9,... | collective-permute-start | bytes 221192 | tf_op jit(solution)/shard_map/ppermute | solution.py:46
  582.4 19.2 %collective-permute-start.86 = (bf16[48,768]{1,0:T(8,128)(2,1)S(1)}, bf16[48,768]{1,0:T(8,128)(2,1)S(1)}, u32[]{:S(2)}, u32[]{:S(2)}) collective-permute-start(bf16[48,768]{1,0:T(8,128)(2,1)S(1)} %fusion.54), channel_id=1, source_target_pairs={{0,24},{1,25},{2,26},{3,27},{4,28},{5,29},{6,30},{7,31},{8,0},{9,1... | collective-permute-start | bytes 221192 | tf_op jit(solution)/shard_map/ppermute | solution.py:46
  602.8 40.8 %collective-permute-start.78 = (bf16[128,2048]{1,0:T(8,128)(2,1)}, bf16[128,2048]{1,0:T(8,128)(2,1)}, u32[]{:S(2)}, u32[]{:S(2)}) collective-permute-start(bf16[128,2048]{1,0:T(8,128)(2,1)} %get-tuple-element.259), channel_id=1, source_target_pairs={{0,4},{1,5},{2,6},{3,7},{4,0},{5,1},{6,2},{7,3},{8,12},{9,13},{10,... | collective-permute-start | bytes 1572872 | tf_op jit(solution)/shard_map/ppermute | solution.py:40
  604.3 39.3 %collective-permute-start.83 = (bf16[128,2048]{1,0:T(8,128)(2,1)}, bf16[128,2048]{1,0:T(8,128)(2,1)}, u32[]{:S(2)}, u32[]{:S(2)}) collective-permute-start(bf16[128,2048]{1,0:T(8,128)(2,1)} %get-tuple-element.257), channel_id=1, source_target_pairs={{0,2},{1,3},{2,0},{3,1},{4,6},{5,7},{6,4},{7,5},{8,10},{9,11},{10,... | collective-permute-start | bytes 1572872 | tf_op jit(solution)/shard_map/ppermute | solution.py:40
  616.5 27.2 %collective-permute-start.80 = (bf16[128,2048]{1,0:T(8,128)(2,1)}, bf16[128,2048]{1,0:T(8,128)(2,1)}, u32[]{:S(2)}, u32[]{:S(2)}) collective-permute-start(bf16[128,2048]{1,0:T(8,128)(2,1)} %get-tuple-element.247), channel_id=1, source_target_pairs={{0,4},{1,5},{2,6},{3,7},{4,0},{5,1},{6,2},{7,3},{8,12},{9,13},{10,... | collective-permute-start | bytes 1572872 | tf_op jit(solution)/shard_map/ppermute | solution.py:40
  618.0 25.7 %collective-permute-start.82 = (bf16[128,2048]{1,0:T(8,128)(2,1)}, bf16[128,2048]{1,0:T(8,128)(2,1)}, u32[]{:S(2)}, u32[]{:S(2)}) collective-permute-start(bf16[128,2048]{1,0:T(8,128)(2,1)} %get-tuple-element.246), channel_id=1, source_target_pairs={{0,2},{1,3},{2,0},{3,1},{4,6},{5,7},{6,4},{7,5},{8,10},{9,11},{10,... | collective-permute-start | bytes 1572872 | tf_op jit(solution)/shard_map/ppermute | solution.py:40
  619.7 22.1 %collective-permute-start.88 = (bf16[192,768]{1,0:T(8,128)(2,1)}, bf16[192,768]{1,0:T(8,128)(2,1)}, u32[]{:S(2)}, u32[]{:S(2)}) collective-permute-start(bf16[192,768]{1,0:T(8,128)(2,1)} %bitcast.79.refs_0_), channel_id=1, source_target_pairs={{0,2},{1,3},{2,0},{3,1},{4,6},{5,7},{6,4},{7,5},{8,10},{9,11},{10,... | collective-permute-start | bytes 884744 | tf_op jit(solution)/shard_map/ppermute | solution.py:40
  632.9 22.1 %all-to-all-start.2 = ((bf16[8,64,768]{2,1,0:T(8,128)(2,1)}), bf16[8,64,768]{2,1,0:T(8,128)(2,1)}, u32[]{:S(2)}, u32[]{:S(2)}) async-start(bf16[8,64,768]{2,1,0:T(8,128)(2,1)} %bitcast.261), calls=%async_computation.6 | async-start | bytes 1572864 | tf_op jit(solution)/shard_map/all_to_all | solution.py:102
  (133 other events, 1934.6 us)
Sparse Core Ops, SparseCore 0:
  36.8 89.9 all-gather.3
  129.0 113.6 all-gather.5
  244.8 61.7 all-gather.7
  322.5 60.1 reduce-scatter.4
  386.4 111.5 reduce-scatter.6
  503.3 35.3 reduce-scatter.8
  566.7 66.2 reduce-scatter.10

commit v6 on v5

--- a/solution.py
+++ b/solution.py
@@ -896,7 +896,8 @@
     packed = ring_stack(packed, turn, groups).reshape(PAD, 2 * WIDE)
     packed, out_grads = lax.optimization_barrier((packed, out_grads))
     across, along = lax.optimization_barrier((swap(packed, 4), swap(packed, 2)))
-    near = [packed, along, across, swap(across, 2)]
+    beyond = [swap(across[: PAD // 2], 2), swap(along[PAD // 2 :], 4)]
+    near = [packed, along, across, jnp.concatenate(beyond, axis=0)]
     near, both_grads = lax.optimization_barrier((near, both_grads))
     grad_gblocks, small = simple_call(
         gates_owner_kernel,

time: 696 us -> 702 us (level)
    reduce_scatter x4, waiting for transfers between devices: 12.9 us -> 0.03 us  [ring_reduce(): lax.psum_scatter(values, AXES, scatter_dimension=0, tiled=True, axis_inde...]
    ppermute x85 -> x86, waiting for transfers between devices: 199 us -> 209 us  [swap(): lax.ppermute(values, AXES, [(i, i ^ bit) for i in range(device_count())])]
    unnamed x192 -> x194, local copies, waits for them, and re-layouts: 74.7 us -> 75.4 us
    ppermute x85 -> x86, starting transfers between devices: 66.7 us -> 66.3 us  [swap(): lax.ppermute(values, AXES, [(i, i ^ bit) for i in range(device_count())])]
  transfers between devices with their start and end apart: 104 -> 105, of which waited for: 42 -> 42; matrix products, arithmetic and copies ran while one was open for 31% -> 31% of each run, Pallas kernels for 11% -> 11%
where the time goes in v6:
time: 702 us; the launch traced here: 696 us
  waiting for transfers between devices  218 us (31%)
  matrix products  134 us (19%)
  local copies, waits for them, and re-layouts  102 us (15%)
  starting transfers between devices  95.8 us (14%)
  Pallas kernels  81.3 us (12%)
  other arithmetic  47.7 us (7%)
  between operations  15.8 us (2%)
    ppermute x86, waiting for transfers between devices, swap(): lax.ppermute(values, AXES, [(i, i ^ bit) for i in range(device_count())])  209 us
    unnamed x194, local copies, waits for them, and re-layouts  75.4 us
    ppermute x86, starting transfers between devices, swap(): lax.ppermute(values, AXES, [(i, i ^ bit) for i in range(device_count())])  66.3 us
    dot_general x8, matrix products, contract_cols(): lax.dot_general(left, right, (((1,), (1,)), ((), ())), preferred_element_...  60.2 us
    dot_general x4, matrix products, contract_rows(): lax.dot_general(left, right, (((0,), (0,)), ((), ())), preferred_element_...  45.2 us
    pallas_call x1, Pallas kernels, local(): mixer_backward(where, pre, pre, segments, segments, state, state, middle_...  33.5 us
    dot_general x2, matrix products, product(): return jnp.dot(left, right, preferred_element_type=F32)  29 us
    pallas_call x1, Pallas kernels, local(): mixer_forward(where, normed_blocks, segments, mixer_weight, gate_weight,...  26 us
  transfers between devices with their start and end apart: 105, of which 42 were waited for; matrix products, arithmetic and copies ran while one was open for 31% of the time, Pallas kernels for 11%

profile of v6, /device:TPU:0, one launch (start us, length us, event | category | flops | bytes accessed | tf_op | source)
XLA Modules:
  0.0 695.6 jit_solution(14165025301141098007)
XLA Ops:
  26.0 5.7 collective-permute-done.14.refs_6_
  31.6 3.9 collective-permute-done.15.refs_7_
  53.5 8.8 %collective-permute-done.1 = bf16[256,2048]{1,0:T(8,128)(2,1)} collective-permute-done((bf16[256,2048]{1,0:T(8,128)(2,1)}, bf16[256,2048]{1,0:T(8,128)(2,1)}, u32[]{:S(2)}, u32[]{:S(2)}) %collective-permute-start.1) | collective-permute-done | bytes 1048608 | tf_op jit(solution)/shard_map/ppermute | solution.py:40
  73.3 4.3 collective-permute-done.2
  92.0 4.2 collective-permute-done.20.refs_2_
  101.8 3.9 collective-permute-done.23.refs_5_
  105.7 8.5 %collective-permute-done.24.refs_6_ = bf16[64,2304]{1,0:T(8,128)(2,1)S(1)} collective-permute-done((bf16[64,2304]{1,0:T(8,128)(2,1)S(1)}, bf16[64,2304]{1,0:T(8,128)(2,1)S(1)}, u32[]{:S(2)}, u32[]{:S(2)}) %collective-permute-start.24) | collective-permute-done | bytes 294944 | tf_op jit(solution)/shard_map/ppermute | solution.py:40
  114.1 5.2 collective-permute-done.25.refs_7_
  122.2 10.2 %norm_rows.1 = bf16[2048,2048]{1,0:T(8,128)(2,1)} custom-call(bf16[2048,2048]{1,0:T(8,128)(2,1)} %constant_dynamic-update-slice_fusion.values, f32[1,2048]{1,0:T(1,128)S(1)} %reshape.460.gain), custom_call_target="tpu_custom_call" | custom-call | flops 1 | bytes 1 | tf_op jit(solution)/shard_map/norm_rows/pallas_call | solution.py:177
  135.6 26.0 %mixer_forward.1 = (f32[8,256,768]{2,1,0:T(8,128)}, f32[8,256,384]{2,1,0:T(8,128)}, bf16[8,256,384]{2,1,0:T(8,128)(2,1)S(1)}) custom-call(s32[1]{0:T(128)} %bitcast.1.place, bf16[8,256,2048]{2,1,0:T(8,128)(2,1)} %bitcast.252, f32[8,256,128]{2,1,0:T(8,128)S(1)} %broadcast_in_dim.71.segment.segment_rim, ...), custom_call_target="tpu_custom_call" | custom-call | flops 7650410496 | bytes 11010048 | tf_op jit(solution)/shard_map/mixer_forward/pallas_call | solution.py:811
  161.7 4.3 convolution_convert_fusion.2
  166.3 7.0 %collective-permute-done.28 = bf16[1024,2048]{1,0:T(8,128)(2,1)S(1)} collective-permute-done((bf16[1024,2048]{1,0:T(8,128)(2,1)S(1)}, bf16[1024,2048]{1,0:T(8,128)(2,1)S(1)}, u32[]{:S(2)}, u32[]{:S(2)}) %collective-permute-start.28) | collective-permute-done | bytes 4194336 | tf_op jit(solution)/shard_map/ppermute | solution.py:40
  173.3 3.8 convert_add_fusion.3
  192.5 4.5 collective-permute-done.30
  211.8 7.8 %collective-permute-done.34 = bf16[128,2048]{1,0:T(8,128)(2,1)S(1)} collective-permute-done((bf16[128,2048]{1,0:T(8,128)(2,1)}, bf16[128,2048]{1,0:T(8,128)(2,1)S(1)}, u32[]{:S(2)}, u32[]{:S(2)}) %collective-permute-start.34) | collective-permute-done | bytes 524320 | tf_op jit(solution)/shard_map/ppermute | solution.py:40
  221.0 9.1 %collective-permute-done.33 = bf16[128,2048]{1,0:T(8,128)(2,1)S(1)} collective-permute-done((bf16[128,2048]{1,0:T(8,128)(2,1)}, bf16[128,2048]{1,0:T(8,128)(2,1)S(1)}, u32[]{:S(2)}, u32[]{:S(2)}) %collective-permute-start.33) | collective-permute-done | bytes 524320 | tf_op jit(solution)/shard_map/ppermute | solution.py:40
  243.3 15.9 %collective-permute-done.42 = bf16[256,2048]{1,0:T(8,128)(2,1)S(1)} collective-permute-done((bf16[256,2048]{1,0:T(8,128)(2,1)}, bf16[256,2048]{1,0:T(8,128)(2,1)S(1)}, u32[]{:S(2)}, u32[]{:S(2)}) %collective-permute-start.42) | collective-permute-done | bytes 1048608 | tf_op jit(solution)/shard_map/ppermute | solution.py:40
  267.4 4.8 collective-permute-done.44
  280.2 15.7 %fusion.74 = f32[2048,1536]{1,0:T(8,128)S(1)} fusion(bf16[2048,2048]{1,0:T(8,128)(2,1)} %constant_dynamic-update-slice_fusion.20, bf16[2048,1536]{1,0:T(8,128)(2,1)S(1)} %bitcast.268), kind=kOutput, calls=%fused_computation.206 | convolution fusion | flops 12884901888 | bytes 27262976 | tf_op jit(solution)/shard_map/dot_general | solution.py:304
  296.0 7.1 %add_multiply_fusion = (f32[2048,768]{1,0:T(8,128)}, bf16[2048,768]{1,0:T(8,128)(2,1)S(1)}, f32[2048,768]{1,0:T(8,128)}) fusion(f32[2048,1536]{1,0:T(8,128)S(1)} %fusion.74), kind=kLoop, calls=%fused_computation.8 | loop fusion | flops 31457280 | bytes 28311552 | tf_op jit(solution)/shard_map/mul | solution.py:828
  304.4 10.6 %convolution_convert_fusion.6 = bf16[2048,768]{1,0:T(8,128)(2,1)} fusion(bf16[2048,2048]{1,0:T(8,128)(2,1)} %constant_dynamic-update-slice_fusion.10, bf16[2048,768]{1,0:T(8,128)(2,1)S(1)} %get-tuple-element.159), kind=kOutput, calls=%fused_computation.17 | convolution fusion | flops 6444023808 | bytes 14680064 | tf_op jit(solution)/shard_map/dot_general | solution.py:308
  315.0 6.9 convolution_convert_fusion.4
  322.5 13.2 %multiply_convert_fusion.1 = (bf16[2048,768]{1,0:T(8,128)(2,1)S(1)}, bf16[2048,768]{1,0:T(8,128)(2,1)S(1)}) fusion(f32[2048,768]{1,0:T(8,128)} %get-tuple-element.164, f32[2048,768]{1,0:T(8,128)} %get-tuple-element.165, bf16[2048,2048]{1,0:T(8,128)(2,1)} %constant_dynamic-update-slice_fusion.10, bf16[2048,768]{1,0:T(8,128)(2,1)} %all-gather.8.cloned.1.call-done), kind=kOutput, calls=%fused_computation.7 | convolution fusion | flops 6448742400 | bytes 30408704 | tf_op jit(solution)/shard_map/dot_general | solution.py:304
  336.2 9.4 %convert_add_fusion.2 = f32[1024,2048]{1,0:T(8,128)S(1)} fusion(bf16[1024,2048]{1,0:T(8,128)(2,1)} %collective-permute-done.51, bf16[1024,768]{1,0:T(8,128)(2,1)} %get-tuple-element.166, bf16[2048,768]{1,0:T(8,128)(2,1)} %all-gather.8.cloned.1.call-done), kind=kOutput, calls=%fused_computation.2 | convolution fusion | flops 3225419776 | bytes 17301504 | tf_op jit(solution)/shard_map/dot_general | solution.py:312
  353.9 17.7 %convolution_convert_fusion = bf16[2048,1536]{1,0:T(8,128)(2,1)} fusion(bf16[2048,2048]{1,0:T(8,128)(2,1)} %constant_dynamic-update-slice_fusion.20, bf16[2048,1536]{1,0:T(8,128)(2,1)S(1)} %pad_maximum_fusion), kind=kOutput, calls=%fused_computation.4 | convolution fusion | flops 12888047616 | bytes 20971520 | tf_op jit(solution)/shard_map/dot_general | solution.py:308
  375.2 11.1 %convolution_convert_fusion.1 = bf16[1024,2048]{1,0:T(8,128)(2,1)} fusion(bf16[2048,1536]{1,0:T(8,128)(2,1)} %all-gather.6.cloned.1.call-done, bf16[2048,1536]{1,0:T(8,128)(2,1)} %copy-done.48), kind=kOutput, calls=%fused_computation.12 | convolution fusion | flops 6444548096 | bytes 13631488 | tf_op jit(solution)/shard_map/dot_general | solution.py:312
  388.9 11.9 %collective-permute-done.56 = bf16[128,2048]{1,0:T(8,128)(2,1)S(1)} collective-permute-done((bf16[128,2048]{1,0:T(8,128)(2,1)S(1)}, bf16[128,2048]{1,0:T(8,128)(2,1)S(1)}, u32[]{:S(2)}, u32[]{:S(2)}) %collective-permute-start.56) | collective-permute-done | bytes 524320 | tf_op jit(solution)/shard_map/ppermute | solution.py:40
  403.6 9.8 %convert_add_fusion.1 = f32[1024,2048]{1,0:T(8,128)S(1)} fusion(bf16[1024,2048]{1,0:T(8,128)(2,1)} %collective-permute-done.58, bf16[1024,1536]{1,0:T(8,128)(2,1)S(1)} %slice-done, bf16[2048,1536]{1,0:T(8,128)(2,1)} %all-gather.6.cloned.1.call-done), kind=kOutput, calls=%fused_computation.1 | convolution fusion | flops 6446645248 | bytes 22020096 | tf_op jit(solution)/shard_map/dot_general | solution.py:312
  418.3 10.8 %collective-permute-done.60 = bf16[128,2048]{1,0:T(8,128)(2,1)S(1)} collective-permute-done((bf16[128,2048]{1,0:T(8,128)(2,1)S(1)}, bf16[128,2048]{1,0:T(8,128)(2,1)S(1)}, u32[]{:S(2)}, u32[]{:S(2)}) %collective-permute-start.60) | collective-permute-done | bytes 524320 | tf_op jit(solution)/shard_map/ppermute | solution.py:40
  432.5 9.3 %collective-permute-done.59 = bf16[128,2048]{1,0:T(8,128)(2,1)S(1)} collective-permute-done((bf16[128,2048]{1,0:T(8,128)(2,1)S(1)}, bf16[128,2048]{1,0:T(8,128)(2,1)S(1)}, u32[]{:S(2)}, u32[]{:S(2)}) %collective-permute-start.59) | collective-permute-done | bytes 524320 | tf_op jit(solution)/shard_map/ppermute | solution.py:40
  441.8 9.4 %collective-permute-done.61 = bf16[128,2048]{1,0:T(8,128)(2,1)S(1)} collective-permute-done((bf16[128,2048]{1,0:T(8,128)(2,1)S(1)}, bf16[128,2048]{1,0:T(8,128)(2,1)S(1)}, u32[]{:S(2)}, u32[]{:S(2)}) %collective-permute-start.61) | collective-permute-done | bytes 524320 | tf_op jit(solution)/shard_map/ppermute | solution.py:40
  452.2 4.0 fusion.12
  457.8 21.9 %collective-permute-done.66 = bf16[256,2048]{1,0:T(8,128)(2,1)S(1)} collective-permute-done((bf16[256,2048]{1,0:T(8,128)(2,1)S(1)}, bf16[256,2048]{1,0:T(8,128)(2,1)S(1)}, u32[]{:S(2)}, u32[]{:S(2)}) %collective-permute-start.66) | collective-permute-done | bytes 1048608 | tf_op jit(solution)/shard_map/ppermute | solution.py:40
  482.9 8.6 %collective-permute-done.67 = bf16[128,2048]{1,0:T(8,128)(2,1)S(1)} collective-permute-done((bf16[128,2048]{1,0:T(8,128)(2,1)S(1)}, bf16[128,2048]{1,0:T(8,128)(2,1)S(1)}, u32[]{:S(2)}, u32[]{:S(2)}) %collective-permute-start.67) | collective-permute-done | bytes 524320 | tf_op jit(solution)/shard_map/ppermute | solution.py:40
  497.5 5.6 convolution_convert_fusion.7
  506.3 3.6 all-to-all-start
  511.1 33.5 %mixer_backward.1 = (bf16[8,256,768]{2,1,0:T(8,128)(2,1)S(1)}, bf16[192,768]{1,0:T(8,128)(2,1)S(1)}) custom-call(s32[1]{0:T(128)} %bitcast.1.place, f32[8,256,768]{2,1,0:T(8,128)} %get-tuple-element.176.pre.rim, f32[8,256,768]{2,1,0:T(8,128)} %get-tuple-element.176.pre.rim, f32[8,256,128]{2,1,0:T(8,128)S(1)} %copy-done.3, f32[8,256,128]{2,1,0:T(8,128)S(1)} %copy-done.3, ...), custom_call_target="tpu_custom_call" | custom-call | flops 6845104128 | bytes 18874368 | tf_op jit(solution)/shard_map/mixer_backward/pallas_call | solution.py:864
  546.9 11.4 %convolution_convert_fusion.5 = bf16[2048,768]{1,0:T(8,128)(2,1)} fusion(bf16[2048,2048]{1,0:T(8,128)(2,1)} %norm_rows.1, bf16[2048,768]{1,0:T(8,128)(2,1)} %bitcast.232), kind=kOutput, calls=%fused_computation.16 | convolution fusion | flops 6444023808 | bytes 14680064 | tf_op jit(solution)/shard_map/dot_general | solution.py:308
  558.3 7.9 %convolution_convert_fusion.3 = bf16[1024,2048]{1,0:T(8,128)(2,1)} fusion(bf16[2048,1152]{1,0:T(8,128)(2,1)} %all-gather.4.cloned.1.call-done.both_weight.out_weight, bf16[2048,768]{1,0:T(8,128)(2,1)} %bitcast.233), kind=kOutput, calls=%fused_computation.14 | convolution fusion | flops 3223322624 | bytes 8912896 | tf_op jit(solution)/shard_map/dot_general | solution.py:312
  579.4 3.9 collective-permute-start.84
  583.2 4.6 all-to-all-start.1
  591.7 7.1 %convert_add_fusion = f32[1024,2048]{1,0:T(8,128)S(1)} fusion(bf16[1024,2048]{1,0:T(8,128)(2,1)} %collective-permute-done.77, bf16[1024,768]{1,0:T(8,128)(2,1)} %slice.350, bf16[2048,1152]{1,0:T(8,128)(2,1)} %all-gather.4.cloned.1.call-done.both_weight.out_weight), kind=kOutput, calls=%fused_computation | convolution fusion | flops 3225419776 | bytes 17301504 | tf_op jit(solution)/shard_map/dot_general | solution.py:312
  608.8 16.4 %collective-permute-done.87.refs_2_ = bf16[192,768]{1,0:T(8,128)(2,1)S(1)} collective-permute-done((bf16[192,768]{1,0:T(8,128)(2,1)}, bf16[192,768]{1,0:T(8,128)(2,1)S(1)}, u32[]{:S(2)}, u32[]{:S(2)}) %collective-permute-start.87) | collective-permute-done | bytes 294944 | tf_op jit(solution)/shard_map/ppermute | solution.py:40
  641.4 3.5 all-to-all-start.2
  645.0 10.9 %collective-permute-done.90 = bf16[96,768]{1,0:T(8,128)(2,1)} collective-permute-done((bf16[96,768]{1,0:T(8,128)(2,1)}, bf16[96,768]{1,0:T(8,128)(2,1)}, u32[]{:S(2)}, u32[]{:S(2)}) %collective-permute-start.90) | collective-permute-done | bytes 147488 | tf_op jit(solution)/shard_map/ppermute | solution.py:40
  662.9 7.0 %fusion.10 = bf16[1,256,2048]{2,1,0:T(8,128)(2,1)} fusion(bf16[1,256,2048]{2,1,0:T(8,128)(2,1)} %param.20, bf16[1,256,2048]{2,1,0:T(8,128)(2,1)} %param.18, f32[1024,2048]{1,0:T(8,128)} %copy-done.45, f32[1024,2048]{1,0:T(8,128)} %copy-done.42, f32[1024,2048]{1,0:T(8,128)} %copy-done.41, bf16[1,128,2048]{2,1,0:T(8,128)(2,1)} %bitcast.255, ...), kind=kLoop, calls=%fused_computation.33 | loop fusion | flops 25165824 | bytes 15749120 | tf_op jit(solution)/shard_map/convert_element_type | solution.py:50
  673.4 4.1 gates_owner.1
  679.4 8.5 %copy.42 = f32[2,16,171,171]{3,1,2,0:T(8,128)} copy(f32[2,16,171,171]{3,2,1,0:T(8,128)} %get-tuple-element.230) | data formatting | bytes 7485696
  (491 shorter events, 236.5 us)
Async XLA Ops:
  7.2 128.1 %all-gather.4.cloned.1.call-start = ((), (), s32[]{:S(2)}) async-start(), calls=%async_computation.7 | async-start | bytes 5898240 | tf_op jit(solution)/shard_map/all_gather | solution.py:75
  36.7 206.6 %all-gather.6.cloned.1.call-start = ((), (), s32[]{:S(2)}) async-start(), calls=%async_computation.8 | async-start | bytes 7864320 | tf_op jit(solution)/shard_map/all_gather | solution.py:75
  36.7 25.6 %collective-permute-start.1 = (bf16[256,2048]{1,0:T(8,128)(2,1)}, bf16[256,2048]{1,0:T(8,128)(2,1)}, u32[]{:S(2)}, u32[]{:S(2)}) collective-permute-start(bf16[256,2048]{1,0:T(8,128)(2,1)} %bitcast.247), channel_id=1, source_target_pairs={{0,4},{1,5},{2,6},{3,7},{4,0},{5,1},{6,2},{7,3},{8,12},{9,13},{10,... | collective-permute-start | bytes 3145736 | tf_op jit(solution)/shard_map/ppermute | solution.py:40
  38.3 25.9 %collective-permute-start = (bf16[256,2048]{1,0:T(8,128)(2,1)}, bf16[256,2048]{1,0:T(8,128)(2,1)}, u32[]{:S(2)}, u32[]{:S(2)}) collective-permute-start(bf16[256,2048]{1,0:T(8,128)(2,1)} %bitcast.248), channel_id=1, source_target_pairs={{0,2},{1,3},{2,0},{3,1},{4,6},{5,7},{6,4},{7,5},{8,10},{9,11},{10,... | collective-permute-start | bytes 3145736 | tf_op jit(solution)/shard_map/ppermute | solution.py:40
  38.5 45.4 %collective-permute-start.4 = (bf16[256,2048]{1,0:T(8,128)(2,1)}, bf16[256,2048]{1,0:T(8,128)(2,1)}, u32[]{:S(2)}, u32[]{:S(2)}) collective-permute-start(bf16[256,2048]{1,0:T(8,128)(2,1)} %bitcast.249), channel_id=1, source_target_pairs={{0,1},{1,0},{2,3},{3,2},{4,5},{5,4},{6,7},{7,6},{8,9},{9,8},{10,11... | collective-permute-start | bytes 3145736 | tf_op jit(solution)/shard_map/ppermute | solution.py:40
  68.1 21.2 %collective-permute-start.6 = (bf16[256,2048]{1,0:T(8,128)(2,1)}, bf16[256,2048]{1,0:T(8,128)(2,1)S(1)}, u32[]{:S(2)}, u32[]{:S(2)}) collective-permute-start(bf16[256,2048]{1,0:T(8,128)(2,1)} %collective-permute-done.1), channel_id=1, source_target_pairs={{0,1},{1,0},{2,3},{3,2},{4,5},{5,4},{6,7},{7,6},{8,9},{9,8},{10,11... | collective-permute-start | bytes 3145736 | tf_op jit(solution)/shard_map/ppermute | solution.py:40
  99.0 20.4 %collective-permute-start.25 = (bf16[64,2304]{1,0:T(8,128)(2,1)S(1)}, bf16[64,2304]{1,0:T(8,128)(2,1)S(1)}, u32[]{:S(2)}, u32[]{:S(2)}) collective-permute-start(bf16[64,2304]{1,0:T(8,128)(2,1)S(1)} %get-tuple-element.140), channel_id=1, source_target_pairs={{0,7},{1,6},{2,5},{3,4},{4,3},{5,2},{6,1},{7,0},{8,15},{9,14},{10,... | collective-permute-start | bytes 884744 | tf_op jit(solution)/shard_map/ppermute | solution.py:40
  121.5 193.4 %all-gather.8.cloned.1.call-start = ((), (), s32[]{:S(2)}) async-start(), calls=%async_computation.9 | async-start | bytes 3932160 | tf_op jit(solution)/shard_map/all_gather | solution.py:75
  132.4 29.3 %collective-permute-start.26 = (bf16[256,2048]{1,0:T(8,128)(2,1)}, bf16[256,2048]{1,0:T(8,128)(2,1)}, u32[]{:S(2)}, u32[]{:S(2)}) collective-permute-start(bf16[256,2048]{1,0:T(8,128)(2,1)} %bitcast.19), channel_id=1, source_target_pairs={{0,4},{1,5},{2,6},{3,7},{4,0},{5,1},{6,2},{7,3},{8,12},{9,13},{10,... | collective-permute-start | bytes 3145736 | tf_op jit(solution)/shard_map/ppermute | solution.py:40
  134.0 27.7 %collective-permute-start.27 = (bf16[256,2048]{1,0:T(8,128)(2,1)}, bf16[256,2048]{1,0:T(8,128)(2,1)}, u32[]{:S(2)}, u32[]{:S(2)}) collective-permute-start(bf16[256,2048]{1,0:T(8,128)(2,1)} %bitcast.19), channel_id=1, source_target_pairs={{0,2},{1,3},{2,0},{3,1},{4,6},{5,7},{6,4},{7,5},{8,10},{9,11},{10,... | collective-permute-start | bytes 3145736 | tf_op jit(solution)/shard_map/ppermute | solution.py:40
  189.1 20.3 %collective-permute-start.35 = (bf16[128,2048]{1,0:T(8,128)(2,1)}, bf16[128,2048]{1,0:T(8,128)(2,1)}, u32[]{:S(2)}, u32[]{:S(2)}) collective-permute-start(bf16[128,2048]{1,0:T(8,128)(2,1)} %slice.321), channel_id=1, source_target_pairs={{0,2},{1,3},{2,0},{3,1},{4,6},{5,7},{6,4},{7,5},{8,10},{9,11},{10,... | collective-permute-start | bytes 1572872 | tf_op jit(solution)/shard_map/ppermute | solution.py:40
  189.4 21.9 %collective-permute-start.29 = (bf16[128,2048]{1,0:T(8,128)(2,1)}, bf16[128,2048]{1,0:T(8,128)(2,1)S(1)}, u32[]{:S(2)}, u32[]{:S(2)}) collective-permute-start(bf16[128,2048]{1,0:T(8,128)(2,1)} %get-tuple-element.268), channel_id=1, source_target_pairs={{0,4},{1,5},{2,6},{3,7},{4,0},{5,1},{6,2},{7,3},{8,12},{9,13},{10,... | collective-permute-start | bytes 1572872 | tf_op jit(solution)/shard_map/ppermute | solution.py:40
  190.7 28.9 %collective-permute-start.34 = (bf16[128,2048]{1,0:T(8,128)(2,1)}, bf16[128,2048]{1,0:T(8,128)(2,1)S(1)}, u32[]{:S(2)}, u32[]{:S(2)}) collective-permute-start(bf16[128,2048]{1,0:T(8,128)(2,1)} %get-tuple-element.269), channel_id=1, source_target_pairs={{0,2},{1,3},{2,0},{3,1},{4,6},{5,7},{6,4},{7,5},{8,10},{9,11},{10,... | collective-permute-start | bytes 1572872 | tf_op jit(solution)/shard_map/ppermute | solution.py:40
  202.3 27.8 %collective-permute-start.33 = (bf16[128,2048]{1,0:T(8,128)(2,1)}, bf16[128,2048]{1,0:T(8,128)(2,1)S(1)}, u32[]{:S(2)}, u32[]{:S(2)}) collective-permute-start(bf16[128,2048]{1,0:T(8,128)(2,1)} %get-tuple-element.253), channel_id=1, source_target_pairs={{0,2},{1,3},{2,0},{3,1},{4,6},{5,7},{6,4},{7,5},{8,10},{9,11},{10,... | collective-permute-start | bytes 1572872 | tf_op jit(solution)/shard_map/ppermute | solution.py:40
  207.0 249.2 %reduce-scatter.5.cloned.1.call-start = ((), (), s32[]{:S(2)}) async-start(), calls=%async_computation.10 | async-start | bytes 3932160 | tf_op jit(solution)/shard_map/reduce_scatter | solution.py:79
  209.4 29.4 %collective-permute-start.37 = (bf16[256,2048]{1,0:T(8,128)(2,1)}, bf16[256,2048]{1,0:T(8,128)(2,1)S(1)}, u32[]{:S(2)}, u32[]{:S(2)}) collective-permute-start(bf16[256,2048]{1,0:T(8,128)(2,1)} %bitcast.19), channel_id=1, source_target_pairs={{0,1},{1,0},{2,3},{3,2},{4,5},{5,4},{6,7},{7,6},{8,9},{9,8},{10,11... | collective-permute-start | bytes 3145736 | tf_op jit(solution)/shard_map/ppermute | solution.py:40
  211.3 28.6 %collective-permute-start.38 = (bf16[256,2048]{1,0:T(8,128)(2,1)}, bf16[256,2048]{1,0:T(8,128)(2,1)S(1)}, u32[]{:S(2)}, u32[]{:S(2)}) collective-permute-start(bf16[256,2048]{1,0:T(8,128)(2,1)} %collective-permute-done.27), channel_id=1, source_target_pairs={{0,1},{1,0},{2,3},{3,2},{4,5},{5,4},{6,7},{7,6},{8,9},{9,8},{10,11... | collective-permute-start | bytes 3145736 | tf_op jit(solution)/shard_map/ppermute | solution.py:40
  219.5 21.8 %collective-permute-start.39 = (bf16[256,2048]{1,0:T(8,128)(2,1)}, bf16[256,2048]{1,0:T(8,128)(2,1)S(1)}, u32[]{:S(2)}, u32[]{:S(2)}) collective-permute-start(bf16[256,2048]{1,0:T(8,128)(2,1)} %collective-permute-done.26), channel_id=1, source_target_pairs={{0,1},{1,0},{2,3},{3,2},{4,5},{5,4},{6,7},{7,6},{8,9},{9,8},{10,11... | collective-permute-start | bytes 3145736 | tf_op jit(solution)/shard_map/ppermute | solution.py:40
  234.4 24.9 %collective-permute-start.42 = (bf16[256,2048]{1,0:T(8,128)(2,1)}, bf16[256,2048]{1,0:T(8,128)(2,1)S(1)}, u32[]{:S(2)}, u32[]{:S(2)}) collective-permute-start(bf16[256,2048]{1,0:T(8,128)(2,1)} %get-tuple-element.240), channel_id=1, source_target_pairs={{0,4},{1,5},{2,6},{3,7},{4,0},{5,1},{6,2},{7,3},{8,12},{9,13},{10,... | collective-permute-start | bytes 3145736 | tf_op jit(solution)/shard_map/ppermute | solution.py:40
  235.2 24.6 %collective-permute-start.43 = (bf16[256,2048]{1,0:T(8,128)(2,1)}, bf16[256,2048]{1,0:T(8,128)(2,1)S(1)}, u32[]{:S(2)}, u32[]{:S(2)}) collective-permute-start(bf16[256,2048]{1,0:T(8,128)(2,1)} %get-tuple-element.240), channel_id=1, source_target_pairs={{0,2},{1,3},{2,0},{3,1},{4,6},{5,7},{6,4},{7,5},{8,10},{9,11},{10,... | collective-permute-start | bytes 3145736 | tf_op jit(solution)/shard_map/ppermute | solution.py:40
  239.8 23.0 %collective-permute-start.41 = (bf16[128,2048]{1,0:T(8,128)(2,1)}, bf16[128,2048]{1,0:T(8,128)(2,1)}, u32[]{:S(2)}, u32[]{:S(2)}) collective-permute-start(bf16[128,2048]{1,0:T(8,128)(2,1)} %collective-permute-done.36), channel_id=1, source_target_pairs={{0,1},{1,0},{2,3},{3,2},{4,5},{5,4},{6,7},{7,6},{8,9},{9,8},{10,11... | collective-permute-start | bytes 1572872 | tf_op jit(solution)/shard_map/ppermute | solution.py:40
  243.3 32.0 %collective-permute-start.46 = (bf16[256,2048]{1,0:T(8,128)(2,1)}, bf16[256,2048]{1,0:T(8,128)(2,1)S(1)}, u32[]{:S(2)}, u32[]{:S(2)}) collective-permute-start(bf16[256,2048]{1,0:T(8,128)(2,1)} %get-tuple-element.240), channel_id=1, source_target_pairs={{0,1},{1,0},{2,3},{3,2},{4,5},{5,4},{6,7},{7,6},{8,9},{9,8},{10,11... | collective-permute-start | bytes 3145736 | tf_op jit(solution)/shard_map/ppermute | solution.py:40
  322.4 180.8 %reduce-scatter.7.cloned.1.call-start = ((), (), s32[]{:S(2)}) async-start(), calls=%async_computation.11 | async-start | bytes 7864320 | tf_op jit(solution)/shard_map/reduce_scatter | solution.py:79
  349.9 21.7 %collective-permute-start.52 = (bf16[128,2048]{1,0:T(8,128)(2,1)}, bf16[128,2048]{1,0:T(8,128)(2,1)S(1)}, u32[]{:S(2)}, u32[]{:S(2)}) collective-permute-start(bf16[128,2048]{1,0:T(8,128)(2,1)} %get-tuple-element.267), channel_id=1, source_target_pairs={{0,2},{1,3},{2,0},{3,1},{4,6},{5,7},{6,4},{7,5},{8,10},{9,11},{10,... | collective-permute-start | bytes 1572872 | tf_op jit(solution)/shard_map/ppermute | solution.py:40
  350.1 22.3 %collective-permute-start.53 = (bf16[128,2048]{1,0:T(8,128)(2,1)S(1)}, bf16[128,2048]{1,0:T(8,128)(2,1)}, u32[]{:S(2)}, u32[]{:S(2)}) collective-permute-start(bf16[128,2048]{1,0:T(8,128)(2,1)S(1)} %get-tuple-element.266), channel_id=1, source_target_pairs={{0,4},{1,5},{2,6},{3,7},{4,0},{5,1},{6,2},{7,3},{8,12},{9,13},{10,... | collective-permute-start | bytes 1572872 | tf_op jit(solution)/shard_map/ppermute | solution.py:40
  351.3 23.9 %collective-permute-start.54 = (bf16[128,2048]{1,0:T(8,128)(2,1)S(1)}, bf16[128,2048]{1,0:T(8,128)(2,1)S(1)}, u32[]{:S(2)}, u32[]{:S(2)}) collective-permute-start(bf16[128,2048]{1,0:T(8,128)(2,1)S(1)} %get-tuple-element.265), channel_id=1, source_target_pairs={{0,4},{1,5},{2,6},{3,7},{4,0},{5,1},{6,2},{7,3},{8,12},{9,13},{10,... | collective-permute-start | bytes 1572872 | tf_op jit(solution)/shard_map/ppermute | solution.py:40
  352.1 23.1 %collective-permute-start.55 = (bf16[128,2048]{1,0:T(8,128)(2,1)S(1)}, bf16[128,2048]{1,0:T(8,128)(2,1)S(1)}, u32[]{:S(2)}, u32[]{:S(2)}) collective-permute-start(bf16[128,2048]{1,0:T(8,128)(2,1)S(1)} %get-tuple-element.264), channel_id=1, source_target_pairs={{0,2},{1,3},{2,0},{3,1},{4,6},{5,7},{6,4},{7,5},{8,10},{9,11},{10,... | collective-permute-start | bytes 1572872 | tf_op jit(solution)/shard_map/ppermute | solution.py:40
  386.3 160.6 %reduce-scatter.9.cloned.1.call-start = ((), (), s32[]{:S(2)}) async-start(), calls=%async_computation.12 | async-start | bytes 1966080 | tf_op jit(solution)/shard_map/reduce_scatter | solution.py:79
  416.5 25.2 %collective-permute-start.59 = (bf16[128,2048]{1,0:T(8,128)(2,1)S(1)}, bf16[128,2048]{1,0:T(8,128)(2,1)S(1)}, u32[]{:S(2)}, u32[]{:S(2)}) collective-permute-start(bf16[128,2048]{1,0:T(8,128)(2,1)S(1)} %get-tuple-element.260), channel_id=1, source_target_pairs={{0,4},{1,5},{2,6},{3,7},{4,0},{5,1},{6,2},{7,3},{8,12},{9,13},{10,... | collective-permute-start | bytes 1572872 | tf_op jit(solution)/shard_map/ppermute | solution.py:40
  417.7 24.1 %collective-permute-start.64 = (bf16[128,2048]{1,0:T(8,128)(2,1)S(1)}, bf16[128,2048]{1,0:T(8,128)(2,1)S(1)}, u32[]{:S(2)}, u32[]{:S(2)}) collective-permute-start(bf16[128,2048]{1,0:T(8,128)(2,1)S(1)} %get-tuple-element.261), channel_id=1, source_target_pairs={{0,2},{1,3},{2,0},{3,1},{4,6},{5,7},{6,4},{7,5},{8,10},{9,11},{10,... | collective-permute-start | bytes 1572872 | tf_op jit(solution)/shard_map/ppermute | solution.py:40
  430.9 20.3 %collective-permute-start.61 = (bf16[128,2048]{1,0:T(8,128)(2,1)S(1)}, bf16[128,2048]{1,0:T(8,128)(2,1)S(1)}, u32[]{:S(2)}, u32[]{:S(2)}) collective-permute-start(bf16[128,2048]{1,0:T(8,128)(2,1)S(1)} %get-tuple-element.248), channel_id=1, source_target_pairs={{0,4},{1,5},{2,6},{3,7},{4,0},{5,1},{6,2},{7,3},{8,12},{9,13},{10,... | collective-permute-start | bytes 1572872 | tf_op jit(solution)/shard_map/ppermute | solution.py:40
  431.8 19.4 %collective-permute-start.63 = (bf16[128,2048]{1,0:T(8,128)(2,1)S(1)}, bf16[128,2048]{1,0:T(8,128)(2,1)S(1)}, u32[]{:S(2)}, u32[]{:S(2)}) collective-permute-start(bf16[128,2048]{1,0:T(8,128)(2,1)S(1)} %get-tuple-element.249), channel_id=1, source_target_pairs={{0,2},{1,3},{2,0},{3,1},{4,6},{5,7},{6,4},{7,5},{8,10},{9,11},{10,... | collective-permute-start | bytes 1572872 | tf_op jit(solution)/shard_map/ppermute | solution.py:40
  456.2 23.5 %collective-permute-start.66 = (bf16[256,2048]{1,0:T(8,128)(2,1)S(1)}, bf16[256,2048]{1,0:T(8,128)(2,1)S(1)}, u32[]{:S(2)}, u32[]{:S(2)}) collective-permute-start(bf16[256,2048]{1,0:T(8,128)(2,1)S(1)} %get-tuple-element.178), channel_id=1, source_target_pairs={{0,4},{1,5},{2,6},{3,7},{4,0},{5,1},{6,2},{7,3},{8,12},{9,13},{10,... | collective-permute-start | bytes 3145736 | tf_op jit(solution)/shard_map/ppermute | solution.py:40
  457.1 23.4 %collective-permute-start.65 = (bf16[256,2048]{1,0:T(8,128)(2,1)S(1)}, bf16[256,2048]{1,0:T(8,128)(2,1)S(1)}, u32[]{:S(2)}, u32[]{:S(2)}) collective-permute-start(bf16[256,2048]{1,0:T(8,128)(2,1)S(1)} %get-tuple-element.178), channel_id=1, source_target_pairs={{0,2},{1,3},{2,0},{3,1},{4,6},{5,7},{6,4},{7,5},{8,10},{9,11},{10,... | collective-permute-start | bytes 3145736 | tf_op jit(solution)/shard_map/ppermute | solution.py:40
  457.7 34.4 %collective-permute-start.69 = (bf16[256,2048]{1,0:T(8,128)(2,1)S(1)}, bf16[256,2048]{1,0:T(8,128)(2,1)S(1)}, u32[]{:S(2)}, u32[]{:S(2)}) collective-permute-start(bf16[256,2048]{1,0:T(8,128)(2,1)S(1)} %get-tuple-element.178), channel_id=1, source_target_pairs={{0,1},{1,0},{2,3},{3,2},{4,5},{5,4},{6,7},{7,6},{8,9},{9,8},{10,11... | collective-permute-start | bytes 3145736 | tf_op jit(solution)/shard_map/ppermute | solution.py:40
  506.3 40.7 %all-to-all-start = ((bf16[8,64,2304]{2,1,0:T(8,128)(2,1)}), bf16[8,64,2304]{2,1,0:T(8,128)(2,1)S(1)}, u32[]{:S(2)}, u32[]{:S(2)}) async-start(bf16[8,64,2304]{2,1,0:T(8,128)(2,1)} %bitcast.251), calls=%async_computation.3 | async-start | bytes 4718592 | tf_op jit(solution)/shard_map/all_to_all | solution.py:102
  509.9 131.5 %reduce-scatter.11.cloned.1.call-start = ((), (), s32[]{:S(2)}) async-start(), calls=%async_computation.13 | async-start | bytes 3932160 | tf_op jit(solution)/shard_map/reduce_scatter | solution.py:79
  566.2 25.6 %collective-permute-start.77 = (bf16[1024,2048]{1,0:T(8,128)(2,1)}, bf16[1024,2048]{1,0:T(8,128)(2,1)}, u32[]{:S(2)}, u32[]{:S(2)}) collective-permute-start(bf16[1024,2048]{1,0:T(8,128)(2,1)} %convolution_convert_fusion.3), channel_id=1, source_target_pairs={{0,1},{1,0},{2,3},{3,2},{4,5},{5,4},{6,7},{7,6},{8,9},{9,8},{10,11... | collective-permute-start | bytes 12582920 | tf_op jit(solution)/shard_map/ppermute | solution.py:40
  583.2 25.0 %all-to-all-start.1 = ((bf16[8,64,384]{2,1,0:T(8,128)(2,1)}), bf16[8,64,384]{2,1,0:T(8,128)(2,1)}, u32[]{:S(2)}, u32[]{:S(2)}) async-start(bf16[8,64,384]{2,1,0:T(8,128)(2,1)} %bitcast.80), calls=%async_computation.4 | async-start | bytes 786432 | tf_op jit(solution)/shard_map/all_to_all | solution.py:102
  587.9 19.7 %collective-permute-start.86 = (bf16[48,768]{1,0:T(8,128)(2,1)S(1)}, bf16[48,768]{1,0:T(8,128)(2,1)S(1)}, u32[]{:S(2)}, u32[]{:S(2)}) collective-permute-start(bf16[48,768]{1,0:T(8,128)(2,1)S(1)} %fusion.54), channel_id=1, source_target_pairs={{0,24},{1,25},{2,26},{3,27},{4,28},{5,29},{6,30},{7,31},{8,0},{9,1... | collective-permute-start | bytes 221192 | tf_op jit(solution)/shard_map/ppermute | solution.py:46
  603.5 26.0 %collective-permute-start.79 = (bf16[128,2048]{1,0:T(8,128)(2,1)}, bf16[128,2048]{1,0:T(8,128)(2,1)}, u32[]{:S(2)}, u32[]{:S(2)}) collective-permute-start(bf16[128,2048]{1,0:T(8,128)(2,1)} %get-tuple-element.258), channel_id=1, source_target_pairs={{0,2},{1,3},{2,0},{3,1},{4,6},{5,7},{6,4},{7,5},{8,10},{9,11},{10,... | collective-permute-start | bytes 1572872 | tf_op jit(solution)/shard_map/ppermute | solution.py:40
  605.5 24.0 %collective-permute-start.81 = (bf16[128,2048]{1,0:T(8,128)(2,1)}, bf16[128,2048]{1,0:T(8,128)(2,1)}, u32[]{:S(2)}, u32[]{:S(2)}) collective-permute-start(bf16[128,2048]{1,0:T(8,128)(2,1)} %get-tuple-element.256), channel_id=1, source_target_pairs={{0,4},{1,5},{2,6},{3,7},{4,0},{5,1},{6,2},{7,3},{8,12},{9,13},{10,... | collective-permute-start | bytes 1572872 | tf_op jit(solution)/shard_map/ppermute | solution.py:40
  626.3 30.6 %collective-permute-start.78 = (bf16[128,2048]{1,0:T(8,128)(2,1)}, bf16[128,2048]{1,0:T(8,128)(2,1)}, u32[]{:S(2)}, u32[]{:S(2)}) collective-permute-start(bf16[128,2048]{1,0:T(8,128)(2,1)} %get-tuple-element.259), channel_id=1, source_target_pairs={{0,4},{1,5},{2,6},{3,7},{4,0},{5,1},{6,2},{7,3},{8,12},{9,13},{10,... | collective-permute-start | bytes 1572872 | tf_op jit(solution)/shard_map/ppermute | solution.py:40
  628.0 28.9 %collective-permute-start.83 = (bf16[128,2048]{1,0:T(8,128)(2,1)}, bf16[128,2048]{1,0:T(8,128)(2,1)}, u32[]{:S(2)}, u32[]{:S(2)}) collective-permute-start(bf16[128,2048]{1,0:T(8,128)(2,1)} %get-tuple-element.257), channel_id=1, source_target_pairs={{0,2},{1,3},{2,0},{3,1},{4,6},{5,7},{6,4},{7,5},{8,10},{9,11},{10,... | collective-permute-start | bytes 1572872 | tf_op jit(solution)/shard_map/ppermute | solution.py:40
  632.6 24.3 %collective-permute-start.80 = (bf16[128,2048]{1,0:T(8,128)(2,1)}, bf16[128,2048]{1,0:T(8,128)(2,1)}, u32[]{:S(2)}, u32[]{:S(2)}) collective-permute-start(bf16[128,2048]{1,0:T(8,128)(2,1)} %get-tuple-element.247), channel_id=1, source_target_pairs={{0,4},{1,5},{2,6},{3,7},{4,0},{5,1},{6,2},{7,3},{8,12},{9,13},{10,... | collective-permute-start | bytes 1572872 | tf_op jit(solution)/shard_map/ppermute | solution.py:40
  633.2 23.8 %collective-permute-start.82 = (bf16[128,2048]{1,0:T(8,128)(2,1)}, bf16[128,2048]{1,0:T(8,128)(2,1)}, u32[]{:S(2)}, u32[]{:S(2)}) collective-permute-start(bf16[128,2048]{1,0:T(8,128)(2,1)} %get-tuple-element.246), channel_id=1, source_target_pairs={{0,2},{1,3},{2,0},{3,1},{4,6},{5,7},{6,4},{7,5},{8,10},{9,11},{10,... | collective-permute-start | bytes 1572872 | tf_op jit(solution)/shard_map/ppermute | solution.py:40
  635.2 20.7 %collective-permute-start.90 = (bf16[96,768]{1,0:T(8,128)(2,1)}, bf16[96,768]{1,0:T(8,128)(2,1)}, u32[]{:S(2)}, u32[]{:S(2)}) collective-permute-start(bf16[96,768]{1,0:T(8,128)(2,1)} %slice.362), channel_id=1, source_target_pairs={{0,4},{1,5},{2,6},{3,7},{4,0},{5,1},{6,2},{7,3},{8,12},{9,13},{10,... | collective-permute-start | bytes 442376 | tf_op jit(solution)/shard_map/ppermute | solution.py:40
  641.4 20.4 %all-to-all-start.2 = ((bf16[8,64,768]{2,1,0:T(8,128)(2,1)}), bf16[8,64,768]{2,1,0:T(8,128)(2,1)S(1)}, u32[]{:S(2)}, u32[]{:S(2)}) async-start(bf16[8,64,768]{2,1,0:T(8,128)(2,1)} %bitcast.261), calls=%async_computation.6 | async-start | bytes 1572864 | tf_op jit(solution)/shard_map/all_to_all | solution.py:102
  (135 other events, 1944.7 us)
Sparse Core Ops, SparseCore 0:
  36.8 89.9 all-gather.3
  129.0 113.6 all-gather.5
  244.8 61.7 all-gather.7
  322.5 60.2 reduce-scatter.4
  386.4 111.6 reduce-scatter.6
  503.3 35.5 reduce-scatter.8
  566.7 66.3 reduce-scatter.10
